TPU v7x, 32 devices: a whole 2x2x4 slice. The times are simulated.
32 devices in a mesh: dp: 4 (over y, core), seq: 8 (over z, x).
Axes of the slice: x: 2, y: 2, z: 4, core: 2. Of those that a mesh axis runs over, the one named last changes fastest.
Arguments:
- activations: bfloat16 [8, 512, 1536], P('dp', 'seq'), may hold values from -6 to 6
- cotangent: bfloat16 [8, 512, 1536], P('dp', 'seq'), may hold values from -6 to 6
- carried_state: float32 [8, 16, 3072], P('dp'), may hold values from -6 to 6
- carried_kv: bfloat16 [8, 2048, 3072], P('dp', 'seq'), may hold values from -6 to 6
- row_lengths: int32 [8], P('dp'), may hold values from 32 to 512, as said below
- mamba_gain: bfloat16 [1536], P(('dp', 'seq')), may hold values from 0.25 to 1.75
- mamba_in: bfloat16 [1536, 6144], P(('dp', 'seq')), may hold values from -0.15625 to 0.15625
- conv_weight: bfloat16 [4, 3072], P(None, ('dp', 'seq')), may hold values from -3 to 3
- conv_bias: bfloat16 [3072], P(('dp', 'seq')), may hold values from -3 to 3
- selection: bfloat16 [3072, 128], P(('dp', 'seq')), may hold values from -0.109375 to 0.109375
- step_proj: bfloat16 [96, 3072], P(None, ('dp', 'seq')), may hold values from -0.625 to 0.625
- step_bias: float32 [3072], P(('dp', 'seq')), may hold values from -11 to -3
- decay_log: float32 [16, 3072], P(None, ('dp', 'seq')), may hold values from 0 to 2.7
- skip_gain: float32 [3072], P(('dp', 'seq')), may hold values from 0.5 to 1.5
- mamba_out: bfloat16 [3072, 1536], P(('dp', 'seq')), may hold values from -0.109375 to 0.109375
- first_gain: bfloat16 [1536], P(('dp', 'seq')), may hold values from 0.25 to 1.75
- first_gate_up: bfloat16 [1536, 8192], P(('dp', 'seq')), may hold values from -0.15625 to 0.15625
- first_down: bfloat16 [4096, 1536], P(('dp', 'seq')), may hold values from -0.09375 to 0.09375
- attention_gain: bfloat16 [1536], P(('dp', 'seq')), may hold values from 0.25 to 1.75
- attention_qkv: bfloat16 [1536, 4608], P(('dp', 'seq')), may hold values from -0.15625 to 0.15625
- attention_out: bfloat16 [1536, 1536], P(('dp', 'seq')), may hold values from -0.625 to 0.625
- second_gain: bfloat16 [1536], P(('dp', 'seq')), may hold values from 0.25 to 1.75
- second_gate_up: bfloat16 [1536, 8192], P(('dp', 'seq')), may hold values from -0.15625 to 0.15625
- second_down: bfloat16 [4096, 1536], P(('dp', 'seq')), may hold values from -0.09375 to 0.09375
Outputs:
- output: bfloat16 [8, 512, 1536], P('dp', 'seq')
- new_state: float32 [8, 16, 3072], P('dp', None, 'seq')
- segment_kv: bfloat16 [8, 512, 3072], P('dp', 'seq')
- grad_input: float32 [8, 512, 1536], P('dp', 'seq')
- grad_state: float32 [8, 16, 3072], P('dp', None, 'seq')
- grad_cache: float32 [8, 2048, 3072], P('dp', 'seq')
- mamba_gain_grad: float32 [1536], P(('dp', 'seq'))
- mamba_in_grad: float32 [1536, 6144], P(('dp', 'seq'))
- conv_weight_grad: float32 [4, 3072], P(None, ('dp', 'seq'))
- conv_bias_grad: float32 [3072], P(('dp', 'seq'))
- selection_grad: float32 [3072, 128], P(('dp', 'seq'))
- step_proj_grad: float32 [96, 3072], P(None, ('dp', 'seq'))
- step_bias_grad: float32 [3072], P(('dp', 'seq'))
- decay_log_grad: float32 [16, 3072], P(None, ('dp', 'seq'))
- skip_gain_grad: float32 [3072], P(('dp', 'seq'))
- mamba_out_grad: float32 [3072, 1536], P(('dp', 'seq'))
- first_gain_grad: float32 [1536], P(('dp', 'seq'))
- first_gate_up_grad: float32 [1536, 8192], P(('dp', 'seq'))
- first_down_grad: float32 [4096, 1536], P(('dp', 'seq'))
- attention_gain_grad: float32 [1536], P(('dp', 'seq'))
- attention_qkv_grad: float32 [1536, 4608], P(('dp', 'seq'))
- attention_out_grad: float32 [1536, 1536], P(('dp', 'seq'))
- second_gain_grad: float32 [1536], P(('dp', 'seq'))
- second_gate_up_grad: float32 [1536, 8192], P(('dp', 'seq'))
- second_down_grad: float32 [4096, 1536], P(('dp', 'seq'))
Inputs may be any that keep to these rules, and one draw needn't show every extreme that they name: `row_lengths`: in each aligned block of 2 rows (the rows of one index of dp), one row drawn from the seed holds 512 real tokens.
All inputs are finite; a program needn't handle non-finite values.
Results may differ from a plain program's by a relative error of at most 0.04.
Values may be sent and summed in bfloat16 or wider, within the bound.
No kernel may reach another device: no remote copies, remote signals or barrier semaphores. Data moves between devices by JAX's collectives and lax.ppermute only.
A program may use at most 640 MiB of HBM per device.

v0:
```python
import jax
import jax.numpy as jnp
from jax import lax
from jax.sharding import PartitionSpec as P

HEAD_DIM = 128
CONV = 4
WINDOW = 2048


EPSILON = 1e-05
NEGATIVE = -1e30


def shifted(block, axis, distance):
    devices = range(lax.axis_size(axis))
    route = [(i - distance, i) for i in devices if i - distance in devices]
    return lax.ppermute(block, axis, route)


def carried_in(part, axis, combine, identity, reverse):
    count = lax.axis_size(axis)
    place = lax.axis_index(axis)
    ahead = count - 1 - place if reverse else place
    gathered = jax.tree.map(lambda a: lax.all_gather(a, axis), part)
    state = jax.tree.map(lambda a, e: jnp.zeros_like(a) + jnp.asarray(e, a.dtype), part, identity)

    def one(lap, state):
        source = count - 1 - lap if reverse else lap
        return combine(
            state, jax.tree.map(lambda a: lax.dynamic_index_in_dim(a, source, 0, False), gathered)
        )

    return lax.fori_loop(0, ahead, one, state)


def rms_gain(values, gain):
    return values * lax.rsqrt(jnp.mean(values * values, axis=-1, keepdims=True) + EPSILON) * gain


def product(left, right):
    return lax.dot_general(
        left, right, (((left.ndim - 1,), (0,)), ((), ())), preferred_element_type=jnp.float32
    )


def product_back(left, right):
    return lax.dot_general(
        left, right, (((left.ndim - 1,), (1,)), ((), ())), preferred_element_type=jnp.float32
    )


def outer(left, right):
    flat_left = left.reshape(-1, left.shape[-1])
    flat_right = right.reshape(-1, right.shape[-1])
    return lax.dot_general(
        flat_left, flat_right, (((0,), (0,)), ((), ())), preferred_element_type=jnp.float32
    )


def fetch_front(shards):
    return (
        lax.all_gather(shards[0], ("dp", "seq"), axis=0, tiled=True),
        lax.all_gather(shards[1], ("dp", "seq"), axis=0, tiled=True),
        lax.all_gather(shards[2], ("dp", "seq"), axis=1, tiled=True),
        lax.all_gather(shards[3], ("dp", "seq"), axis=0, tiled=True),
        lax.all_gather(shards[4], ("dp", "seq"), axis=0, tiled=True),
        lax.all_gather(shards[5], ("dp", "seq"), axis=1, tiled=True),
        lax.all_gather(shards[6].astype(jnp.bfloat16), ("dp", "seq"), axis=0, tiled=True).astype(
            jnp.float32
        ),
        lax.all_gather(shards[7].astype(jnp.bfloat16), ("dp", "seq"), axis=1, tiled=True).astype(
            jnp.float32
        ),
        lax.all_gather(shards[8].astype(jnp.bfloat16), ("dp", "seq"), axis=0, tiled=True).astype(
            jnp.float32
        ),
        lax.all_gather(shards[9], ("dp", "seq"), axis=0, tiled=True),
        lax.all_gather(shards[10], ("dp", "seq"), axis=0, tiled=True),
        lax.all_gather(shards[11], ("dp", "seq"), axis=0, tiled=True),
        lax.all_gather(shards[12], ("dp", "seq"), axis=0, tiled=True),
    )


def settle_front(grads):
    return (
        lax.psum_scatter(grads[0], ("dp", "seq"), scatter_dimension=0, tiled=True),
        lax.psum_scatter(grads[1], ("dp", "seq"), scatter_dimension=0, tiled=True),
        lax.psum_scatter(grads[2], ("dp", "seq"), scatter_dimension=1, tiled=True),
        lax.psum_scatter(grads[3], ("dp", "seq"), scatter_dimension=0, tiled=True),
        lax.psum_scatter(grads[4], ("dp", "seq"), scatter_dimension=0, tiled=True),
        lax.psum_scatter(grads[5], ("dp", "seq"), scatter_dimension=1, tiled=True),
        lax.psum_scatter(grads[6], ("dp", "seq"), scatter_dimension=0, tiled=True),
        lax.psum_scatter(grads[7], ("dp", "seq"), scatter_dimension=1, tiled=True),
        lax.psum_scatter(grads[8], ("dp", "seq"), scatter_dimension=0, tiled=True),
        lax.psum_scatter(grads[9], ("dp", "seq"), scatter_dimension=0, tiled=True),
        lax.psum_scatter(grads[10], ("dp", "seq"), scatter_dimension=0, tiled=True),
        lax.psum_scatter(grads[11], ("dp", "seq"), scatter_dimension=0, tiled=True),
        lax.psum_scatter(grads[12], ("dp", "seq"), scatter_dimension=0, tiled=True),
    )


def fetch_rear(shards):
    return (
        lax.all_gather(shards[0], ("dp", "seq"), axis=0, tiled=True),
        lax.all_gather(shards[1], ("dp", "seq"), axis=0, tiled=True),
        lax.all_gather(shards[2], ("dp", "seq"), axis=0, tiled=True),
        lax.all_gather(shards[3], ("dp", "seq"), axis=0, tiled=True),
        lax.all_gather(shards[4], ("dp", "seq"), axis=0, tiled=True),
        lax.all_gather(shards[5], ("dp", "seq"), axis=0, tiled=True),
    )


def settle_rear(grads):
    return (
        lax.psum_scatter(grads[0], ("dp", "seq"), scatter_dimension=0, tiled=True),
        lax.psum_scatter(grads[1], ("dp", "seq"), scatter_dimension=0, tiled=True),
        lax.psum_scatter(grads[2], ("dp", "seq"), scatter_dimension=0, tiled=True),
        lax.psum_scatter(grads[3], ("dp", "seq"), scatter_dimension=0, tiled=True),
        lax.psum_scatter(grads[4], ("dp", "seq"), scatter_dimension=0, tiled=True),
        lax.psum_scatter(grads[5], ("dp", "seq"), scatter_dimension=0, tiled=True),
    )


def ffn_forward(values, weights):
    gain, gate_up, down = weights
    width = down.shape[0]
    normed = rms_gain(values, gain.astype(jnp.float32)).astype(jnp.bfloat16)
    both = product(normed, gate_up)
    hidden = (jax.nn.silu(both[..., :width]) * both[..., width:]).astype(jnp.bfloat16)
    return (values + product(hidden, down), (normed, both, hidden))


def ffn_backward(values, grad, weights, kept):
    gain, gate_up, down = weights
    normed, both, hidden = kept
    width = down.shape[0]
    grad_low = grad.astype(jnp.bfloat16)
    grad_down = outer(hidden, grad_low)
    grad_hidden = product_back(grad_low, down)

    def ffn_gating(pair):
        return jax.nn.silu(pair[..., :width]) * pair[..., width:]

    unused, gating_back = jax.vjp(ffn_gating, both)
    grad_both = gating_back(grad_hidden)[0].astype(jnp.bfloat16)
    grad_gate_up = outer(normed, grad_both)
    grad_normed = product_back(grad_both, gate_up)
    unused, norm_back = jax.vjp(rms_gain, values, gain.astype(jnp.float32))
    grad_values, grad_gain = norm_back(grad_normed)
    return (grad + grad_values, (grad_gain, grad_gate_up, grad_down))


def convolve(before, inner, conv_weight, conv_bias):
    group = inner.shape[1]
    padded = jnp.concatenate([before, inner], axis=1)
    total = conv_bias
    for index in range(CONV):
        total = total + conv_weight[index] * padded[:, index : index + group]
    return jax.nn.silu(total)


def recurrence(decay):

    def advance(carry, slot):
        mixed_now, step_now, input_now, output_now = slot
        carry = (
            jnp.exp(step_now[:, None, :] * decay) * carry
            + (step_now * mixed_now)[:, None, :] * input_now[:, :, None]
        )
        return (carry, jnp.sum(output_now[:, :, None] * carry, axis=1))

    return advance


def selective(mixed, step, inputs_b, outputs_c, decay, state):
    slots = tuple((jnp.moveaxis(item, 1, 0) for item in (mixed, step, inputs_b, outputs_c)))
    state_end, core = lax.scan(recurrence(decay), state, slots, unroll=8)
    return (jnp.moveaxis(core, 0, 1), state_end)


def chain(earlier, later):
    return (earlier[0] * later[0], later[0] * earlier[1] + later[1])


def chain_both(earlier, later):
    return (
        earlier[0] * later[0],
        later[0] * earlier[1] + later[1],
        earlier[2] * later[2],
        earlier[2] * later[3] + earlier[3],
    )


def stepping(pre, step_bias, valid):
    return jax.nn.softplus(pre + step_bias) * valid[..., None]


def mamba_forward(values, lengths, carried_state, weights):
    (
        gain,
        mamba_in,
        conv_weight,
        conv_bias,
        selection,
        step_proj,
        step_bias,
        decay_log,
        skip_gain,
        mamba_out,
    ) = weights
    rows, group, width = values.shape
    inner_width = mamba_out.shape[0]
    rank = step_proj.shape[0]
    states = decay_log.shape[0]
    shard = lax.axis_index("seq")
    positions = shard * group + jnp.arange(group)
    valid = (positions[None, :] < lengths[:, None]).astype(jnp.float32)
    normed = rms_gain(values, gain.astype(jnp.float32)).astype(jnp.bfloat16)
    projected = product(normed, mamba_in)
    inner = projected[..., :inner_width]
    gate = projected[..., inner_width:]
    before = shifted(inner[:, group - CONV + 1 :], "seq", 1)
    mixed = convolve(before, inner, conv_weight.astype(jnp.float32), conv_bias.astype(jnp.float32))
    mixed_low = mixed.astype(jnp.bfloat16)
    select = product(mixed_low, selection)
    step_low = select[..., :rank].astype(jnp.bfloat16)
    inputs_b = select[..., rank : rank + states]
    outputs_c = select[..., rank + states :]
    pre = product(step_low, step_proj)
    step = stepping(pre, step_bias.astype(jnp.float32), valid)
    decay = -jnp.exp(decay_log.astype(jnp.float32))
    empty = jnp.zeros((rows, states, inner_width), jnp.float32)
    local_end = selective(mixed, step, inputs_b, outputs_c, decay, empty)[1]
    through = jnp.exp(decay * jnp.sum(step, axis=1)[:, None, :])
    prefix_decay, prefix_state = carried_in(
        (through, local_end), "seq", chain, (jnp.ones_like(through), empty), False
    )
    state = prefix_decay * carried_state + prefix_state
    core, state_end = selective(mixed, step, inputs_b, outputs_c, decay, state)
    mixed_out = core + skip_gain.astype(jnp.float32) * mixed
    gated = (mixed_out * jax.nn.silu(gate)).astype(jnp.bfloat16)
    kept = (
        valid,
        normed,
        projected,
        before,
        mixed,
        mixed_low,
        step_low,
        pre,
        step,
        inputs_b,
        outputs_c,
        decay,
        state,
        through,
        prefix_decay,
        mixed_out,
        gated,
        local_end,
        state_end,
    )
    return (values + product(gated, mamba_out), kept)


def mamba_backward(values, grad, weights, kept):
    (
        gain,
        mamba_in,
        conv_weight,
        conv_bias,
        selection,
        step_proj,
        step_bias,
        decay_log,
        skip_gain,
        mamba_out,
    ) = weights
    (
        valid,
        normed,
        projected,
        before,
        mixed,
        mixed_low,
        step_low,
        pre,
        step,
        inputs_b,
        outputs_c,
        decay,
        state,
        through,
        prefix_decay,
        mixed_out,
        gated,
        local_end,
        state_end,
    ) = kept
    group = values.shape[1]
    inner_width = mamba_out.shape[0]
    grad_low = grad.astype(jnp.bfloat16)
    grad_out = outer(gated, grad_low)
    grad_gated = product_back(grad_low, mamba_out)
    gate = projected[..., inner_width:]

    def mamba_gating(mixed_part, gate_part):
        return mixed_part * jax.nn.silu(gate_part)

    unused, gating_back = jax.vjp(mamba_gating, mixed_out, gate)
    grad_mixed_out, grad_gate = gating_back(grad_gated)
    skip = skip_gain.astype(jnp.float32)
    grad_skip = jnp.sum(grad_mixed_out * mixed, axis=(0, 1))
    unused, scan_back = jax.vjp(selective, mixed, step, inputs_b, outputs_c, decay, state)
    zero = jnp.zeros_like(state)
    ones = jnp.ones_like(state)
    own = scan_back((grad_mixed_out, zero))[5]
    suffix = carried_in(
        (through, own, through, local_end), "seq", chain_both, (ones, zero, ones, zero), True
    )
    final = suffix[2] * state_end + suffix[3]
    piece_width = inner_width // lax.axis_size("seq")
    new_state = lax.dynamic_slice_in_dim(final, lax.axis_index("seq") * piece_width, piece_width, 2)
    grad_state = lax.psum_scatter(prefix_decay * own, "seq", scatter_dimension=2, tiled=True)
    grad_mixed, grad_step, grad_inputs, grad_outputs, grad_decay, unused_state = scan_back(
        (grad_mixed_out, suffix[1])
    )
    grad_mixed = grad_mixed + grad_mixed_out * skip
    unused, step_back = jax.vjp(
        lambda pre_part, bias_part: stepping(pre_part, bias_part, valid),
        pre,
        step_bias.astype(jnp.float32),
    )
    grad_pre, grad_step_bias = step_back(grad_step)
    grad_pre_low = grad_pre.astype(jnp.bfloat16)
    grad_step_proj = outer(step_low, grad_pre_low)
    grad_step_low = product_back(grad_pre_low, step_proj)
    grad_select = jnp.concatenate([grad_step_low, grad_inputs, grad_outputs], axis=-1).astype(
        jnp.bfloat16
    )
    grad_selection = outer(mixed_low, grad_select)
    grad_mixed = grad_mixed + product_back(grad_select, selection)
    inner = projected[..., :inner_width]
    unused, conv_back = jax.vjp(
        convolve, before, inner, conv_weight.astype(jnp.float32), conv_bias.astype(jnp.float32)
    )
    grad_before, grad_inner, grad_conv_weight, grad_conv_bias = conv_back(grad_mixed)
    returned = shifted(grad_before, "seq", -1)
    grad_inner = jnp.concatenate(
        [grad_inner[:, : group - CONV + 1], grad_inner[:, group - CONV + 1 :] + returned], axis=1
    )
    grad_projected = jnp.concatenate([grad_inner, grad_gate], axis=-1).astype(jnp.bfloat16)
    grad_in = outer(normed, grad_projected)
    grad_normed = product_back(grad_projected, mamba_in)
    unused, norm_back = jax.vjp(rms_gain, values, gain.astype(jnp.float32))
    grad_values, grad_gain = norm_back(grad_normed)
    grads = (
        grad_gain,
        grad_in,
        grad_conv_weight,
        grad_conv_bias,
        grad_selection,
        grad_step_proj,
        grad_step_bias,
        grad_decay * decay,
        grad_skip,
        grad_out,
    )
    return (grad + grad_values, grads, grad_state, new_state)


def key_positions(start, count, cache_rows, group):
    index = start + jnp.arange(count)
    owner = index // (cache_rows + group)
    offset = index % (cache_rows + group)
    return jnp.where(
        offset < cache_rows,
        owner * cache_rows + offset - WINDOW,
        owner * group + offset - cache_rows,
    )


def visible(query_pos, key_pos, lengths):
    near = (key_pos[None, :] > query_pos[:, None] - WINDOW) & (
        key_pos[None, :] <= query_pos[:, None]
    )
    real = (key_pos[None, None, :] < lengths[:, None, None]) | (
        key_pos[None, None, :] == query_pos[None, :, None]
    )
    return (near[None] & real)[:, :, None, :]


def blockwise(step_fn, carry, piece, size):
    count = jax.tree.leaves(piece)[0].shape[1]
    blocks = count // size

    def split(item):
        return jnp.moveaxis(item.reshape((item.shape[0], blocks, size) + item.shape[2:]), 1, 0)

    def turn(inner, pair):
        return (step_fn(inner, pair[1], pair[0] * size), None)

    carry, unused = lax.scan(turn, carry, (jnp.arange(blocks), jax.tree.map(split, piece)))
    return carry


def over_keys(local_kv, fold, init):
    return fold(init, lax.all_gather(local_kv, "seq", axis=1, tiled=True), jnp.int32(0))


def attention_forward(values, lengths, carried_kv, weights):
    gain, qkv_proj, out_proj = weights
    rows, group, width = values.shape
    heads = width // HEAD_DIM
    cache_rows = carried_kv.shape[1]
    size = cache_rows + group
    scale = HEAD_DIM ** (-0.5)
    query_pos = lax.axis_index("seq") * group + jnp.arange(group)
    normed = rms_gain(values, gain.astype(jnp.float32)).astype(jnp.bfloat16)
    qkv = product(normed, qkv_proj).astype(jnp.bfloat16)
    queries = qkv[..., :width].reshape(rows, group, heads, HEAD_DIM)
    segment_kv = qkv[..., width:]
    local_kv = jnp.concatenate([carried_kv, segment_kv], axis=1)

    def one_block(carry, piece, start):
        count = piece.shape[1]
        inside = visible(query_pos, key_positions(start, count, cache_rows, group), lengths)

        def one_work(state):
            top, total, accum = state
            keys = piece[..., :width].reshape(rows, count, heads, HEAD_DIM)
            contents = piece[..., width:].reshape(rows, count, heads, HEAD_DIM)
            scores = (
                jnp.einsum("rqhd,rkhd->rqhk", queries, keys, preferred_element_type=jnp.float32)
                * scale
            )
            new_top = jnp.maximum(top, jnp.max(jnp.where(inside, scores, NEGATIVE), axis=-1))
            weights_now = jnp.exp(jnp.where(inside, scores - new_top[..., None], NEGATIVE))
            factor = jnp.exp(top - new_top)
            total = total * factor + jnp.sum(weights_now, axis=-1)
            accum = accum * factor[..., None] + jnp.einsum(
                "rqhk,rkhd->rqhd",
                weights_now.astype(jnp.bfloat16),
                contents,
                preferred_element_type=jnp.float32,
            )
            return (new_top, total, accum)

        return lax.cond(jnp.any(inside), one_work, lambda state: state, carry)

    init = (
        jnp.full((rows, group, heads), NEGATIVE, jnp.float32),
        jnp.zeros((rows, group, heads), jnp.float32),
        jnp.zeros((rows, group, heads, HEAD_DIM), jnp.float32),
    )
    top, total, accum = over_keys(
        local_kv, lambda carry, piece, start: blockwise(one_block, carry, piece, size), init
    )
    attended = accum / total[..., None]
    logsum = top + jnp.log(total)
    attended_low = attended.astype(jnp.bfloat16).reshape(rows, group, width)
    kept = (normed, queries, local_kv, attended, attended_low, logsum, query_pos)
    return (values + product(attended_low, out_proj), segment_kv, kept)


def attention_backward(values, grad, lengths, weights, kept):
    gain, qkv_proj, out_proj = weights
    normed, queries, local_kv, attended, attended_low, logsum, query_pos = kept
    rows, group, width = values.shape
    heads = width // HEAD_DIM
    size = local_kv.shape[1]
    cache_rows = size - group
    scale = HEAD_DIM ** (-0.5)
    grad_low = grad.astype(jnp.bfloat16)
    grad_out = outer(attended_low, grad_low)
    grad_attended = (
        product_back(grad_low, out_proj).astype(jnp.bfloat16).reshape(rows, group, heads, HEAD_DIM)
    )
    delta = jnp.sum(grad_attended.astype(jnp.float32) * attended, axis=-1)

    def query_block(carry, piece, start):
        count = piece.shape[1]
        inside = visible(query_pos, key_positions(start, count, cache_rows, group), lengths)

        def query_work(grad_queries):
            keys = piece[..., :width].reshape(rows, count, heads, HEAD_DIM)
            contents = piece[..., width:].reshape(rows, count, heads, HEAD_DIM)
            scores = (
                jnp.einsum("rqhd,rkhd->rqhk", queries, keys, preferred_element_type=jnp.float32)
                * scale
            )
            weights_now = jnp.exp(jnp.where(inside, scores - logsum[..., None], NEGATIVE))
            grad_weights = jnp.einsum(
                "rqhd,rkhd->rqhk", grad_attended, contents, preferred_element_type=jnp.float32
            )
            grad_scores = (weights_now * (grad_weights - delta[..., None])).astype(jnp.bfloat16)
            return (
                grad_queries
                + jnp.einsum(
                    "rqhk,rkhd->rqhd", grad_scores, keys, preferred_element_type=jnp.float32
                )
                * scale
            )

        return lax.cond(jnp.any(inside), query_work, lambda state: state, carry)

    grad_queries = over_keys(
        local_kv,
        lambda carry, piece, start: blockwise(query_block, carry, piece, size),
        jnp.zeros((rows, group, heads, HEAD_DIM), jnp.float32),
    )
    whole_logsum, whole_delta = (
        lax.all_gather(logsum, "seq", axis=1, tiled=True),
        lax.all_gather(delta, "seq", axis=1, tiled=True),
    )
    own_pos = key_positions(lax.axis_index("seq") * size, size, cache_rows, group)
    own_keys = local_kv[..., :width].reshape(rows, size, heads, HEAD_DIM)
    own_contents = local_kv[..., width:].reshape(rows, size, heads, HEAD_DIM)

    def key_block(carry, piece, start):
        part_queries, part_grads = piece
        count = part_queries.shape[1]
        inside = visible(start + jnp.arange(count), own_pos, lengths)

        def key_work(state):
            grad_keys, grad_contents = state
            part_logsum = lax.dynamic_slice_in_dim(whole_logsum, start, count, 1)
            part_delta = lax.dynamic_slice_in_dim(whole_delta, start, count, 1)
            scores = (
                jnp.einsum(
                    "rqhd,rkhd->rqhk", part_queries, own_keys, preferred_element_type=jnp.float32
                )
                * scale
            )
            weights_now = jnp.exp(jnp.where(inside, scores - part_logsum[..., None], NEGATIVE))
            grad_contents = grad_contents + jnp.einsum(
                "rqhk,rqhd->rkhd",
                weights_now.astype(jnp.bfloat16),
                part_grads,
                preferred_element_type=jnp.float32,
            )
            grad_weights = jnp.einsum(
                "rqhd,rkhd->rqhk", part_grads, own_contents, preferred_element_type=jnp.float32
            )
            grad_scores = (weights_now * (grad_weights - part_delta[..., None])).astype(
                jnp.bfloat16
            )
            grad_keys = (
                grad_keys
                + jnp.einsum(
                    "rqhk,rqhd->rkhd", grad_scores, part_queries, preferred_element_type=jnp.float32
                )
                * scale
            )
            return (grad_keys, grad_contents)

        return lax.cond(jnp.any(inside), key_work, lambda state: state, carry)

    empty = jnp.zeros((rows, size, heads, HEAD_DIM), jnp.float32)
    grad_keys, grad_contents = blockwise(
        key_block,
        (empty, empty),
        (
            lax.all_gather(queries, "seq", axis=1, tiled=True),
            lax.all_gather(grad_attended, "seq", axis=1, tiled=True),
        ),
        group,
    )
    grad_local = jnp.concatenate(
        [grad_keys.reshape(rows, size, width), grad_contents.reshape(rows, size, width)], axis=-1
    )
    grad_cache = grad_local[:, :cache_rows]
    grad_qkv = jnp.concatenate(
        [grad_queries.reshape(rows, group, width), grad_local[:, cache_rows:]], axis=-1
    ).astype(jnp.bfloat16)
    grad_qkv_proj = outer(normed, grad_qkv)
    grad_normed = product_back(grad_qkv, qkv_proj)
    unused, norm_back = jax.vjp(rms_gain, values, gain.astype(jnp.float32))
    grad_values, grad_gain = norm_back(grad_normed)
    return (grad + grad_values, (grad_gain, grad_qkv_proj, grad_out), grad_cache)


def local(
    activations,
    cotangent,
    carried_state,
    carried_kv,
    row_lengths,
    mamba_gain,
    mamba_in,
    conv_weight,
    conv_bias,
    selection,
    step_proj,
    step_bias,
    decay_log,
    skip_gain,
    mamba_out,
    first_gain,
    first_gate_up,
    first_down,
    attention_gain,
    attention_qkv,
    attention_out,
    second_gain,
    second_gate_up,
    second_down,
):
    front_shards = (
        mamba_gain,
        mamba_in,
        conv_weight,
        conv_bias,
        selection,
        step_proj,
        step_bias,
        decay_log,
        skip_gain,
        mamba_out,
        first_gain,
        first_gate_up,
        first_down,
    )
    rear_shards = (
        attention_gain,
        attention_qkv,
        attention_out,
        second_gain,
        second_gate_up,
        second_down,
    )
    stream = activations.astype(jnp.float32)
    front_whole = fetch_front(front_shards)
    first_stream, mamba_kept = mamba_forward(stream, row_lengths, carried_state, front_whole[:10])
    second_stream, first_kept = ffn_forward(first_stream, front_whole[10:])
    rear_whole = fetch_rear(rear_shards)
    third_stream, segment_kv, attention_kept = attention_forward(
        second_stream, row_lengths, carried_kv, rear_whole[:3]
    )
    fourth_stream, second_kept = ffn_forward(third_stream, rear_whole[3:])
    grad = cotangent.astype(jnp.float32)
    rear_back = fetch_rear(rear_shards)
    grad, second_grads = ffn_backward(third_stream, grad, rear_back[3:], second_kept)
    grad, attention_grads, grad_cache = attention_backward(
        second_stream, grad, row_lengths, rear_back[:3], attention_kept
    )
    rear_grads = settle_rear(attention_grads + second_grads)
    front_back = fetch_front(front_shards)
    grad, first_grads = ffn_backward(first_stream, grad, front_back[10:], first_kept)
    grad, mamba_grads, grad_state, new_state = mamba_backward(
        stream, grad, front_back[:10], mamba_kept
    )
    front_grads = settle_front(mamba_grads + first_grads)
    return (
        fourth_stream.astype(jnp.bfloat16),
        new_state,
        segment_kv,
        grad,
        grad_state,
        grad_cache,
        front_grads[0],
        front_grads[1],
        front_grads[2],
        front_grads[3],
        front_grads[4],
        front_grads[5],
        front_grads[6],
        front_grads[7],
        front_grads[8],
        front_grads[9],
        front_grads[10],
        front_grads[11],
        front_grads[12],
        rear_grads[0],
        rear_grads[1],
        rear_grads[2],
        rear_grads[3],
        rear_grads[4],
        rear_grads[5],
    )


def solution(mesh):
    return jax.shard_map(
        local,
        mesh=mesh,
        in_specs=(
            P("dp", "seq", None),
            P("dp", "seq", None),
            P("dp", None, None),
            P("dp", "seq", None),
            P("dp"),
            P(("dp", "seq")),
            P(("dp", "seq"), None),
            P(None, ("dp", "seq")),
            P(("dp", "seq")),
            P(("dp", "seq"), None),
            P(None, ("dp", "seq")),
            P(("dp", "seq")),
            P(None, ("dp", "seq")),
            P(("dp", "seq")),
            P(("dp", "seq"), None),
            P(("dp", "seq")),
            P(("dp", "seq"), None),
            P(("dp", "seq"), None),
            P(("dp", "seq")),
            P(("dp", "seq"), None),
            P(("dp", "seq"), None),
            P(("dp", "seq")),
            P(("dp", "seq"), None),
            P(("dp", "seq"), None),
        ),
        out_specs=(
            P("dp", "seq", None),
            P("dp", None, "seq"),
            P("dp", "seq", None),
            P("dp", "seq", None),
            P("dp", None, "seq"),
            P("dp", "seq", None),
            P(("dp", "seq")),
            P(("dp", "seq"), None),
            P(None, ("dp", "seq")),
            P(("dp", "seq")),
            P(("dp", "seq"), None),
            P(None, ("dp", "seq")),
            P(("dp", "seq")),
            P(None, ("dp", "seq")),
            P(("dp", "seq")),
            P(("dp", "seq"), None),
            P(("dp", "seq")),
            P(("dp", "seq"), None),
            P(("dp", "seq"), None),
            P(("dp", "seq")),
            P(("dp", "seq"), None),
            P(("dp", "seq"), None),
            P(("dp", "seq")),
            P(("dp", "seq"), None),
            P(("dp", "seq"), None),
        ),
        check_vma=False,
    )
```

profile of v0, /device:TPU:0, one launch (start us, length us, event | category | flops | bytes accessed | tf_op | source)
XLA Modules:
  0.0 5588.9 jit_solution(7872157699643771989)
XLA Ops:
  14.0 44.8 all-reduce.27
  58.8 67.2 %all-gather.3 = bf16[32,96,4]{1,2,0:T(4,128)(2,1)S(1)} all-gather(bf16[1,96,4]{1,2,0:T(4,128)(2,1)} %bitcast.1680), channel_id=1, replica_groups=mesh['dp'=4,'seq'=8] {'dp','seq'}, dimensions={0}, use_global_device_ids=true | all-gather | bytes 25344 | tf_op jit(solution)/shard_map/all_gather | solution.py:65
  127.7 64.2 %all-gather.2 = bf16[32,96,16]{1,2,0:T(8,128)(2,1)S(1)} all-gather(bf16[1,96,16]{1,2,0:T(8,128)(2,1)S(1)} %convert_bitcast_fusion.1), channel_id=1, replica_groups=mesh['dp'=4,'seq'=8] {'dp','seq'}, dimensions={0}, use_global_device_ids=true | all-gather | bytes 101376 | tf_op jit(solution)/shard_map/all_gather | solution.py:72
  193.9 74.8 %all_gather.119 = bf16[96,3072]{0,1:T(8,128)(2,1)} all-gather(bf16[96,96]{0,1:T(8,128)(2,1)S(1)} %copy.299), channel_id=1, replica_groups=mesh['dp'=4,'seq'=8] {'dp','seq'}, dimensions={1}, use_global_device_ids=true | all-gather | bytes 608256 | tf_op jit(solution)/shard_map/all_gather | solution.py:68
  268.7 73.3 %all_gather.118 = bf16[3072,128]{1,0:T(8,128)(2,1)} all-gather(bf16[96,128]{1,0:T(8,128)(2,1)S(1)} %copy-done.116), channel_id=1, replica_groups=mesh['dp'=4,'seq'=8] {'dp','seq'}, dimensions={0}, use_global_device_ids=true | all-gather | bytes 811008 | tf_op jit(solution)/shard_map/all_gather | solution.py:67
  392.4 49.6 all-gather.43.cloned.1.call-done
  442.0 61.9 %all-gather.21.cloned.1.call-done = f32[8,2,16,3072]{3,2,1,0:T(8,128)} async-done(((f32[1,2,16,3072]{3,2,1,0:T(8,128)}), f32[8,2,16,3072]{3,2,1,0:T(8,128)}) %all-gather.21.cloned.1.call-update) | async-done | bytes 3145744 | tf_op jit(solution)/shard_map/all_gather | solution.py:25
  507.3 31.6 while.169
  543.8 43.6 all-gather.23.cloned.1.call-done
  592.9 150.7 %all-gather.25.cloned.1.call-done = bf16[1536,8192]{1,0:T(8,128)(2,1)} async-done(((bf16[48,8192]{1,0:T(8,128)(2,1)}), bf16[1536,8192]{1,0:T(8,128)(2,1)}) %all-gather.25.cloned.1.call-update) | async-done | bytes 25165840 | tf_op jit(solution)/shard_map/all_gather | solution.py:80
  757.3 83.3 %all-gather.27.cloned.1.call-done = bf16[4096,1536]{1,0:T(8,128)(2,1)} async-done(((bf16[128,1536]{1,0:T(8,128)(2,1)}), bf16[4096,1536]{1,0:T(8,128)(2,1)}) %all-gather.27.cloned.1.call-update) | async-done | bytes 12582928 | tf_op jit(solution)/shard_map/all_gather | solution.py:81
  847.5 97.5 %all-gather.29.cloned.1.call-done = bf16[1536,4608]{1,0:T(8,128)(2,1)} async-done(((bf16[48,4608]{1,0:T(8,128)(2,1)}), bf16[1536,4608]{1,0:T(8,128)(2,1)}) %all-gather.29.cloned.1.call-update) | async-done | bytes 14155792 | tf_op jit(solution)/shard_map/all_gather | solution.py:106
  964.0 219.0 %while.170 = (s32[]{:T(128)}, f32[2,16,3072]{2,1,0:T(8,128)S(1)}, f32[8,8,2,1,3072]{4,2,1,3,0:T(2,128)}, f32[8,8,2,16,3072]{4,3,2,1,0:T(8,128)}, f32[8,8,2,16,30...) while((s32[]{:T(128)}, f32[2,16,3072]{2,1,0:T(8,128)S(1)}, ...), condition=%wide.region_41.42_spmd, body=%wide.region_40.41_spmd.sunk | while | flops 8749062 | bytes 40170600 | solution.py:178
  1203.3 422.3 %all-gather.31.cloned.1.call-done = bf16[2,2560,3072]{2,1,0:T(8,128)(2,1)} async-done(((bf16[2,320,3072]{2,1,0:T(8,128)(2,1)}), bf16[2,2560,3072]{2,1,0:T(8,128)(2,1)}) %all-gather.31.cloned.1.call-update) | async-done | bytes 31457296 | tf_op jit(solution)/shard_map/all_gather | solution.py:409
  1625.6 42.3 copy.309
  1668.0 81.5 %while.172 = (s32[]{:T(128)}, f32[2,64,12]{1,2,0:T(8,128)S(1)}, f32[2,64,12]{1,2,0:T(8,128)S(1)}, f32[2,64,12,128]{3,1,2,0:T(8,128)S(1)}, s32[8]{0:T(128)S(1)}, ...) while((s32[]{:T(128)}, f32[2,64,12]{1,2,0:T(8,128)S(1)}, ...), condition=%wide.region_24.25_spmd.clone, body=%wide.region_18.24_spmd.clone.sunk | while | flops 257673536 | bytes 27875600 | solution.py:404
  1754.7 93.9 %all-gather.35.cloned.1.call-done = bf16[1536,8192]{1,0:T(8,128)(2,1)} async-done(((bf16[48,8192]{1,0:T(8,128)(2,1)}), bf16[1536,8192]{1,0:T(8,128)(2,1)}) %all-gather.35.cloned.1.call-update) | async-done | bytes 25165840 | tf_op jit(solution)/shard_map/all_gather | solution.py:109
  1862.3 83.3 %all-gather.37.cloned.1.call-done = bf16[4096,1536]{1,0:T(8,128)(2,1)} async-done(((bf16[128,1536]{1,0:T(8,128)(2,1)}), bf16[4096,1536]{1,0:T(8,128)(2,1)}) %all-gather.37.cloned.1.call-update) | async-done | bytes 12582928 | tf_op jit(solution)/shard_map/all_gather | solution.py:110
  1958.2 15.6 multiply_reduce_fusion.47
  1982.8 32.8 all_gather.137
  2015.6 33.2 all_gather.139
  2051.0 126.5 %while.173 = (s32[]{:T(128)}, f32[2,64,12,128]{3,1,2,0:T(8,128)S(1)}, s32[8]{0:T(128)}, s32[2]{0:T(128)}, bf16[8,2,320,3072]{2,3,1,0:T(8,128)(2,1)}, /*index=5*/...) while((s32[]{:T(128)}, ...), condition=%wide.region_32.33_spmd.clone, body=%wide.region_28.32_spmd.clone.sunk | while | flops 381041984 | bytes 28100848 | solution.py:404
  2187.7 150.0 %while.174 = (s32[]{:T(128)}, f32[2,320,12,128]{3,1,2,0:T(8,128)}, f32[2,320,12,128]{3,1,2,0:T(8,128)}, s32[8]{0:T(128)S(1)}, s32[2]{0:T(128)}, /*index=5*/bf16[...) while((s32[]{:T(128)}, f32[2,320,12,128]{3,1,2,0:T(8,128)}, ...), condition=%wide.region_37.38_spmd.clone, body=%wide.region_33.37_spmd.clone.sunk | while | flops 511393088 | bytes 27388248 | solution.py:404
  2191.2 15.3 conditional.11
  2210.0 15.3 conditional.11
  2228.7 15.3 conditional.11
  2247.5 15.3 conditional.11
  2266.2 15.3 conditional.11
  2285.0 15.3 conditional.11
  2303.7 15.3 conditional.11
  2386.7 15.9 multiply_reduce_fusion.49
  2413.8 24.9 while.176
  2439.5 58.8 %all-gather.45.cloned.1.call-done = f32[16,16,3072]{2,1,0:T(8,128)} async-done(((f32[2,16,3072]{2,1,0:T(8,128)}), f32[16,16,3072]{2,1,0:T(8,128)}) %all-gather.45.cloned.1.call-update) | async-done | bytes 3145744 | tf_op jit(solution)/shard_map/all_gather | solution.py:25
  2513.4 225.3 %while.177 = (s32[]{:T(128)}, f32[16,3072]{1,0:T(8,128)S(1)}, f32[2,16,3072]{2,1,0:T(8,128)S(1)}, f32[8,8,2,3072]{3,1,0,2:T(8,128)}, f32[8,8,2,3072]{3,1,0,2:T(8...) while((s32[]{:T(128)}, f32[16,3072]{1,0:T(8,128)S(1)}, ...), condition=%wide.region_87.88_spmd.clone, body=%wide.region_46.87_spmd.clone.sunk | while | flops 11894281 | bytes 34832180 | solution.py:178
  2841.6 22.1 convolution_bitcast_fusion.1
  2864.8 22.2 convolution_bitcast_fusion.2
  2913.1 39.1 all-reduce.26
  2959.6 93.0 %reduce-scatter.42.cloned.1.call-done = f32[96,96]{1,0:T(8,128)} async-done(((f32[3072,96]{1,0:T(8,128)}), f32[96,96]{1,0:T(8,128)}) %reduce-scatter.42.cloned.1.call-update) | async-done | bytes 36880
  3054.2 62.7 %reduce-scatter.20.cloned.1.call-done = f32[2,16,384]{2,1,0:T(8,128)} async-done(((f32[2,16,3072]{2,1,0:T(8,128)}), f32[2,16,384]{2,1,0:T(8,128)}) %reduce-scatter.20.cloned.1.call-update) | async-done | bytes 49168 | tf_op jit(solution)/shard_map/reduce_scatter | solution.py:325
  3116.9 141.0 %reduce-scatter.34.cloned.1.call-done = f32[48,1536]{1,0:T(8,128)} async-done(((f32[1536,1536]{1,0:T(8,128)}), f32[48,1536]{1,0:T(8,128)}) %reduce-scatter.34.cloned.1.call-update) | async-done | bytes 294928 | tf_op jit(solution)/shard_map/reduce_scatter | solution.py:118
  3257.9 102.7 %reduce-scatter.24.cloned.1.call-done = f32[96,128]{1,0:T(8,128)} async-done(((f32[3072,128]{1,0:T(8,128)}), f32[96,128]{1,0:T(8,128)}) %reduce-scatter.24.cloned.1.call-update) | async-done | bytes 49168 | tf_op jit(solution)/shard_map/reduce_scatter | solution.py:91
  3360.6 213.9 %reduce-scatter.26.cloned.1.call-done = f32[96,1536]{1,0:T(8,128)} async-done(((f32[3072,1536]{1,0:T(8,128)}), f32[96,1536]{1,0:T(8,128)}) %reduce-scatter.26.cloned.1.call-update) | async-done | bytes 589840 | tf_op jit(solution)/shard_map/reduce_scatter | solution.py:96
  3574.5 252.5 %reduce-scatter.38.cloned.1.call-done = f32[128,1536]{1,0:T(8,128)} async-done(((f32[4096,1536]{1,0:T(8,128)}), f32[128,1536]{1,0:T(8,128)}) %reduce-scatter.38.cloned.1.call-update) | async-done | bytes 786448 | tf_op jit(solution)/shard_map/reduce_scatter | solution.py:121
  3827.0 252.1 %reduce-scatter.30.cloned.1.call-done = f32[128,1536]{1,0:T(8,128)} async-done(((f32[4096,1536]{1,0:T(8,128)}), f32[128,1536]{1,0:T(8,128)}) %reduce-scatter.30.cloned.1.call-update) | async-done | bytes 786448 | tf_op jit(solution)/shard_map/reduce_scatter | solution.py:99
  4079.1 271.1 %reduce-scatter.32.cloned.1.call-done = f32[48,4608]{1,0:T(8,128)} async-done(((f32[1536,4608]{1,0:T(8,128)}), f32[48,4608]{1,0:T(8,128)}) %reduce-scatter.32.cloned.1.call-update) | async-done | bytes 884752 | tf_op jit(solution)/shard_map/reduce_scatter | solution.py:117
  4350.2 356.6 %reduce-scatter.22.cloned.1.call-done = f32[48,6144]{1,0:T(8,128)} async-done(((f32[1536,6144]{1,0:T(8,128)}), f32[48,6144]{1,0:T(8,128)}) %reduce-scatter.22.cloned.1.call-update) | async-done | bytes 1179664 | tf_op jit(solution)/shard_map/reduce_scatter | solution.py:88
  4706.8 437.7 %reduce-scatter.36.cloned.1.call-done = f32[48,8192]{1,0:T(8,128)} async-done(((f32[1536,8192]{1,0:T(8,128)}), f32[48,8192]{1,0:T(8,128)}) %reduce-scatter.36.cloned.1.call-update) | async-done | bytes 1572880 | tf_op jit(solution)/shard_map/reduce_scatter | solution.py:120
  5144.4 437.4 %reduce-scatter.28.cloned.1.call-done = f32[48,8192]{1,0:T(8,128)} async-done(((f32[1536,8192]{1,0:T(8,128)}), f32[48,8192]{1,0:T(8,128)}) %reduce-scatter.28.cloned.1.call-update) | async-done | bytes 1572880 | tf_op jit(solution)/shard_map/reduce_scatter | solution.py:98
  (1738 shorter events, 1405.0 us)
Async XLA Ops:
  7.2 261.5 %copy-start.116 = (bf16[96,128]{1,0:T(8,128)(2,1)S(1)}, bf16[96,128]{1,0:T(8,128)(2,1)}, u32[]{:S(2)}) copy-start(bf16[96,128]{1,0:T(8,128)(2,1)} %param.59) | copy-start | bytes 73732
  7.2 335.4 %all-gather.19.cloned.1.call-start = ((), (), s32[]{:S(2)}) async-start(), calls=%async_computation.13 | async-start | bytes 19464192 | tf_op jit(solution)/shard_map/all_gather | solution.py:64
  7.9 434.0 %all-gather.43.cloned.1.call-start = ((), (), s32[]{:S(2)}) async-start(), calls=%async_computation.35 | async-start | bytes 3538944 | tf_op jit(solution)/shard_map/all_gather | solution.py:25
  58.8 291.8 %copy-start.78 = (f32[1536]{0:T(1024)}, f32[1536]{0:T(1024)S(1)}, u32[]{:S(2)}) copy-start(f32[1536]{0:T(1024)S(1)} %convert_element_type.167) | copy-start | bytes 18436
  192.0 163.2 %copy-start.134 = (s32[64]{0:T(128)}, s32[64]{0:T(128)S(1)}, u32[]{:S(2)}) copy-start(s32[64]{0:T(128)S(1)} %iota_add_fusion.6) | copy-start | bytes 772
  193.1 157.5 %copy-start.120 = (f32[2,64]{1,0:T(2,128)}, f32[2,64]{1,0:T(2,128)S(1)}, u32[]{:S(2)}) copy-start(f32[2,64]{1,0:T(2,128)S(1)} %fusion.347) | copy-start | bytes 1540
  193.1 157.5 %copy-start.100 = (f32[2,64]{1,0:T(2,128)}, f32[2,64]{1,0:T(2,128)S(1)}, u32[]{:S(2)}) copy-start(f32[2,64]{1,0:T(2,128)S(1)} %fusion.374) | copy-start | bytes 1540
  350.6 9.5 collective-permute-start
  385.5 118.3 %all-gather.21.cloned.1.call-start = ((), (), s32[]{:S(2)}) async-start(), calls=%async_computation.14 | async-start | bytes 3538944 | tf_op jit(solution)/shard_map/all_gather | solution.py:25
  389.7 197.7 %all-gather.23.cloned.1.call-start = ((), (), s32[]{:S(2)}) async-start(), calls=%async_computation.15 | async-start | bytes 9732096 | tf_op jit(solution)/shard_map/all_gather | solution.py:78
  390.2 353.3 %all-gather.25.cloned.1.call-start = ((), (), s32[]{:S(2)}) async-start(), calls=%async_computation.16 | async-start | bytes 25952256 | tf_op jit(solution)/shard_map/all_gather | solution.py:80
  390.8 449.8 %all-gather.27.cloned.1.call-start = ((), (), s32[]{:S(2)}) async-start(), calls=%async_computation.17 | async-start | bytes 12976128 | tf_op jit(solution)/shard_map/all_gather | solution.py:81
  391.4 553.7 %all-gather.29.cloned.1.call-start = ((), (), s32[]{:S(2)}) async-start(), calls=%async_computation.18 | async-start | bytes 14598144 | tf_op jit(solution)/shard_map/all_gather | solution.py:106
  392.2 806.5 %all-gather.39.cloned.1.call-start = ((), (), s32[]{:S(2)}) async-start(), calls=%async_computation.23 | async-start | bytes 4718592 | tf_op jit(solution)/shard_map/all_gather | solution.py:565
  392.2 147.3 %copy-start.105 = (f32[3072]{0:T(1024)}, f32[3072]{0:T(1024)S(1)}, u32[]{:S(2)}) copy-start(f32[3072]{0:T(1024)S(1)} %convert_element_type.175) | copy-start | bytes 36868
  392.3 351.3 %copy-start.68 = (f32[1536]{0:T(1024)}, f32[1536]{0:T(1024)S(1)}, u32[]{:S(2)}) copy-start(f32[1536]{0:T(1024)S(1)} %convert_element_type.177) | copy-start | bytes 18436
  392.3 552.8 %copy-start.80 = (f32[1536]{0:T(1024)}, f32[1536]{0:T(1024)S(1)}, u32[]{:S(2)}) copy-start(f32[1536]{0:T(1024)S(1)} %convert_element_type.180) | copy-start | bytes 18436
  592.8 160.8 %copy-start.12 = (f32[2,64,1536]{2,1,0:T(8,128)}, f32[2,64,1536]{2,1,0:T(8,128)S(1)}, u32[]{:S(2)}) copy-start(f32[2,64,1536]{2,1,0:T(8,128)S(1)} %get-tuple-element.2643) | copy-start | bytes 2359300
  592.8 160.8 %copy-start.122 = (f32[2,64]{1,0:T(2,128)}, f32[2,64]{1,0:T(2,128)S(1)}, u32[]{:S(2)}) copy-start(f32[2,64]{1,0:T(2,128)S(1)} %get-tuple-element.2642) | copy-start | bytes 1540
  592.9 160.8 %copy-start.95 = (f32[2,64]{1,0:T(2,128)}, f32[2,64]{1,0:T(2,128)S(1)}, u32[]{:S(2)}) copy-start(f32[2,64]{1,0:T(2,128)S(1)} %fusion.375) | copy-start | bytes 1540
  847.5 97.6 %copy-start.124 = (f32[2,64]{1,0:T(2,128)}, f32[2,64]{1,0:T(2,128)S(1)}, u32[]{:S(2)}) copy-start(f32[2,64]{1,0:T(2,128)S(1)} %get-tuple-element.2644) | copy-start | bytes 1540
  847.5 904.0 %copy-start.9 = (f32[2,64,1536]{2,1,0:T(8,128)}, f32[2,64,1536]{2,1,0:T(8,128)S(1)}, u32[]{:S(2)}) copy-start(f32[2,64,1536]{2,1,0:T(8,128)S(1)} %get-tuple-element.2645) | copy-start | bytes 2359300
  955.1 670.5 %all-gather.31.cloned.1.call-start = ((), (), s32[]{:S(2)}) async-start(), calls=%async_computation.19 | async-start | bytes 35389440 | tf_op jit(solution)/shard_map/all_gather | solution.py:409
  961.3 790.1 %all-gather.33.cloned.1.call-start = ((), (), s32[]{:S(2)}) async-start(), calls=%async_computation.20 | async-start | bytes 4866048 | tf_op jit(solution)/shard_map/all_gather | solution.py:107
  961.9 886.7 %all-gather.35.cloned.1.call-start = ((), (), s32[]{:S(2)}) async-start(), calls=%async_computation.21 | async-start | bytes 25952256 | tf_op jit(solution)/shard_map/all_gather | solution.py:109
  962.7 983.0 %all-gather.37.cloned.1.call-start = ((), (), s32[]{:S(2)}) async-start(), calls=%async_computation.22 | async-start | bytes 12976128 | tf_op jit(solution)/shard_map/all_gather | solution.py:110
  963.2 1215.0 %all-gather.41.cloned.1.call-start = ((), (), s32[]{:S(2)}) async-start(), calls=%async_computation.24 | async-start | bytes 4718592 | tf_op jit(solution)/shard_map/all_gather | solution.py:566
  1754.7 107.7 %copy-start.128 = (f32[2,64]{1,0:T(2,128)}, f32[2,64]{1,0:T(2,128)S(1)}, u32[]{:S(2)}) copy-start(f32[2,64]{1,0:T(2,128)S(1)} %get-tuple-element.2646) | copy-start | bytes 1540
  1754.7 219.2 %copy-start.4 = (f32[2,64,1536]{2,1,0:T(8,128)}, f32[2,64,1536]{2,1,0:T(8,128)S(1)}, u32[]{:S(2)}) copy-start(f32[2,64,1536]{2,1,0:T(8,128)S(1)} %get-tuple-element.2647) | copy-start | bytes 2359300
  1754.7 219.1 %copy-start.92 = (f32[2,64]{1,0:T(2,128)}, f32[2,64]{1,0:T(2,128)S(1)}, u32[]{:S(2)}) copy-start(f32[2,64]{1,0:T(2,128)S(1)} %fusion.377) | copy-start | bytes 1540
  1981.8 516.5 %all-gather.45.cloned.1.call-start = ((), (), s32[]{:S(2)}) async-start(), calls=%async_computation.36 | async-start | bytes 3538944 | tf_op jit(solution)/shard_map/all_gather | solution.py:25
  2404.2 366.8 %copy-start.31 = (f32[2,64,1536]{2,1,0:T(8,128)}, f32[2,64,1536]{2,1,0:T(8,128)S(1)}, u32[]{:S(2)}) copy-start(f32[2,64,1536]{2,1,0:T(8,128)S(1)} %fusion.345) | copy-start | bytes 2359300
  2439.5 461.0 %reduce-scatter.40.cloned.1.call-start = ((), (), s32[]{:S(2)}) async-start(), calls=%async_computation.37 | async-start | bytes 1622016
  2513.3 225.4 %copy-start.73 = (u8[64,3072]{1,0:T(8,128)(4,1)S(1)}, u8[64,3072]{1,0:T(8,128)(4,1)}, u32[]{:S(2)}) copy-start(u8[64,3072]{1,0:T(8,128)(4,1)} %copy-done.72) | copy-start | bytes 589828
  2513.4 225.4 %copy-start.127 = (f32[2,64]{1,0:T(2,128)S(1)}, f32[2,64]{1,0:T(2,128)}, u32[]{:S(2)}) copy-start(f32[2,64]{1,0:T(2,128)} %copy-done.126) | copy-start | bytes 1540
  2755.8 202.4 %reduce-scatter.44.cloned.1.call-start = ((), (), s32[]{:S(2)}) async-start(), calls=%async_computation.39 | async-start | bytes 1622016
  2757.5 295.1 %reduce-scatter.42.cloned.1.call-start = ((), (), s32[]{:S(2)}) async-start(), calls=%async_computation.38 | async-start | bytes 1622016
  2760.4 356.5 %reduce-scatter.20.cloned.1.call-start = ((), (), s32[]{:S(2)}) async-start(), calls=%async_computation.25 | async-start | bytes 442368 | tf_op jit(solution)/shard_map/reduce_scatter | solution.py:325
  2761.3 496.6 %reduce-scatter.34.cloned.1.call-start = ((), (), s32[]{:S(2)}) async-start(), calls=%async_computation.32 | async-start | bytes 9732096 | tf_op jit(solution)/shard_map/reduce_scatter | solution.py:118
  2767.6 593.0 %reduce-scatter.24.cloned.1.call-start = ((), (), s32[]{:S(2)}) async-start(), calls=%async_computation.27 | async-start | bytes 1622016 | tf_op jit(solution)/shard_map/reduce_scatter | solution.py:91
  2770.9 803.6 %reduce-scatter.26.cloned.1.call-start = ((), (), s32[]{:S(2)}) async-start(), calls=%async_computation.28 | async-start | bytes 19464192 | tf_op jit(solution)/shard_map/reduce_scatter | solution.py:96
  2780.4 1046.6 %reduce-scatter.38.cloned.1.call-start = ((), (), s32[]{:S(2)}) async-start(), calls=%async_computation.34 | async-start | bytes 25952256 | tf_op jit(solution)/shard_map/reduce_scatter | solution.py:121
  2791.9 1287.2 %reduce-scatter.30.cloned.1.call-start = ((), (), s32[]{:S(2)}) async-start(), calls=%async_computation.30 | async-start | bytes 25952256 | tf_op jit(solution)/shard_map/reduce_scatter | solution.py:99
  2803.8 1546.3 %reduce-scatter.32.cloned.1.call-start = ((), (), s32[]{:S(2)}) async-start(), calls=%async_computation.31 | async-start | bytes 29196288 | tf_op jit(solution)/shard_map/reduce_scatter | solution.py:117
  2816.8 1889.9 %reduce-scatter.22.cloned.1.call-start = ((), (), s32[]{:S(2)}) async-start(), calls=%async_computation.26 | async-start | bytes 38928384 | tf_op jit(solution)/shard_map/reduce_scatter | solution.py:88
  2818.1 6.6 collective-permute-start.1
  2840.5 2303.9 %reduce-scatter.36.cloned.1.call-start = ((), (), s32[]{:S(2)}) async-start(), calls=%async_computation.33 | async-start | bytes 51904512 | tf_op jit(solution)/shard_map/reduce_scatter | solution.py:120
  2863.7 2718.2 %reduce-scatter.28.cloned.1.call-start = ((), (), s32[]{:S(2)}) async-start(), calls=%async_computation.29 | async-start | bytes 51904512 | tf_op jit(solution)/shard_map/reduce_scatter | solution.py:98
  (117 other events, 1171.1 us)
Sparse Core Ops, SparseCore 0:
  11.0 129.2 all-gather.18
  385.6 56.3 all-gather.42
  444.7 59.0 all-gather.20
  506.7 80.6 all-gather.22
  590.2 153.2 all-gather.24
  746.4 94.1 all-gather.26
  843.6 101.4 all-gather.28
  955.2 71.4 all-gather.38
  1028.9 596.6 all-gather.30
  1628.4 63.6 all-gather.32
  1695.1 153.4 all-gather.34
  1851.4 94.1 all-gather.36
  1981.9 81.8 all-gather.40
  2439.6 58.6 all-gather.44
  2755.9 94.2 reduce-scatter.39
  2855.3 96.0 reduce-scatter.43
  2956.5 96.1 reduce-scatter.41
  3056.4 60.4 reduce-scatter.19
  3123.4 134.4 reduce-scatter.33
  3264.4 96.1 reduce-scatter.23
  3368.7 205.7 reduce-scatter.25
  3582.6 244.3 reduce-scatter.37
  3834.0 245.0 reduce-scatter.29
  4087.1 263.0 reduce-scatter.31
  4358.3 348.4 reduce-scatter.21
  4713.6 430.7 reduce-scatter.35
  5151.3 430.5 reduce-scatter.27
where the time goes:
time: 5620 us; the launch traced here: 5590 us
  waiting for transfers between devices  3770 us (67%)
  matrix products  459 us (8%)
  local copies, waits for them, and re-layouts  451 us (8%)
  blocking collectives  429 us (8%)
  other arithmetic  415 us (7%)
    reduce_scatter x1, waiting for transfers between devices, settle_rear(): lax.psum_scatter(grads[4], ('dp', 'seq'), scatter_dimension=0, tiled=True)  438 us
    reduce_scatter x1, waiting for transfers between devices, settle_front(): lax.psum_scatter(grads[11], ('dp', 'seq'), scatter_dimension=0, tiled=True)  437 us
    all_gather x1, waiting for transfers between devices, over_keys(): lax.all_gather(local_kv, 'seq', axis=1, tiled=True)  422 us
    reduce_scatter x1, waiting for transfers between devices, settle_front(): lax.psum_scatter(grads[1], ('dp', 'seq'), scatter_dimension=0, tiled=True)  357 us
    reduce_scatter x1, waiting for transfers between devices, settle_rear(): lax.psum_scatter(grads[1], ('dp', 'seq'), scatter_dimension=0, tiled=True)  271 us
    reduce_scatter x1, waiting for transfers between devices, settle_rear(): lax.psum_scatter(grads[5], ('dp', 'seq'), scatter_dimension=0, tiled=True)  252 us
    reduce_scatter x1, waiting for transfers between devices, settle_front(): lax.psum_scatter(grads[12], ('dp', 'seq'), scatter_dimension=0, tiled=True)  252 us
    reduce_scatter x1, waiting for transfers between devices, settle_front(): lax.psum_scatter(grads[9], ('dp', 'seq'), scatter_dimension=0, tiled=True)  214 us
  transfers between devices with their start and end apart: 29, of which 22 were waited for; matrix products, arithmetic and copies ran while one was open for 13% of the time, Pallas kernels for 0%

commit v1 on v0

--- a/solution.py
+++ b/solution.py
@@ -1,6 +1,9 @@
 import jax
 import jax.numpy as jnp
 from jax import lax
+from jax.experimental import pallas as pl
+from jax.experimental.pallas import tpu as pltpu
+from jax.sharding import Mesh
 from jax.sharding import PartitionSpec as P
 
 HEAD_DIM = 128
@@ -681,62 +684,1071 @@
     )
 
 
+EVERY = ("y", "c", "z", "x")
+PLANE = ("y", "c", "x")
+BF = jnp.bfloat16
+F32 = jnp.float32
+
+
+def params(**more):
+    return pltpu.CompilerParams(vmem_limit_bytes=60 * 2**20, **more)
+
+
+def swap_planes(block):
+    planes = lax.axis_size("z")
+    inner = lax.axis_size("x")
+    route = []
+    for d in range(planes):
+        for z in range(planes):
+            for x in range(inner):
+                route.append(((d * planes + z) * inner + x, (z * planes + d) * inner + x))
+    return lax.ppermute(block, EVERY, route)
+
+
+def other(block, axis):
+    return lax.ppermute(block, axis, [(0, 1), (1, 0)])
+
+
+def gather_plane(block):
+    from_y = other(block, "y")
+    from_x = other(block, "x")
+    corner = jnp.concatenate([other(from_y[:1], "x"), other(from_x[1:], "y")], axis=0)
+    own = jnp.stack([block, from_x, from_y, corner])
+    return jnp.concatenate([own, other(own, "c")], axis=0)
+
+
+def scatter_plane(parts):
+    kind = parts.dtype
+    half = parts.shape[0] // 2
+    mine = parts[:half].astype(F32) + other(parts[half:], "c").astype(F32)
+    sent = mine[1:].astype(kind)
+    to_x, to_y, corner = sent[0], sent[1], sent[2]
+    via_y = other(corner[:1], "y").astype(F32)
+    via_x = other(corner[1:], "x").astype(F32)
+    to_x = jnp.concatenate([(mine[1][:1] + via_y).astype(kind), to_x[1:]], axis=0)
+    to_y = jnp.concatenate([to_y[:1], (mine[2][1:] + via_x).astype(kind)], axis=0)
+    return mine[0] + other(to_x, "x").astype(F32) + other(to_y, "y").astype(F32)
+
+
+def sum_plane(parts):
+    return gather_plane(scatter_plane(parts))
+
+
+def trade(block, axes):
+    return lax.all_to_all(block, axes, 0, 0, tiled=True)
+
+
+def turned(block, distance):
+    planes = lax.axis_size("z")
+    return lax.ppermute(block, "z", [(z, (z + distance) % planes) for z in range(planes)])
+
+
+def gather_z(block):
+    planes = lax.axis_size("z")
+    ring = [block] + [turned(block, planes - k) for k in range(1, planes)]
+    ring = jnp.stack(ring + ring[:-1])
+    first = (planes - lax.axis_index("z")) % planes
+    return lax.dynamic_slice_in_dim(ring, first, planes, 0)
+
+
+def gather_small(block):
+    for axis in ("x", "c", "y"):
+        pair = (block, other(block, axis))
+        here = lax.axis_index(axis) == 0
+        block = jnp.stack([jnp.where(here, pair[0], pair[1]), jnp.where(here, pair[1], pair[0])])
+    return gather_z(block)
+
+
+def total_small(block):
+    for axis in ("x", "y", "c"):
+        block = block + other(block, axis)
+    return block + sum(turned(block, k) for k in range(1, lax.axis_size("z")))
+
+
+def reduce_z(parts):
+    return lax.psum_scatter(parts, "z", scatter_dimension=0)
+
+
+def deal(pieces, back):
+    planes, inner = lax.axis_size("z"), lax.axis_size("x")
+    result = []
+    for k, piece in enumerate(pieces):
+        turn, flip = k // inner, k % inner
+        route = []
+        for d in range(planes):
+            for z in range(planes):
+                for x in range(inner):
+                    goal = (z, d ^ turn, x ^ flip) if back else (z ^ turn, d, x ^ flip)
+                    place = (d * planes + z) * inner + x
+                    route.append((place, (goal[0] * planes + goal[1]) * inner + goal[2]))
+        result.append(lax.ppermute(piece, EVERY, route))
+    return result
+
+
+def rows_gather(block):
+    x = lax.axis_index("x")
+    mine = lax.dynamic_index_in_dim(block, x, 0, False)
+    theirs = lax.dynamic_index_in_dim(block, 1 - x, 0, False)
+    pair = jnp.stack([mine, other(theirs, "x")])
+    four = jnp.concatenate([pair, other(pair, "y")], axis=0)
+    return jnp.concatenate([four, other(four, "c")], axis=0)
+
+
+def rows_scatter(parts):
+    kind = parts.dtype
+    for axis in ("c", "y"):
+        half = parts.shape[0] // 2
+        parts = (
+            parts[:half].astype(F32) + other(parts[half:].astype(kind), axis).astype(F32)
+        )
+    mine, theirs = parts[0], other(parts[1].astype(kind), "x").astype(F32)
+    first = lax.axis_index("x") == 0
+    return jnp.stack([jnp.where(first, mine, theirs), jnp.where(first, theirs, mine)])
+
+
+def rows_of(gathered):
+    planes, members, rows, width = gathered.shape
+    inner = lax.axis_size("x")
+    split = gathered.reshape(planes, members // inner, inner, rows, width)
+    return split.transpose(1, 0, 2, 3, 4).reshape(planes * members * rows, width)
+
+
+def by_plane(grad):
+    planes, inner = lax.axis_size("z"), lax.axis_size("x")
+    total, width = grad.shape
+    rows = total // (planes * planes * inner)
+    split = grad.reshape(planes, planes, inner, rows, width).transpose(1, 0, 2, 3, 4)
+    return split.reshape(planes, planes * inner, rows, width)
+
+
+def columns_in(payload):
+    return rows_of(lax.all_gather(trade(payload, PLANE), "z", axis=0))
+
+
+def columns_out(grad):
+    return trade(reduce_z(by_plane(grad.astype(BF))), PLANE)
+
+
+def relocate(block, back):
+    planes, inner = lax.axis_size("z"), lax.axis_size("x")
+    route = []
+    for place in range(planes * inner):
+        goal = (place % planes) * inner + place // planes
+        route.append((goal, place) if back else (place, goal))
+    return lax.ppermute(block, ("z", "x"), route)
+
+
+def dot(left, right, left_dim, right_dim):
+    return lax.dot_general(
+        left, right, (((left_dim,), (right_dim,)), ((), ())), preferred_element_type=F32
+    )
+
+
+def conv_body(order, inner_ref, taps_ref, bias_ref, total_ref, mixed_ref, low_ref, held):
+    step = pl.program_id(0)
+    rows, group = inner_ref.shape[1], inner_ref.shape[2]
+
+    @pl.when(step == 0)
+    def clear():
+        held[:, :8] = jnp.zeros_like(held[:, :8])
+
+    @pl.when(step > 0)
+    def keep():
+        held[:, :8] = held[:, group:]
+
+    for row in range(rows):
+        held[row, 8:] = inner_ref[0, row]
+        total = bias_ref[...] + taps_ref[0:1] * held[row, 5 : 5 + group]
+        for tap in range(1, CONV):
+            total = total + taps_ref[tap : tap + 1] * held[row, 5 + tap : 5 + tap + group]
+        mixed = total / (1.0 + jnp.exp(-total))
+        total_ref[0, row] = total
+        mixed_ref[0, row] = mixed
+        low_ref[0, row] = mixed.astype(BF)
+
+
+def conv_forward(order, projected, taps, bias):
+    blocks, rows, group, both = projected.shape
+    width = both // 2
+    spec = pl.BlockSpec((1, rows, group, width), lambda i, order: (order[i], 0, 0, 0))
+    shape = (blocks, rows, group, width)
+    return pl.pallas_call(
+        conv_body,
+        grid_spec=pltpu.PrefetchScalarGridSpec(
+            num_scalar_prefetch=1,
+            grid=(blocks,),
+            in_specs=[
+                spec,
+                pl.BlockSpec((CONV, width), lambda i, order: (0, 0)),
+                pl.BlockSpec((1, width), lambda i, order: (0, 0)),
+            ],
+            out_specs=[spec, spec, spec],
+            scratch_shapes=[pltpu.VMEM((rows, group + 8, width), F32)],
+        ),
+        out_shape=[
+            jax.ShapeDtypeStruct(shape, F32),
+            jax.ShapeDtypeStruct(shape, F32),
+            jax.ShapeDtypeStruct(shape, BF),
+        ],
+        compiler_params=params(),
+        name="conv_forward",
+    )(order, projected, taps, bias)
+
+
+def conv_back_body(order, grad_ref, total_ref, inner_ref, taps_ref, out_ref, sums_ref, held):
+    step = pl.program_id(0)
+    rows, group = inner_ref.shape[1], inner_ref.shape[2]
+
+    @pl.when(step == 0)
+    def clear():
+        held[:, group:] = jnp.zeros_like(held[:, group:])
+        sums_ref[...] = jnp.zeros_like(sums_ref)
+
+    @pl.when(step > 0)
+    def keep():
+        held[:, group:] = held[:, :8]
+
+    for row in range(rows):
+        total = total_ref[0, row]
+        sig = 1.0 / (1.0 + jnp.exp(-total))
+        grad = grad_ref[0, row] * (sig * (1.0 + total * (1.0 - sig)))
+        held[row, :group] = grad
+        inner = inner_ref[0, row]
+        back = None
+        for tap in range(CONV):
+            later = held[row, CONV - 1 - tap : CONV - 1 - tap + group]
+            part = taps_ref[tap : tap + 1] * later
+            back = part if back is None else back + part
+            sums_ref[tap : tap + 1] += jnp.sum(inner * later, axis=0, keepdims=True)
+        sums_ref[CONV : CONV + 1] += jnp.sum(grad, axis=0, keepdims=True)
+        out_ref[0, row] = back.astype(BF)
+
+
+def conv_back(order, grad, total, projected, taps):
+    blocks, rows, group, width = grad.shape
+    spec = pl.BlockSpec(
+        (1, rows, group, width), lambda i, order: (order[blocks - 1 - i], 0, 0, 0)
+    )
+    return pl.pallas_call(
+        conv_back_body,
+        grid_spec=pltpu.PrefetchScalarGridSpec(
+            num_scalar_prefetch=1,
+            grid=(blocks,),
+            in_specs=[spec, spec, spec, pl.BlockSpec((CONV, width), lambda i, order: (0, 0))],
+            out_specs=[spec, pl.BlockSpec((8, width), lambda i, order: (0, 0))],
+            scratch_shapes=[pltpu.VMEM((rows, group + 8, width), F32)],
+        ),
+        out_shape=[
+            jax.ShapeDtypeStruct(grad.shape, BF),
+            jax.ShapeDtypeStruct((8, width), F32),
+        ],
+        compiler_params=params(),
+        name="conv_back",
+    )(order, grad, total, projected, taps)
+
+
+def widen(tile, width):
+    return jnp.concatenate([tile] * (width // 128), axis=1)
+
+
+def narrow(tile):
+    total = tile[:, :128]
+    for start in range(128, tile.shape[1], 128):
+        total = total + tile[:, start : start + 128]
+    return total
+
+
+def scan_body(
+    order, mixed_ref, step_ref, b_ref, c_ref, decay_ref, start_ref, core_ref, past_ref, end_ref, held
+):
+    @pl.when(pl.program_id(0) == 0)
+    def begin():
+        held[...] = start_ref[...]
+
+    decay = decay_ref[...]
+    rows, group, width = mixed_ref.shape[1:]
+
+    def eight(turn, states):
+        base = pl.multiple_of(turn * 8, 8)
+        states = list(states)
+        steps = [step_ref[0, row, pl.ds(base, 8), :] for row in range(rows)]
+        drives = [steps[row] * mixed_ref[0, row, pl.ds(base, 8), :] for row in range(rows)]
+        cores = [[] for row in range(rows)]
+        for k in range(8):
+            for row in range(rows):
+                past_ref[0, row, base + k] = states[row]
+                fade = jnp.exp(steps[row][k : k + 1] * decay)
+                state = fade * states[row] + drives[row][k : k + 1] * widen(
+                    b_ref[0, row, base + k], width
+                )
+                states[row] = state
+                seen = widen(c_ref[0, row, base + k], width) * state
+                cores[row].append(jnp.sum(seen, axis=0, keepdims=True))
+        for row in range(rows):
+            core_ref[0, row, pl.ds(base, 8), :] = jnp.concatenate(cores[row], axis=0)
+        return tuple(states)
+
+    states = lax.fori_loop(0, group // 8, eight, tuple(held[row] for row in range(rows)))
+    for row in range(rows):
+        held[row] = states[row]
+        end_ref[row] = states[row]
+
+
+def scan_forward(order, mixed, step, wide_b, wide_c, decay, start):
+    blocks, rows, group, width = mixed.shape
+    states = decay.shape[0]
+    spec = pl.BlockSpec((1, rows, group, width), lambda i, order: (order[i], 0, 0, 0))
+    maps = pl.BlockSpec((1, rows, group, states, 128), lambda i, order: (order[i], 0, 0, 0, 0))
+    whole = pl.BlockSpec((rows, states, width), lambda i, order: (0, 0, 0))
+    return pl.pallas_call(
+        scan_body,
+        grid_spec=pltpu.PrefetchScalarGridSpec(
+            num_scalar_prefetch=1,
+            grid=(blocks,),
+            in_specs=[
+                spec,
+                spec,
+                maps,
+                maps,
+                pl.BlockSpec((states, width), lambda i, order: (0, 0)),
+                whole,
+            ],
+            out_specs=[
+                spec,
+                pl.BlockSpec(
+                    (1, rows, group, states, width), lambda i, order: (order[i], 0, 0, 0, 0)
+                ),
+                whole,
+            ],
+            scratch_shapes=[pltpu.VMEM((rows, states, width), F32)],
+        ),
+        out_shape=[
+            jax.ShapeDtypeStruct(mixed.shape, F32),
+            jax.ShapeDtypeStruct((blocks, rows, group, states, width), F32),
+            jax.ShapeDtypeStruct(start.shape, F32),
+        ],
+        compiler_params=params(),
+        name="scan_forward",
+    )(order, mixed, step, wide_b, wide_c, decay, start)
+
+
+def scan_back_body(
+    order,
+    mixed_ref,
+    step_ref,
+    b_ref,
+    c_ref,
+    grad_ref,
+    past_ref,
+    decay_ref,
+    end_ref,
+    dmixed_ref,
+    dstep_ref,
+    db_ref,
+    dc_ref,
+    ddecay_ref,
+    dstart_ref,
+    held,
+    after,
+):
+    @pl.when(pl.program_id(0) == 0)
+    def begin():
+        held[...] = jnp.zeros_like(held)
+        after[...] = end_ref[...]
+        ddecay_ref[...] = jnp.zeros_like(ddecay_ref)
+
+    decay = decay_ref[...]
+    rows, group, width = mixed_ref.shape[1:]
+    turns = group // 8
+
+    def eight(turn, carry):
+        base = pl.multiple_of((turns - 1 - turn) * 8, 8)
+        backs, states, sums = list(carry[0]), list(carry[1]), carry[2]
+        steps = [step_ref[0, row, pl.ds(base, 8), :] for row in range(rows)]
+        inputs = [mixed_ref[0, row, pl.ds(base, 8), :] for row in range(rows)]
+        grads = [grad_ref[0, row, pl.ds(base, 8), :] for row in range(rows)]
+        drives = [steps[row] * inputs[row] for row in range(rows)]
+        firsts = [[None] * 8 for row in range(rows)]
+        seconds = [[None] * 8 for row in range(rows)]
+        for k in reversed(range(8)):
+            for row in range(rows):
+                now = steps[row][k : k + 1]
+                grad = grads[row][k : k + 1]
+                past = past_ref[0, row, base + k]
+                fade = jnp.exp(now * decay)
+                back = widen(c_ref[0, row, base + k], width) * grad + backs[row]
+                dc_ref[0, row, base + k] = narrow(states[row] * grad)
+                firsts[row][k] = jnp.sum(
+                    widen(b_ref[0, row, base + k], width) * back, axis=0, keepdims=True
+                )
+                db_ref[0, row, base + k] = narrow(back * drives[row][k : k + 1])
+                faded = fade * back
+                flow = faded * past
+                seconds[row][k] = jnp.sum(flow * decay, axis=0, keepdims=True)
+                sums = sums + flow * now
+                backs[row] = faded
+                states[row] = past
+        for row in range(rows):
+            first = jnp.concatenate(firsts[row], axis=0)
+            second = jnp.concatenate(seconds[row], axis=0)
+            dmixed_ref[0, row, pl.ds(base, 8), :] = steps[row] * first
+            dstep_ref[0, row, pl.ds(base, 8), :] = inputs[row] * first + second
+        return (tuple(backs), tuple(states), sums)
+
+    backs, states, sums = lax.fori_loop(
+        0,
+        turns,
+        eight,
+        (
+            tuple(held[row] for row in range(rows)),
+            tuple(after[row] for row in range(rows)),
+            ddecay_ref[...],
+        ),
+    )
+    ddecay_ref[...] = sums
+    for row in range(rows):
+        held[row] = backs[row]
+        after[row] = states[row]
+        dstart_ref[row] = backs[row]
+
+
+def scan_back(order, mixed, step, wide_b, wide_c, grad, past, decay, end):
+    blocks, rows, group, width = mixed.shape
+    states = decay.shape[0]
+    last = blocks - 1
+    spec = pl.BlockSpec((1, rows, group, width), lambda i, order: (order[last - i], 0, 0, 0))
+    maps = pl.BlockSpec(
+        (1, rows, group, states, 128), lambda i, order: (order[last - i], 0, 0, 0, 0)
+    )
+    kept = pl.BlockSpec(
+        (1, rows, group, states, width), lambda i, order: (order[last - i], 0, 0, 0, 0)
+    )
+    whole = pl.BlockSpec((rows, states, width), lambda i, order: (0, 0, 0))
+    rates = pl.BlockSpec((states, width), lambda i, order: (0, 0))
+    return pl.pallas_call(
+        scan_back_body,
+        grid_spec=pltpu.PrefetchScalarGridSpec(
+            num_scalar_prefetch=1,
+            grid=(blocks,),
+            in_specs=[spec, spec, maps, maps, spec, kept, rates, whole],
+            out_specs=[spec, spec, maps, maps, rates, whole],
+            scratch_shapes=[
+                pltpu.VMEM((rows, states, width), F32),
+                pltpu.VMEM((rows, states, width), F32),
+            ],
+        ),
+        out_shape=[
+            jax.ShapeDtypeStruct(mixed.shape, F32),
+            jax.ShapeDtypeStruct(mixed.shape, F32),
+            jax.ShapeDtypeStruct((blocks, rows, group, states, 128), F32),
+            jax.ShapeDtypeStruct((blocks, rows, group, states, 128), F32),
+            jax.ShapeDtypeStruct(decay.shape, F32),
+            jax.ShapeDtypeStruct(end.shape, F32),
+        ],
+        compiler_params=params(),
+        name="scan_back",
+    )(order, mixed, step, wide_b, wide_c, grad, past, decay, end)
+
+
+def own_positions(shape, axis, first, member, group):
+    index = first + lax.broadcasted_iota(jnp.int32, shape, axis)
+    slot = index // group
+    block = (((slot & 2) << 1) | ((slot & 4) >> 1) | (slot & 1)) ^ member
+    return block * group + index % group
+
+
+def seen_cache(query, place, shape, group):
+    index = lax.broadcasted_iota(jnp.int32, shape, 1)
+    return (index + place * group) > query
+
+
+def seen_own(query, key, length):
+    return (key <= query) & ((key < length) | (key == query))
+
+
+def attend_body(meta_ref, q_ref, ck_ref, cv_ref, k_ref, v_ref, out_ref, log_ref):
+    count = q_ref.shape[0]
+    first = pl.program_id(1) * count
+    scale = HEAD_DIM ** (-0.5)
+    queries = q_ref[...]
+    pieces = ck_ref.shape[0]
+    size = ck_ref.shape[2]
+    tokens = k_ref.shape[0]
+    member = meta_ref[1]
+    group = tokens // pieces
+    query = own_positions((count, 1), 0, first, member, group)
+    scores = []
+    for piece in range(pieces):
+        score = dot(queries, ck_ref[piece, 0], 1, 1) * scale
+        inside = seen_cache(query, member ^ piece, (1, size), size)
+        scores.append(jnp.where(inside, score, NEGATIVE))
+    score = dot(queries, k_ref[...], 1, 1) * scale
+    key = own_positions((1, tokens), 1, 0, member, group)
+    scores.append(jnp.where(seen_own(query, key, meta_ref[0]), score, NEGATIVE))
+    top = jnp.max(scores[0], axis=1, keepdims=True)
+    for score in scores[1:]:
+        top = jnp.maximum(top, jnp.max(score, axis=1, keepdims=True))
+    total = jnp.zeros_like(top)
+    result = jnp.zeros((count, HEAD_DIM), F32)
+    for piece, score in enumerate(scores):
+        part = jnp.exp(score - top)
+        total = total + jnp.sum(part, axis=1, keepdims=True)
+        contents = cv_ref[piece, 0] if piece < pieces else v_ref[...]
+        result = result + dot(part.astype(BF), contents, 1, 0)
+    out_ref[...] = result / total
+    log_ref[0] = jnp.broadcast_to(top + jnp.log(total), (count, 128))
+
+
+def attend(meta, qkv, cache):
+    tokens, width = qkv.shape
+    width = width // 3
+    heads = width // HEAD_DIM
+    count = 256
+    shards, two, group, unused = cache.shape
+    own = lambda base: pl.BlockSpec((tokens, HEAD_DIM), lambda h, i, meta: (0, base + h))
+    held = lambda which: pl.BlockSpec(
+        (shards, 1, group, HEAD_DIM), lambda h, i, meta: (0, which, 0, h)
+    )
+    block = pl.BlockSpec((count, HEAD_DIM), lambda h, i, meta: (i, h))
+    return pl.pallas_call(
+        attend_body,
+        grid_spec=pltpu.PrefetchScalarGridSpec(
+            num_scalar_prefetch=1,
+            grid=(heads, tokens // count),
+            in_specs=[block, held(0), held(1), own(heads), own(2 * heads)],
+            out_specs=[block, pl.BlockSpec((1, count, 128), lambda h, i, meta: (h, i, 0))],
+        ),
+        out_shape=[
+            jax.ShapeDtypeStruct((tokens, width), F32),
+            jax.ShapeDtypeStruct((heads, tokens, 128), F32),
+        ],
+        compiler_params=params(),
+        name="attend",
+    )(meta, qkv, cache, cache, qkv, qkv)
+
+
+def attend_back_body(
+    meta_ref,
+    q_ref,
+    grad_ref,
+    out_ref,
+    log_ref,
+    ck_ref,
+    cv_ref,
+    k_ref,
+    v_ref,
+    dcache_ref,
+    dq_ref,
+    dk_ref,
+    dv_ref,
+    total,
+    delta,
+):
+    piece = pl.program_id(1)
+    pieces = pl.num_programs(1) - 1
+    scale = HEAD_DIM ** (-0.5)
+    queries = q_ref[...]
+    grad = grad_ref[...]
+    count = queries.shape[0]
+    size = ck_ref.shape[2]
+    member = meta_ref[1]
+    group = count // (2 * pieces)
+    query = own_positions((count, 1), 0, 0, member, group)
+
+    @pl.when(piece == 0)
+    def begin():
+        total[...] = jnp.zeros_like(total)
+        mine = jnp.sum(grad.astype(F32) * out_ref[...], axis=1, keepdims=True)
+        delta[...] = jnp.broadcast_to(mine, delta.shape)
+
+    def work(keys, contents, inside):
+        score = dot(queries, keys, 1, 1) * scale
+        part = jnp.where(inside, jnp.exp(score - log_ref[0][:, :1]), 0.0)
+        dcontents = dot(part.astype(BF), grad, 0, 0)
+        slope = dot(grad, contents, 1, 1)
+        dscore = (part * (slope - delta[:, :1])).astype(BF)
+        total[...] += dot(dscore, keys, 1, 0) * scale
+        return dot(dscore, queries, 0, 0) * scale, dcontents
+
+    @pl.when(piece < pieces)
+    def cached():
+        for half in range(2):
+            inside = seen_cache(query, member ^ (2 * piece + half), (1, size), size)
+            dkeys, dcontents = work(ck_ref[half, 0], cv_ref[half, 0], inside)
+            dcache_ref[half, 0] = dkeys.astype(BF)
+            dcache_ref[half, 1] = dcontents.astype(BF)
+
+    @pl.when(piece == pieces)
+    def own():
+        key = own_positions((1, count), 1, 0, member, group)
+        dkeys, dcontents = work(k_ref[...], v_ref[...], seen_own(query, key, meta_ref[0]))
+        dk_ref[...] = dkeys.astype(BF)
+        dv_ref[...] = dcontents.astype(BF)
+        dq_ref[...] = total[...].astype(BF)
+
+
+def attend_back(meta, qkv, grad, out, log, cache):
+    tokens, width = grad.shape
+    heads = width // HEAD_DIM
+    shards, two, group, unused = cache.shape
+    pieces = shards // 2
+    own = lambda base: pl.BlockSpec((tokens, HEAD_DIM), lambda h, i, meta: (0, base + h))
+    place = lambda i: jnp.minimum(i, pieces - 1)
+    held = lambda which: pl.BlockSpec(
+        (2, 1, group, HEAD_DIM), lambda h, i, meta: (place(i), which, 0, h)
+    )
+    result = jax.ShapeDtypeStruct((tokens, width), BF)
+    return pl.pallas_call(
+        attend_back_body,
+        grid_spec=pltpu.PrefetchScalarGridSpec(
+            num_scalar_prefetch=1,
+            grid=(heads, pieces + 1),
+            in_specs=[
+                own(0),
+                own(0),
+                own(0),
+                pl.BlockSpec((1, tokens, 128), lambda h, i, meta: (h, 0, 0)),
+                held(0),
+                held(1),
+                own(heads),
+                own(2 * heads),
+            ],
+            out_specs=[
+                pl.BlockSpec((2, 2, group, HEAD_DIM), lambda h, i, meta: (place(i), 0, 0, h)),
+                own(0),
+                own(0),
+                own(0),
+            ],
+            scratch_shapes=[
+                pltpu.VMEM((tokens, HEAD_DIM), F32),
+                pltpu.VMEM((tokens, 128), F32),
+            ],
+        ),
+        out_shape=[jax.ShapeDtypeStruct(cache.shape, BF), result, result, result],
+        compiler_params=params(),
+        name="attend_back",
+    )(meta, qkv, grad, out, log, cache, cache, qkv, qkv)
+
+
+def silu_slope(values):
+    sig = jax.nn.sigmoid(values)
+    return sig * (1.0 + values * (1.0 - sig))
+
+
+def norm_back(values, gain, grad):
+    back = jax.vjp(rms_gain, values, gain)[1](grad)
+    return back
+
+
+def plane_forward_ffn(stream, gain, gate_up, down):
+    rows, group, wide = stream.shape
+    normed = gather_plane(rms_gain(stream, gain).astype(BF)).reshape(-1, wide)
+    both = dot(normed, gate_up, 1, 0)
+    hidden_width = down.shape[0]
+    hidden = (jax.nn.silu(both[:, :hidden_width]) * both[:, hidden_width:]).astype(BF)
+    parts = dot(hidden, down, 1, 0).astype(BF).reshape(-1, rows, group, wide)
+    return stream + scatter_plane(parts), (normed, both, hidden)
+
+
+def plane_backward_ffn(stream, grad, grad_whole, gain, gate_up, down, kept):
+    normed, both, hidden = kept
+    rows, group, wide = stream.shape
+    hidden_width = down.shape[0]
+    grad_hidden = dot(grad_whole, down, 1, 1)
+    gate, up = both[:, :hidden_width], both[:, hidden_width:]
+    grad_both = jnp.concatenate(
+        [grad_hidden * up * silu_slope(gate), grad_hidden * jax.nn.silu(gate)], axis=1
+    ).astype(BF)
+    parts = dot(grad_both, gate_up, 1, 1).astype(BF).reshape(-1, rows, group, wide)
+    grad_normed = scatter_plane(parts)
+    grad_stream, grad_gain = norm_back(stream, gain, grad_normed)
+    grad_down = dot(hidden, grad_whole, 0, 0)
+    grad_gate_up = dot(normed, grad_both, 0, 0)
+    return grad + grad_stream, grad_gain, grad_gate_up, grad_down
+
+
+def plane_local(
+    activations,
+    cotangent,
+    carried_state,
+    carried_kv,
+    row_lengths,
+    mamba_gain,
+    mamba_in,
+    conv_weight,
+    conv_bias,
+    selection,
+    step_proj,
+    step_bias,
+    decay_log,
+    skip_gain,
+    mamba_out,
+    first_gain,
+    first_gate_up,
+    first_down,
+    attention_gain,
+    attention_qkv,
+    attention_out,
+    second_gain,
+    second_gate_up,
+    second_down,
+):
+    rows, group, wide = activations.shape
+    planes, inner = lax.axis_size("z"), lax.axis_size("x")
+    members = planes * inner
+    y, c, z, x = (lax.axis_index(name) for name in EVERY)
+    member = (y * 2 + c) * inner + x
+    place = z * inner + x
+    slots = jnp.arange(members) ^ member
+    order = (((slots & 2) << 1) | ((slots & 4) >> 1) | (slots & 1)).astype(jnp.int32)
+    tokens = swap_planes(activations)
+    stream = tokens.astype(F32)
+    lengths = swap_planes(row_lengths)
+
+    shard = mamba_gain.shape[0]
+    gains = jnp.stack([mamba_gain, first_gain, attention_gain, second_gain])
+    gains = gather_small(gains).reshape(planes, planes, inner, 4, shard).transpose(3, 1, 0, 2, 4)
+    gains = gains.reshape(4, wide).astype(F32)
+    channels = skip_gain.shape[0]
+    width = channels * planes
+    rank = step_proj.shape[0]
+    states = decay_log.shape[0]
+    cuts = (selection.shape[1], rank, CONV, 1, 1, states, 1)
+    packed = jnp.concatenate(
+        [
+            selection.astype(F32),
+            step_proj.astype(F32).T,
+            conv_weight.astype(F32).T,
+            conv_bias.astype(F32)[:, None],
+            step_bias[:, None],
+            decay_log.T,
+            skip_gain[:, None],
+        ],
+        axis=1,
+    )
+    packed = jnp.pad(packed, ((0, 0), (0, -packed.shape[1] % 128)))
+    packed = gather_z(relocate(packed, False)).reshape(width, -1)
+    starts = [sum(cuts[:index]) for index in range(len(cuts) + 1)]
+    pieces = [packed[:, starts[index] : starts[index + 1]] for index in range(len(cuts))]
+    own_selection = pieces[0].astype(BF)
+    own_step_proj = pieces[1].astype(BF)
+    taps = pieces[2].T
+    tap_bias = pieces[3].T
+    own_step_bias = pieces[4].T
+    decay = -jnp.exp(pieces[5].T)
+    skip = pieces[6].T
+    own_in = columns_in(
+        mamba_in.reshape(shard, 2, members, width).transpose(2, 0, 1, 3).reshape(members, shard, -1)
+    )
+    own_out = lax.all_gather(relocate(mamba_out, False), "z", axis=0, tiled=True)
+
+    def hidden_columns(gate_up, units):
+        split = gate_up.reshape(shard, 2, planes, planes, inner, units)
+        return split.transpose(2, 4, 0, 1, 3, 5).reshape(members, shard, -1)
+
+    units = first_down.shape[0]
+    head_width = wide // planes
+    split = attention_qkv.reshape(shard, 3, planes, head_width).transpose(2, 0, 1, 3)
+    split = jnp.broadcast_to(
+        split.reshape(planes, 1, shard, 3 * head_width), (planes, inner, shard, 3 * head_width)
+    )
+    dealt = trade(
+        jnp.concatenate(
+            [
+                hidden_columns(first_gate_up, units),
+                split.reshape(members, shard, 3 * head_width),
+                hidden_columns(second_gate_up, units),
+            ],
+            axis=2,
+        ),
+        PLANE,
+    )
+    edges = (0, 2 * planes * units, 2 * planes * units + 3 * head_width, dealt.shape[2])
+    own_first, own_qkv, own_second = (
+        rows_of(lax.all_gather(dealt[:, :, edges[k] : edges[k + 1]], "z", axis=0)) for k in range(3)
+    )
+    own_first_down = lax.all_gather(first_down, "z", axis=0, tiled=True)
+    own_attention_out = lax.all_gather(attention_out, ("z", "x"), axis=0, tiled=True)
+    own_second_down = lax.all_gather(second_down, "z", axis=0, tiled=True)
+    cache_rows = carried_kv.shape[1]
+    chunks = []
+    for k in range(members):
+        group_of, row_of = z ^ (k // inner), x ^ (k % inner)
+        row = lax.dynamic_index_in_dim(carried_kv, row_of, 0, False)
+        chunks.append(
+            jnp.stack(
+                [
+                    lax.dynamic_slice_in_dim(row, which * wide + group_of * head_width, head_width, 1)
+                    for which in range(2)
+                ]
+            )
+        )
+    cache = jnp.stack(deal(chunks, False))
+    start = swap_planes(lax.dynamic_slice_in_dim(carried_state, place * width, width, 2))
+    grad = swap_planes(cotangent)
+    grad_whole = gather_plane(grad).reshape(-1, wide)
+    grad = grad.astype(F32)
+
+    normed = gather_plane(tokens).reshape(-1, wide).astype(F32)
+    normed = rms_gain(normed, gains[0]).astype(BF)
+    projected = dot(normed, own_in, 1, 0).reshape(members, rows, group, 2 * width)
+    gate = projected[..., width:]
+    total, mixed, mixed_low = conv_forward(order, projected, taps, tap_bias)
+    flat_low = mixed_low.reshape(-1, width)
+    select = sum_plane(dot(flat_low, own_selection, 1, 0).reshape(members, rows, group, -1))
+    step_low = select[..., :rank].astype(BF).reshape(-1, rank)
+    pre = dot(step_low, own_step_proj, 1, 1).reshape(members, rows, group, width) + own_step_bias
+    blocks = jnp.zeros((members,), jnp.int32).at[order].set(jnp.arange(members, dtype=jnp.int32))
+    positions = blocks[:, None] * group + jnp.arange(group)[None, :]
+    valid = (positions[:, None, :] < lengths[None, :, None]).astype(F32)[..., None]
+    step = jax.nn.softplus(pre) * valid
+    wide_shape = (members, rows, group, states, 128)
+    wide_b = jnp.broadcast_to(select[..., rank : rank + states, None], wide_shape)
+    wide_c = jnp.broadcast_to(select[..., rank + states :, None], wide_shape)
+    core, past, end = scan_forward(order, mixed, step, wide_b, wide_c, decay, start)
+    mixed_out = core + skip * mixed
+    gated = (mixed_out * jax.nn.silu(gate)).astype(BF).reshape(-1, width)
+    parts = dot(gated, own_out, 1, 0).astype(BF).reshape(members, rows, group, wide)
+    first_stream = stream + scatter_plane(parts)
+    new_state = swap_planes(end)
+
+    second_stream, first_kept = plane_forward_ffn(first_stream, gains[1], own_first, own_first_down)
+
+    def kv_back(pieces, kind):
+        count = pieces[0].shape[1]
+        whole = jnp.zeros((rows, count, 2 * wide), kind)
+        for k, piece in enumerate(deal(pieces, True)):
+            group_of, row_of = z ^ (k // inner), x ^ (k % inner)
+            for which in range(2):
+                whole = lax.dynamic_update_slice(
+                    whole,
+                    piece[which : which + 1].astype(kind),
+                    (row_of, 0, which * wide + group_of * head_width),
+                )
+        return whole
+
+    length = jnp.concatenate([lax.dynamic_slice_in_dim(lengths, x, 1), member[None]])
+    normed_rows = rows_gather(rms_gain(second_stream, gains[2]).astype(BF)).reshape(-1, wide)
+    qkv = dot(normed_rows, own_qkv, 1, 0).astype(BF)
+    attended, log = attend(length, qkv, cache)
+    attended_low = attended.astype(BF)
+    parts = dot(attended_low, own_attention_out, 1, 0).astype(BF)
+    third_stream = second_stream + rows_scatter(parts.reshape(members, group, wide))
+    slot_of = [((k & 2) << 1) | ((k & 4) >> 1) | (k & 1) for k in range(members)]
+    own_kv = qkv[:, head_width:].reshape(members, group, 2, head_width).transpose(0, 2, 1, 3)
+    segment_kv = kv_back([own_kv[slot_of[k]] for k in range(members)], BF)
+
+    fourth_stream, second_kept = plane_forward_ffn(
+        third_stream, gains[3], own_second, own_second_down
+    )
+    output = swap_planes(fourth_stream.astype(BF))
+
+    def hidden_back(grad_columns):
+        got = columns_out(grad_columns).astype(F32)
+        got = got.reshape(planes, inner, shard, 2, planes, units)
+        return got.transpose(2, 3, 0, 4, 1, 5).reshape(shard, -1)
+
+    def down_back(grad_down):
+        return reduce_z(grad_down.astype(BF).reshape(planes, units, wide)).astype(F32)
+
+    grad, second_gain_grad, grad_columns, grad_down = plane_backward_ffn(
+        third_stream, grad, grad_whole, gains[3], own_second, own_second_down, second_kept
+    )
+    second_gate_up_grad = hidden_back(grad_columns)
+    second_down_grad = down_back(grad_down)
+
+    grad_rows = rows_gather(grad.astype(BF)).reshape(-1, wide)
+    grad_attended = dot(grad_rows, own_attention_out, 1, 1).astype(BF)
+    grad_cache, dq, dk, dv = attend_back(length, qkv, grad_attended, attended, log, cache)
+    grad_qkv = jnp.concatenate([dq, dk, dv], axis=1)
+    parts = dot(grad_qkv, own_qkv, 1, 1).astype(BF)
+    grad_normed = rows_scatter(parts.reshape(members, group, wide))
+    grad_stream, attention_gain_grad = norm_back(second_stream, gains[2], grad_normed)
+    grad = grad + grad_stream
+    grad_cache = kv_back([grad_cache[k] for k in range(members)], F32)
+    grad_out = dot(attended_low, grad_rows, 0, 0).astype(BF)
+    grad_out = reduce_z(grad_out.reshape(planes, inner, shard, wide))
+    theirs = other(lax.dynamic_index_in_dim(grad_out, 1 - x, 0, False), "x").astype(F32)
+    attention_out_grad = lax.dynamic_index_in_dim(grad_out, x, 0, False).astype(F32) + theirs
+    got = columns_out(dot(normed_rows, grad_qkv, 0, 0)).astype(F32)
+    got = jnp.sum(got.reshape(planes, inner, shard, 3, head_width), axis=1)
+    attention_qkv_grad = got.transpose(1, 2, 0, 3).reshape(shard, 3 * wide)
+
+    grad_whole = gather_plane(grad.astype(BF)).reshape(-1, wide)
+    grad, first_gain_grad, grad_columns, grad_down = plane_backward_ffn(
+        first_stream, grad, grad_whole, gains[1], own_first, own_first_down, first_kept
+    )
+    first_gate_up_grad = hidden_back(grad_columns)
+    first_down_grad = down_back(grad_down)
+
+    grad_whole = gather_plane(grad.astype(BF)).reshape(-1, wide)
+    grad_gated = dot(grad_whole, own_out, 1, 1).reshape(mixed.shape)
+    grad_core = grad_gated * jax.nn.silu(gate)
+    grad_gate = (grad_gated * mixed_out * silu_slope(gate)).astype(BF)
+    skip_grad = jnp.sum(grad_core * mixed, axis=(0, 1, 2))
+    grad_mixed, grad_step, grad_b, grad_c, grad_decay, grad_start = scan_back(
+        order, mixed, step, wide_b, wide_c, grad_core, past, decay, end
+    )
+    grad_state = swap_planes(grad_start)
+    grad_pre = grad_step * valid * jax.nn.sigmoid(pre)
+    step_bias_grad = jnp.sum(grad_pre, axis=(0, 1, 2))
+    grad_pre = grad_pre.astype(BF).reshape(-1, width)
+    step_proj_grad = dot(grad_pre, step_low, 0, 0)
+    grad_low = dot(grad_pre, own_step_proj, 1, 0).reshape(members, rows, group, rank)
+    grad_select = sum_plane(
+        jnp.concatenate([grad_low, jnp.sum(grad_b, axis=-1), jnp.sum(grad_c, axis=-1)], axis=-1)
+    )
+    grad_select = grad_select.astype(BF).reshape(-1, rank + 2 * states)
+    selection_grad = dot(flat_low, grad_select, 0, 0)
+    grad_mixed = (
+        grad_mixed
+        + grad_core * skip
+        + dot(grad_select, own_selection, 1, 1).reshape(mixed.shape)
+    )
+    grad_inner, tap_sums = conv_back(order, grad_mixed, total, projected, taps)
+    grad_projected = jnp.concatenate([grad_inner, grad_gate], axis=-1).reshape(-1, 2 * width)
+    parts = dot(grad_projected, own_in, 1, 1).astype(BF).reshape(members, rows, group, wide)
+    grad_normed = scatter_plane(parts)
+    grad_stream, mamba_gain_grad = norm_back(stream, gains[0], grad_normed)
+    grad_input = swap_planes(grad + grad_stream)
+
+    got = columns_out(dot(normed, grad_projected, 0, 0)).astype(F32)
+    got = got.reshape(members, shard, 2, width)
+    mamba_in_grad = got.transpose(1, 2, 0, 3).reshape(shard, -1)
+    grad_out = dot(gated, grad_whole, 0, 0).astype(BF).reshape(planes, channels, wide)
+    mamba_out_grad = relocate(reduce_z(grad_out), True).astype(F32)
+    packed = jnp.concatenate(
+        [
+            selection_grad,
+            step_proj_grad,
+            tap_sums[: CONV + 1].T,
+            step_bias_grad[:, None],
+            (grad_decay * decay).T,
+            skip_grad[:, None],
+        ],
+        axis=1,
+    )
+    packed = jnp.pad(packed, ((0, 0), (0, -packed.shape[1] % 128)))
+    packed = packed.reshape(planes, channels, -1)
+    summed = lax.dynamic_index_in_dim(packed, z, 0, False)
+    for distance in range(1, planes):
+        goal = (z + distance) % planes
+        summed = summed + turned(lax.dynamic_index_in_dim(packed, goal, 0, False), distance)
+    packed = relocate(summed, True)
+    pieces = [packed[:, starts[index] : starts[index + 1]] for index in range(len(cuts))]
+
+    gain_grads = total_small(jnp.stack([first_gain_grad, attention_gain_grad, second_gain_grad]))
+    mamba_gain_grad = total_small(mamba_gain_grad[None])
+    gain_grads = jnp.concatenate([mamba_gain_grad, gain_grads], axis=0)
+    index = ((y * 2 + c) * planes + z) * inner + x
+    gain_grads = lax.dynamic_slice_in_dim(gain_grads, index * shard, shard, 1)
+    return (
+        output,
+        new_state,
+        segment_kv,
+        grad_input,
+        grad_state,
+        grad_cache,
+        gain_grads[0],
+        mamba_in_grad,
+        pieces[2].T,
+        pieces[3][:, 0],
+        pieces[0],
+        pieces[1].T,
+        pieces[4][:, 0],
+        pieces[5].T,
+        pieces[6][:, 0],
+        mamba_out_grad,
+        gain_grads[1],
+        first_gate_up_grad,
+        first_down_grad,
+        gain_grads[2],
+        attention_qkv_grad,
+        attention_out_grad,
+        gain_grads[3],
+        second_gate_up_grad,
+        second_down_grad,
+    )
+
+
+def placements(dp, seq):
+    every = dp + seq
+    places = (
+        P(dp, seq, None),
+        P(dp, seq, None),
+        P(dp, None, None),
+        P(dp, seq, None),
+        P(dp),
+        P(every),
+        P(every, None),
+        P(None, every),
+        P(every),
+        P(every, None),
+        P(None, every),
+        P(every),
+        P(None, every),
+        P(every),
+        P(every, None),
+        P(every),
+        P(every, None),
+        P(every, None),
+        P(every),
+        P(every, None),
+        P(every, None),
+        P(every),
+        P(every, None),
+        P(every, None),
+
+    )
+    results = (
+        P(dp, seq, None),
+        P(dp, None, seq),
+        P(dp, seq, None),
+        P(dp, seq, None),
+        P(dp, None, seq),
+        P(dp, seq, None),
+        P(every),
+        P(every, None),
+        P(None, every),
+        P(every),
+        P(every, None),
+        P(None, every),
+        P(every),
+        P(None, every),
+        P(every),
+        P(every, None),
+        P(every),
+        P(every, None),
+        P(every, None),
+        P(every),
+        P(every, None),
+        P(every, None),
+        P(every),
+        P(every, None),
+        P(every, None),
+
+    )
+    return places, results
+
+
+def plane_fits(mesh):
+    dp, seq = mesh.shape["dp"], mesh.shape["seq"]
+    return dp == 4 and seq == 2 * dp
+
+
 def solution(mesh):
+    if not plane_fits(mesh):
+        places, results = placements(("dp",), ("seq",))
+        return jax.shard_map(
+            local, mesh=mesh, in_specs=places, out_specs=results, check_vma=False
+        )
+    dp, seq = mesh.shape["dp"], mesh.shape["seq"]
+    devices = mesh.devices.reshape(dp // 2, 2, dp, seq // dp)
+    places, results = placements(("y", "c"), ("z", "x"))
     return jax.shard_map(
-        local,
-        mesh=mesh,
-        in_specs=(
-            P("dp", "seq", None),
-            P("dp", "seq", None),
-            P("dp", None, None),
-            P("dp", "seq", None),
-            P("dp"),
-            P(("dp", "seq")),
-            P(("dp", "seq"), None),
-            P(None, ("dp", "seq")),
-            P(("dp", "seq")),
-            P(("dp", "seq"), None),
-            P(None, ("dp", "seq")),
-            P(("dp", "seq")),
-            P(None, ("dp", "seq")),
-            P(("dp", "seq")),
-            P(("dp", "seq"), None),
-            P(("dp", "seq")),
-            P(("dp", "seq"), None),
-            P(("dp", "seq"), None),
-            P(("dp", "seq")),
-            P(("dp", "seq"), None),
-            P(("dp", "seq"), None),
-            P(("dp", "seq")),
-            P(("dp", "seq"), None),
-            P(("dp", "seq"), None),
-        ),
-        out_specs=(
-            P("dp", "seq", None),
-            P("dp", None, "seq"),
-            P("dp", "seq", None),
-            P("dp", "seq", None),
-            P("dp", None, "seq"),
-            P("dp", "seq", None),
-            P(("dp", "seq")),
-            P(("dp", "seq"), None),
-            P(None, ("dp", "seq")),
-            P(("dp", "seq")),
-            P(("dp", "seq"), None),
-            P(None, ("dp", "seq")),
-            P(("dp", "seq")),
-            P(None, ("dp", "seq")),
-            P(("dp", "seq")),
-            P(("dp", "seq"), None),
-            P(("dp", "seq")),
-            P(("dp", "seq"), None),
-            P(("dp", "seq"), None),
-            P(("dp", "seq")),
-            P(("dp", "seq"), None),
-            P(("dp", "seq"), None),
-            P(("dp", "seq")),
-            P(("dp", "seq"), None),
-            P(("dp", "seq"), None),
-        ),
+        plane_local,
+        mesh=Mesh(devices, EVERY),
+        in_specs=places,
+        out_specs=results,
         check_vma=False,
     )

time: 5620 us -> 1330 us (0.24)
  waiting for transfers between devices: 3770 us -> 309 us
  starting transfers between devices: 7.41 us -> 521 us
  blocking collectives: 429 us -> 0 us
  matrix products: 459 us -> 102 us
  other arithmetic: 415 us -> 108 us
  local copies, waits for them, and re-layouts: 451 us -> 154 us
  Pallas kernels: 0 us -> 107 us
    reduce_scatter x10 -> x8, waiting for transfers between devices: 2530 us -> 0.03 us  [reduce_z(): return lax.psum_scatter(parts, 'z', scatter_dimension=0)]
    all_gather x14 -> x8, waiting for transfers between devices: 1140 us -> 16.7 us  [the longest x1 11 us: columns_in(): return rows_of(lax.all_gather(trade(payload, PLANE), 'z', axis=0))]
    ppermute x2 -> x153, starting transfers between devices: 5.92 us -> 491 us  [the longest x102 312 us: other(): return lax.ppermute(block, axis, [(0, 1), (1, 0)])]
    dot_general x86 -> x30, matrix products: 459 us -> 102 us  [dot(): lax.dot_general(left, right, (((left_dim,), (right_dim,)), ((), ())), pre...]
    all_gather x6 -> x0, blocking collectives: 346 us -> none  [the longest x1 74.8 us: fetch_front(): lax.all_gather(shards[5], ('dp', 'seq'), axis=1, tiled=True)]
    ppermute x2 -> x153, waiting for transfers between devices: 4.27 us -> 284 us  [the longest x102 202 us: other(): return lax.ppermute(block, axis, [(0, 1), (1, 0)])]
    reduce_sum x107 -> x8, other arithmetic: 130 us -> 19.8 us  [the longest x1 5.64 us: plane_local(): jnp.sum(grad_c, axis=-1)]
    pallas_call x0 -> x6, Pallas kernels: none -> 107 us  [the longest x1 29.4 us: scan_back(): pl.pallas_call(scan_back_body, grid_spec=pltpu.PrefetchScalarGridSpec(num...]
  transfers between devices with their start and end apart: 29 -> 175, of which waited for: 22 -> 75; matrix products, arithmetic and copies ran while one was open for 13% -> 25% of each run, Pallas kernels for 0% -> 8%
where the time goes in v1:
time: 1330 us; the launch traced here: 1320 us
  starting transfers between devices  521 us (39%)
  waiting for transfers between devices  309 us (23%)
  local copies, waits for them, and re-layouts  154 us (12%)
  other arithmetic  108 us (8%)
  Pallas kernels  107 us (8%)
  matrix products  102 us (8%)
  between operations  17.8 us (1%)
    ppermute x102, starting transfers between devices, other(): return lax.ppermute(block, axis, [(0, 1), (1, 0)])  312 us
    ppermute x102, waiting for transfers between devices, other(): return lax.ppermute(block, axis, [(0, 1), (1, 0)])  202 us
    ppermute x24, starting transfers between devices, deal(): result.append(lax.ppermute(piece, EVERY, route))  128 us
    dot_general x30, matrix products, dot(): lax.dot_general(left, right, (((left_dim,), (right_dim,)), ((), ())), pre...  102 us
    ppermute x15, waiting for transfers between devices, turned(): lax.ppermute(block, 'z', [(z, (z + distance) % planes) for z in range(pla...  42.9 us
    unnamed x361, local copies, waits for them, and re-layouts  39.6 us
    ppermute x24, waiting for transfers between devices, deal(): result.append(lax.ppermute(piece, EVERY, route))  38.9 us
    pallas_call x1, Pallas kernels, scan_back(): pl.pallas_call(scan_back_body, grid_spec=pltpu.PrefetchScalarGridSpec(num...  29.4 us
  transfers between devices with their start and end apart: 175, of which 75 were waited for; matrix products, arithmetic and copies ran while one was open for 25% of the time, Pallas kernels for 8%

profile of v1, /device:TPU:0, one launch (start us, length us, event | category | flops | bytes accessed | tf_op | source)
XLA Modules:
  0.0 1318.3 jit_solution(11309371048661505692)
XLA Ops:
  15.5 6.5 all-to-all-start
  68.8 5.4 collective-permute-done.13
  75.4 6.4 collective-permute-done.14
  81.9 6.3 collective-permute-done.15
  107.7 20.8 %collective-permute-done.3 = bf16[1,64,1536]{2,1,0:T(8,128)(2,1)S(1)} collective-permute-done((bf16[1,64,1536]{2,1,0:T(8,128)(2,1)S(1)}, bf16[1,64,1536]{2,1,0:T(8,128)(2,1)S(1)}, u32[]{:S(2)}, u32[]{:S(2)}) %collective-permute-start.3) | collective-permute-done | bytes 196640 | tf_op jit(solution)/shard_map/ppermute | solution.py:709
  135.9 11.0 all-gather.21.cloned.1.call-done
  154.7 7.3 conv_forward.1
  202.6 22.9 %scan_forward.1 = (f32[8,2,64,384]{3,2,1,0:T(8,128)}, f32[8,2,64,16,384]{4,3,2,1,0:T(8,128)}, f32[2,16,384]{2,1,0:T(8,128)}) custom-call(s32[8]{0:T(128)} %and_or_fusion.order, f32[8,2,64,384]{3,2,1,0:T(8,128)} %get-tuple-element.45.mixed_ref, f32[8,2,64,384]{3,2,1,0:T(8,128)} %get-tuple-element.402.step_ref, f32[8,2,64,16,128]{4,3,2,1,0:T(8,128)} %broadcast_in_dim.79.b_ref, ...), custom_call_target="tpu_custom_call" | custom-call | tf_op jit(solution)/shard_map/scan_forward/pallas_call | solution.py:1003
  247.9 7.1 collective-permute-done.31
  261.4 7.5 collective-permute-done.35
  290.2 5.6 all-gather.15.cloned.1.call-done
  338.0 8.6 collective-permute-done.41
  346.6 28.2 %collective-permute-start.51 = (bf16[2,256,384]{2,1,0:T(8,128)(2,1)}, bf16[2,256,384]{2,1,0:T(8,128)(2,1)S(1)}, u32[]{:S(2)}, u32[]{:S(2)}) collective-permute-start(bf16[2,256,384]{2,1,0:T(8,128)(2,1)} %pad_maximum_fusion.29), channel_id=1, source_target_pairs={{0,16},{1,17},{2,24},{3,25},{4,0},{5,1},{6,8},{7,9},{8,18},{9,19},... | collective-permute-start | bytes 1179656 | tf_op jit(solution)/shard_map/ppermute | solution.py:784
  379.8 21.7 %collective-permute-done.44 = bf16[64,1536]{1,0:T(8,128)(2,1)S(1)} collective-permute-done((bf16[64,1536]{1,0:T(8,128)(2,1)S(1)}, bf16[64,1536]{1,0:T(8,128)(2,1)S(1)}, u32[]{:S(2)}, u32[]{:S(2)}) %collective-permute-start.44) | collective-permute-done | bytes 196640 | tf_op jit(solution)/shard_map/ppermute | solution.py:709
  401.6 33.7 %collective-permute-start.45 = (bf16[2,64,1536]{2,1,0:T(8,128)(2,1)S(1)}, bf16[2,64,1536]{2,1,0:T(8,128)(2,1)S(1)}, u32[]{:S(2)}, u32[]{:S(2)}) collective-permute-start(bf16[2,64,1536]{2,1,0:T(8,128)(2,1)S(1)} %pad_maximum_fusion.24), channel_id=1, source_target_pairs={{0,16},{16,0},{1,17},{17,1},{2,18},{18,2},{3,19},{19,3},{4,20},{20... | collective-permute-start | bytes 1179656 | tf_op jit(solution)/shard_map/ppermute | solution.py:709
  436.4 28.4 %collective-permute-start.54 = (bf16[2,256,384]{2,1,0:T(8,128)(2,1)S(1)}, bf16[2,256,384]{2,1,0:T(8,128)(2,1)S(1)}, u32[]{:S(2)}, u32[]{:S(2)}) collective-permute-start(bf16[2,256,384]{2,1,0:T(8,128)(2,1)S(1)} %copy-done.77), channel_id=1, source_target_pairs={{0,25},{1,24},{2,17},{3,16},{4,9},{5,8},{6,1},{7,0},{8,27},{9,26},... | collective-permute-start | bytes 1179656 | tf_op jit(solution)/shard_map/ppermute | solution.py:784
  467.5 21.3 %collective-permute-done.51 = bf16[2,256,384]{2,1,0:T(8,128)(2,1)S(1)} collective-permute-done((bf16[2,256,384]{2,1,0:T(8,128)(2,1)}, bf16[2,256,384]{2,1,0:T(8,128)(2,1)S(1)}, u32[]{:S(2)}, u32[]{:S(2)}) %collective-permute-start.51) | collective-permute-done | bytes 393248 | tf_op jit(solution)/shard_map/ppermute | solution.py:784
  488.9 14.6 %collective-permute-done.52 = bf16[2,256,384]{2,1,0:T(8,128)(2,1)S(1)} collective-permute-done((bf16[2,256,384]{2,1,0:T(8,128)(2,1)}, bf16[2,256,384]{2,1,0:T(8,128)(2,1)S(1)}, u32[]{:S(2)}, u32[]{:S(2)}) %collective-permute-start.52) | collective-permute-done | bytes 393248 | tf_op jit(solution)/shard_map/ppermute | solution.py:784
  513.6 11.2 attend.1
  527.4 23.4 %collective-permute-start.55 = (bf16[4,64,1536]{2,1,0:T(8,128)(2,1)S(1)}, bf16[4,64,1536]{2,1,0:T(8,128)(2,1)S(1)}, u32[]{:S(2)}, u32[]{:S(2)}) collective-permute-start(bf16[4,64,1536]{2,1,0:T(8,128)(2,1)S(1)} %bitcast.762), channel_id=1, source_target_pairs={{0,8},{8,0},{1,9},{9,1},{2,10},{10,2},{3,11},{11,3},{4,12},{12,4},... | collective-permute-start | bytes 2359304 | tf_op jit(solution)/shard_map/ppermute | solution.py:709
  550.8 10.4 collective-permute-start.80
  563.5 7.8 collective-permute-done.80
  593.4 5.5 collective-permute-done.59
  622.6 6.2 multiply_convert_fusion.3
  662.1 6.2 collective-permute-done.86
  669.2 6.3 collective-permute-done.65
  684.5 7.8 collective-permute-done.90
  704.4 6.7 collective-permute-start.72
  711.7 9.0 collective-permute-start.74
  720.6 10.7 collective-permute-start.75
  752.3 28.2 %attend_back.1 = (bf16[8,2,256,384]{3,2,1,0:T(8,128)(2,1)}, bf16[512,384]{1,0:T(8,128)(2,1)}, bf16[512,384]{1,0:T(8,128)(2,1)}, bf16[512,384]{1,0:T(8,128)(2,1)}) custom-call(s32[2]{0:T(128)} %pad_add_fusion.meta_ref, bf16[512,1152]{1,0:T(8,128)(2,1)} %convolution_convert_fusion.10.q_ref.k_ref.v_ref, bf16[512,384]{1,0:T(8,128)(2,1)} %convolution_convert_fusion.15.grad_ref, ...), custom_call_target="tpu_custom_call" | custom-call | tf_op jit(solution)/shard_map/attend_back/pallas_call | solution.py:1301
  789.3 31.3 %collective-permute-start.92 = (bf16[4,64,1536]{2,1,0:T(8,128)(2,1)}, bf16[4,64,1536]{2,1,0:T(8,128)(2,1)S(1)}, u32[]{:S(2)}, u32[]{:S(2)}) collective-permute-start(bf16[4,64,1536]{2,1,0:T(8,128)(2,1)} %bitcast.152), channel_id=1, source_target_pairs={{0,8},{8,0},{1,9},{9,1},{2,10},{10,2},{3,11},{11,3},{4,12},{12,4},... | collective-permute-start | bytes 2359304 | tf_op jit(solution)/shard_map/ppermute | solution.py:709
  838.2 18.2 %collective-permute-start.131 = (bf16[2,256,384]{2,1,0:T(8,128)(2,1)}, bf16[2,256,384]{2,1,0:T(8,128)(2,1)S(1)}, u32[]{:S(2)}, u32[]{:S(2)}) collective-permute-start(bf16[2,256,384]{2,1,0:T(8,128)(2,1)} %get-tuple-element.263), channel_id=1, source_target_pairs={{0,4},{1,5},{2,12},{3,13},{4,20},{5,21},{6,28},{7,29},{8,6},{9,7},... | collective-permute-start | bytes 1179656 | tf_op jit(solution)/shard_map/ppermute | solution.py:784
  856.7 57.2 %collective-permute-start.93 = (bf16[2,64,1536]{2,1,0:T(8,128)(2,1)S(1)}, bf16[2,64,1536]{2,1,0:T(8,128)(2,1)S(1)}, u32[]{:S(2)}, u32[]{:S(2)}) collective-permute-start(bf16[2,64,1536]{2,1,0:T(8,128)(2,1)S(1)} %slice.1582), channel_id=1, source_target_pairs={{0,16},{16,0},{1,17},{17,1},{2,18},{18,2},{3,19},{19,3},{4,20},{20... | collective-permute-start | bytes 1179656 | tf_op jit(solution)/shard_map/ppermute | solution.py:709
  928.2 20.8 %collective-permute-start.96 = (bf16[2,64,1536]{2,1,0:T(8,128)(2,1)S(1)}, bf16[2,64,1536]{2,1,0:T(8,128)(2,1)S(1)}, u32[]{:S(2)}, u32[]{:S(2)}) collective-permute-start(bf16[2,64,1536]{2,1,0:T(8,128)(2,1)S(1)} %get-tuple-element.239), channel_id=1, source_target_pairs={{0,16},{16,0},{1,17},{17,1},{2,18},{18,2},{3,19},{19,3},{4,20},{20... | collective-permute-start | bytes 1179656 | tf_op jit(solution)/shard_map/ppermute | solution.py:709
  950.7 10.0 collective-permute-start.132
  970.4 9.0 collective-permute-start.99
  995.3 19.9 %collective-permute-start.101 = (bf16[1,64,1536]{2,1,0:T(8,128)(2,1)}, bf16[1,64,1536]{2,1,0:T(8,128)(2,1)}, u32[]{:S(2)}, u32[]{:S(2)}) collective-permute-start(bf16[1,64,1536]{2,1,0:T(8,128)(2,1)} %get-tuple-element.326), channel_id=1, source_target_pairs={{0,16},{16,0},{1,17},{17,1},{2,18},{18,2},{3,19},{19,3},{4,20},{20... | collective-permute-start | bytes 589832 | tf_op jit(solution)/shard_map/ppermute | solution.py:709
  1081.1 6.5 multiply_reduce_fusion
  1087.6 29.4 %scan_back.1 = (f32[8,2,64,384]{3,2,1,0:T(8,128)}, f32[8,2,64,384]{3,2,1,0:T(8,128)}, f32[8,2,64,16,128]{4,3,2,1,0:T(8,128)}, f32[8,2,64,16,128]{4,3,2,1,0:T(8,1...) custom-call(s32[8]{0:T(128)} %and_or_fusion.order, f32[8,2,64,384]{3,2,1,0:T(8,128)} %get-tuple-element.45.mixed_ref, ...), custom_call_target="tpu_custom_call" | custom-call | tf_op jit(solution)/shard_map/scan_back/pallas_call | solution.py:1128
  1117.0 5.6 reduce_sum.169
  1122.7 5.6 reduce_sum.170
  1142.9 7.5 all-to-all-done.4
  1180.0 8.1 conv_back.1
  1218.9 9.0 collective-permute-start.122
  1261.1 7.4 collective-permute-start.125
  1286.4 5.5 all-to-all-start.2
  1291.9 12.1 collective-permute-done.139
  (1029 shorter events, 634.3 us)
Async XLA Ops:
  11.0 77.3 %collective-permute-start = (bf16[2,64,1536]{2,1,0:T(8,128)(2,1)}, bf16[2,64,1536]{2,1,0:T(8,128)(2,1)S(1)}, u32[]{:S(2)}, u32[]{:S(2)}) collective-permute-start(bf16[2,64,1536]{2,1,0:T(8,128)(2,1)} %param.24), channel_id=1, source_target_pairs={{0,0},{1,1},{2,8},{3,9},{4,16},{5,17},{6,24},{7,25},{8,2},{9,3},{1... | collective-permute-start | bytes 1179656 | tf_op jit(solution)/shard_map/ppermute | solution.py:705
  15.5 74.8 %all-to-all-start = ((bf16[8,48,768]{2,1,0:T(8,128)(2,1)}), bf16[8,48,768]{2,1,0:T(8,128)(2,1)S(1)}, u32[]{:S(2)}, u32[]{:S(2)}) async-start(bf16[8,48,768]{2,1,0:T(8,128)(2,1)} %reshape.602), calls=%async_computation | async-start | bytes 1179648 | tf_op jit(solution)/shard_map/all_to_all | solution.py:738
  24.2 44.3 %collective-permute-start.12 = (f32[96,256]{1,0:T(8,128)}, f32[96,256]{1,0:T(8,128)S(1)}, u32[]{:S(2)}, u32[]{:S(2)}) collective-permute-start(f32[96,256]{1,0:T(8,128)} %pad.8), channel_id=1, source_target_pairs={{0,0},{1,2},{2,4},{3,6},{4,1},{5,3},{6,5},{7,7},{8,8},{9,10},{10,1... | collective-permute-start | bytes 294920 | tf_op jit(solution)/shard_map/ppermute | solution.py:838
  25.7 143.2 %collective-permute-start.26 = (s32[2]{0:T(128)}, s32[2]{0:T(128)}, u32[]{:S(2)}, u32[]{:S(2)}) collective-permute-start(s32[2]{0:T(128)} %param.28), channel_id=1, source_target_pairs={{0,0},{1,1},{2,8},{3,9},{4,16},{5,17},{6,24},{7,25},{8,2},{9,3},{1... | collective-permute-start | bytes 32 | tf_op jit(solution)/shard_map/ppermute | solution.py:705
  28.3 165.2 %collective-permute-start.27 = (f32[2,16,384]{2,1,0:T(8,128)}, f32[2,16,384]{2,1,0:T(8,128)}, u32[]{:S(2)}, u32[]{:S(2)}) collective-permute-start(f32[2,16,384]{2,1,0:T(8,128)} %constant_dynamic-slice_fusion.18), channel_id=1, source_target_pairs={{0,0},{1,1},{2,8},{3,9},{4,16},{5,17},{6,24},{7,25},{8,2},{9,3},{1... | collective-permute-start | bytes 147464 | tf_op jit(solution)/shard_map/ppermute | solution.py:705
  63.9 100.3 %collective-permute-start.28 = (bf16[96,1536]{1,0:T(8,128)(2,1)}, bf16[96,1536]{1,0:T(8,128)(2,1)}, u32[]{:S(2)}, u32[]{:S(2)}) collective-permute-start(bf16[96,1536]{1,0:T(8,128)(2,1)} %param.38), channel_id=1, source_target_pairs={{0,0},{1,2},{2,4},{3,6},{4,1},{5,3},{6,5},{7,7},{8,8},{9,10},{10,1... | collective-permute-start | bytes 884744 | tf_op jit(solution)/shard_map/ppermute | solution.py:838
  91.2 87.8 %all-to-all-start.1 = ((bf16[8,48,3200]{2,1,0:T(8,128)(2,1)}), bf16[8,48,3200]{2,1,0:T(8,128)(2,1)S(1)}, u32[]{:S(2)}, u32[]{:S(2)}) async-start(bf16[8,48,3200]{2,1,0:T(8,128)(2,1)} %pad_maximum_fusion), calls=%async_computation.1 | async-start | bytes 4915200 | tf_op jit(solution)/shard_map/all_to_all | solution.py:738
  94.8 52.1 %all-gather.21.cloned.1.call-start = ((), (), s32[]{:S(2)}) async-start(), calls=%async_computation.26 | async-start | bytes 2949120 | tf_op jit(solution)/shard_map/all_gather | solution.py:825
  95.5 133.3 %all-gather.13.cloned.1.call-start = ((), (), s32[]{:S(2)}) async-start(), calls=%async_computation.14 | async-start | bytes 1474560 | tf_op jit(solution)/shard_map/all_gather | solution.py:1443
  164.2 114.6 %all-gather.23.cloned.1.call-start = ((), (), s32[]{:S(2)}) async-start(), calls=%async_computation.27 | async-start | bytes 3932160 | tf_op jit(solution)/shard_map/all_gather | solution.py:1468
  180.6 115.2 %all-gather.15.cloned.1.call-start = ((), (), s32[]{:S(2)}) async-start(), calls=%async_computation.15 | async-start | bytes 1966080 | tf_op jit(solution)/shard_map/all_gather | solution.py:1470
  247.4 256.3 %all-gather.25.cloned.1.call-start = ((), (), s32[]{:S(2)}) async-start(), calls=%async_computation.28 | async-start | bytes 4423680 | tf_op jit(solution)/shard_map/all_gather | solution.py:1468
  278.8 246.0 %all-gather.17.cloned.1.call-start = ((), (), s32[]{:S(2)}) async-start(), calls=%async_computation.16 | async-start | bytes 1327104 | tf_op jit(solution)/shard_map/all_gather | solution.py:1471
  310.6 66.7 %collective-permute-start.48 = (bf16[2,256,384]{2,1,0:T(8,128)(2,1)}, bf16[2,256,384]{2,1,0:T(8,128)(2,1)}, u32[]{:S(2)}, u32[]{:S(2)}) collective-permute-start(bf16[2,256,384]{2,1,0:T(8,128)(2,1)} %pad_maximum_fusion.26), channel_id=1, source_target_pairs={{0,1},{1,0},{2,9},{3,8},{4,17},{5,16},{6,25},{7,24},{8,3},{9,2},{1... | collective-permute-start | bytes 1179656 | tf_op jit(solution)/shard_map/ppermute | solution.py:784
  312.8 88.8 %collective-permute-start.49 = (bf16[2,256,384]{2,1,0:T(8,128)(2,1)}, bf16[2,256,384]{2,1,0:T(8,128)(2,1)}, u32[]{:S(2)}, u32[]{:S(2)}) collective-permute-start(bf16[2,256,384]{2,1,0:T(8,128)(2,1)} %pad_maximum_fusion.27), channel_id=1, source_target_pairs={{0,8},{1,9},{2,0},{3,1},{4,24},{5,25},{6,16},{7,17},{8,10},{9,11},... | collective-permute-start | bytes 1179656 | tf_op jit(solution)/shard_map/ppermute | solution.py:784
  312.9 298.0 %all-gather.27.cloned.1.call-start = ((), (), s32[]{:S(2)}) async-start(), calls=%async_computation.29 | async-start | bytes 3932160 | tf_op jit(solution)/shard_map/all_gather | solution.py:1468
  330.7 44.2 %collective-permute-start.43 = (bf16[2,64,1536]{2,1,0:T(8,128)(2,1)}, bf16[2,64,1536]{2,1,0:T(8,128)(2,1)}, u32[]{:S(2)}, u32[]{:S(2)}) collective-permute-start(bf16[2,64,1536]{2,1,0:T(8,128)(2,1)} %pad_maximum_fusion.23), channel_id=1, source_target_pairs={{0,16},{16,0},{1,17},{17,1},{2,18},{18,2},{3,19},{19,3},{4,20},{20... | collective-permute-start | bytes 1179656 | tf_op jit(solution)/shard_map/ppermute | solution.py:709
  336.3 100.1 %collective-permute-start.50 = (bf16[2,256,384]{2,1,0:T(8,128)(2,1)}, bf16[2,256,384]{2,1,0:T(8,128)(2,1)S(1)}, u32[]{:S(2)}, u32[]{:S(2)}) collective-permute-start(bf16[2,256,384]{2,1,0:T(8,128)(2,1)} %pad_maximum_fusion.28), channel_id=1, source_target_pairs={{0,9},{1,8},{2,1},{3,0},{4,25},{5,24},{6,17},{7,16},{8,11},{9,10},... | collective-permute-start | bytes 1179656 | tf_op jit(solution)/shard_map/ppermute | solution.py:784
  338.0 284.6 %all-gather.19.cloned.1.call-start = ((), (), s32[]{:S(2)}) async-start(), calls=%async_computation.17 | async-start | bytes 1966080 | tf_op jit(solution)/shard_map/all_gather | solution.py:1472
  346.6 142.2 %collective-permute-start.51 = (bf16[2,256,384]{2,1,0:T(8,128)(2,1)}, bf16[2,256,384]{2,1,0:T(8,128)(2,1)S(1)}, u32[]{:S(2)}, u32[]{:S(2)}) collective-permute-start(bf16[2,256,384]{2,1,0:T(8,128)(2,1)} %pad_maximum_fusion.29), channel_id=1, source_target_pairs={{0,16},{1,17},{2,24},{3,25},{4,0},{5,1},{6,8},{7,9},{8,18},{9,19},... | collective-permute-start | bytes 1179656 | tf_op jit(solution)/shard_map/ppermute | solution.py:784
  374.8 128.6 %collective-permute-start.52 = (bf16[2,256,384]{2,1,0:T(8,128)(2,1)}, bf16[2,256,384]{2,1,0:T(8,128)(2,1)S(1)}, u32[]{:S(2)}, u32[]{:S(2)}) collective-permute-start(bf16[2,256,384]{2,1,0:T(8,128)(2,1)} %pad_maximum_fusion.30), channel_id=1, source_target_pairs={{0,17},{1,16},{2,25},{3,24},{4,1},{5,0},{6,9},{7,8},{8,19},{9,18},... | collective-permute-start | bytes 1179656 | tf_op jit(solution)/shard_map/ppermute | solution.py:784
  401.5 102.0 %collective-permute-start.53 = (bf16[2,256,384]{2,1,0:T(8,128)(2,1)}, bf16[2,256,384]{2,1,0:T(8,128)(2,1)S(1)}, u32[]{:S(2)}, u32[]{:S(2)}) collective-permute-start(bf16[2,256,384]{2,1,0:T(8,128)(2,1)} %pad_maximum_fusion.31), channel_id=1, source_target_pairs={{0,24},{1,25},{2,16},{3,17},{4,8},{5,9},{6,0},{7,1},{8,26},{9,27},... | collective-permute-start | bytes 1179656 | tf_op jit(solution)/shard_map/ppermute | solution.py:784
  401.6 63.3 %collective-permute-start.45 = (bf16[2,64,1536]{2,1,0:T(8,128)(2,1)S(1)}, bf16[2,64,1536]{2,1,0:T(8,128)(2,1)S(1)}, u32[]{:S(2)}, u32[]{:S(2)}) collective-permute-start(bf16[2,64,1536]{2,1,0:T(8,128)(2,1)S(1)} %pad_maximum_fusion.24), channel_id=1, source_target_pairs={{0,16},{16,0},{1,17},{17,1},{2,18},{18,2},{3,19},{19,3},{4,20},{20... | collective-permute-start | bytes 1179656 | tf_op jit(solution)/shard_map/ppermute | solution.py:709
  436.4 67.2 %collective-permute-start.54 = (bf16[2,256,384]{2,1,0:T(8,128)(2,1)S(1)}, bf16[2,256,384]{2,1,0:T(8,128)(2,1)S(1)}, u32[]{:S(2)}, u32[]{:S(2)}) collective-permute-start(bf16[2,256,384]{2,1,0:T(8,128)(2,1)S(1)} %copy-done.77), channel_id=1, source_target_pairs={{0,25},{1,24},{2,17},{3,16},{4,9},{5,8},{6,1},{7,0},{8,27},{9,26},... | collective-permute-start | bytes 1179656 | tf_op jit(solution)/shard_map/ppermute | solution.py:784
  464.9 86.0 %collective-permute-start.78 = (bf16[2,64,1536]{2,1,0:T(8,128)(2,1)}, bf16[2,64,1536]{2,1,0:T(8,128)(2,1)S(1)}, u32[]{:S(2)}, u32[]{:S(2)}) collective-permute-start(bf16[2,64,1536]{2,1,0:T(8,128)(2,1)} %param.25), channel_id=1, source_target_pairs={{0,0},{1,1},{2,8},{3,9},{4,16},{5,17},{6,24},{7,25},{8,2},{9,3},{1... | collective-permute-start | bytes 1179656 | tf_op jit(solution)/shard_map/ppermute | solution.py:705
  527.4 46.8 %collective-permute-start.55 = (bf16[4,64,1536]{2,1,0:T(8,128)(2,1)S(1)}, bf16[4,64,1536]{2,1,0:T(8,128)(2,1)S(1)}, u32[]{:S(2)}, u32[]{:S(2)}) collective-permute-start(bf16[4,64,1536]{2,1,0:T(8,128)(2,1)S(1)} %bitcast.762), channel_id=1, source_target_pairs={{0,8},{8,0},{1,9},{9,1},{2,10},{10,2},{3,11},{11,3},{4,12},{12,4},... | collective-permute-start | bytes 2359304 | tf_op jit(solution)/shard_map/ppermute | solution.py:709
  562.6 258.0 %reduce-scatter.23.cloned.1.call-start = ((), (), s32[]{:S(2)}) async-start(), calls=%async_computation.25 | async-start | bytes 1966080 | tf_op jit(solution)/shard_map/reduce_scatter | solution.py:769
  643.8 381.9 %reduce-scatter.19.cloned.1.call-start = ((), (), s32[]{:S(2)}) async-start(), calls=%async_computation.23 | async-start | bytes 1474560 | tf_op jit(solution)/shard_map/reduce_scatter | solution.py:769
  696.7 331.4 %reduce-scatter.21.cloned.1.call-start = ((), (), s32[]{:S(2)}) async-start(), calls=%async_computation.24 | async-start | bytes 3932160 | tf_op jit(solution)/shard_map/reduce_scatter | solution.py:769
  703.4 36.4 %collective-permute-start.71 = (bf16[2,64,384]{2,1,0:T(8,128)(2,1)}, bf16[2,64,384]{2,1,0:T(8,128)(2,1)}, u32[]{:S(2)}, u32[]{:S(2)}) collective-permute-start(bf16[2,64,384]{2,1,0:T(8,128)(2,1)} %get-tuple-element.362), channel_id=1, source_target_pairs={{0,1},{1,0},{2,9},{3,8},{4,17},{5,16},{6,25},{7,24},{8,3},{9,2},{1... | collective-permute-start | bytes 294920 | tf_op jit(solution)/shard_map/ppermute | solution.py:784
  704.4 37.2 %collective-permute-start.72 = (bf16[2,64,384]{2,1,0:T(8,128)(2,1)}, bf16[2,64,384]{2,1,0:T(8,128)(2,1)}, u32[]{:S(2)}, u32[]{:S(2)}) collective-permute-start(bf16[2,64,384]{2,1,0:T(8,128)(2,1)} %get-tuple-element.361), channel_id=1, source_target_pairs={{0,2},{1,3},{2,10},{3,11},{4,18},{5,19},{6,26},{7,27},{8,0},{9,1},... | collective-permute-start | bytes 294920 | tf_op jit(solution)/shard_map/ppermute | solution.py:784
  738.9 394.1 %reduce-scatter.17.cloned.1.call-start = ((), (), s32[]{:S(2)}) async-start(), calls=%async_computation.22 | async-start | bytes 4423680 | tf_op jit(solution)/shard_map/reduce_scatter | solution.py:769
  789.3 48.8 %collective-permute-start.92 = (bf16[4,64,1536]{2,1,0:T(8,128)(2,1)}, bf16[4,64,1536]{2,1,0:T(8,128)(2,1)S(1)}, u32[]{:S(2)}, u32[]{:S(2)}) collective-permute-start(bf16[4,64,1536]{2,1,0:T(8,128)(2,1)} %bitcast.152), channel_id=1, source_target_pairs={{0,8},{8,0},{1,9},{9,1},{2,10},{10,2},{3,11},{11,3},{4,12},{12,4},... | collective-permute-start | bytes 2359304 | tf_op jit(solution)/shard_map/ppermute | solution.py:709
  830.7 90.7 %collective-permute-start.128 = (bf16[2,256,384]{2,1,0:T(8,128)(2,1)}, bf16[2,256,384]{2,1,0:T(8,128)(2,1)}, u32[]{:S(2)}, u32[]{:S(2)}) collective-permute-start(bf16[2,256,384]{2,1,0:T(8,128)(2,1)} %get-tuple-element.266), channel_id=1, source_target_pairs={{0,1},{1,0},{2,9},{3,8},{4,17},{5,16},{6,25},{7,24},{8,3},{9,2},{1... | collective-permute-start | bytes 1179656 | tf_op jit(solution)/shard_map/ppermute | solution.py:784
  833.7 116.9 %collective-permute-start.129 = (bf16[2,256,384]{2,1,0:T(8,128)(2,1)}, bf16[2,256,384]{2,1,0:T(8,128)(2,1)}, u32[]{:S(2)}, u32[]{:S(2)}) collective-permute-start(bf16[2,256,384]{2,1,0:T(8,128)(2,1)} %get-tuple-element.265), channel_id=1, source_target_pairs={{0,2},{1,3},{2,10},{3,11},{4,18},{5,19},{6,26},{7,27},{8,0},{9,1},... | collective-permute-start | bytes 1179656 | tf_op jit(solution)/shard_map/ppermute | solution.py:784
  833.7 136.7 %collective-permute-start.130 = (bf16[2,256,384]{2,1,0:T(8,128)(2,1)}, bf16[2,256,384]{2,1,0:T(8,128)(2,1)}, u32[]{:S(2)}, u32[]{:S(2)}) collective-permute-start(bf16[2,256,384]{2,1,0:T(8,128)(2,1)} %get-tuple-element.264), channel_id=1, source_target_pairs={{0,3},{1,2},{2,11},{3,10},{4,19},{5,18},{6,27},{7,26},{8,1},{9,0},... | collective-permute-start | bytes 1179656 | tf_op jit(solution)/shard_map/ppermute | solution.py:784
  838.1 302.8 %reduce-scatter.15.cloned.1.call-start = ((), (), s32[]{:S(2)}) async-start(), calls=%async_computation.21 | async-start | bytes 1966080 | tf_op jit(solution)/shard_map/reduce_scatter | solution.py:769
  838.2 152.2 %collective-permute-start.131 = (bf16[2,256,384]{2,1,0:T(8,128)(2,1)}, bf16[2,256,384]{2,1,0:T(8,128)(2,1)S(1)}, u32[]{:S(2)}, u32[]{:S(2)}) collective-permute-start(bf16[2,256,384]{2,1,0:T(8,128)(2,1)} %get-tuple-element.263), channel_id=1, source_target_pairs={{0,4},{1,5},{2,12},{3,13},{4,20},{5,21},{6,28},{7,29},{8,6},{9,7},... | collective-permute-start | bytes 1179656 | tf_op jit(solution)/shard_map/ppermute | solution.py:784
  856.7 63.1 %collective-permute-start.93 = (bf16[2,64,1536]{2,1,0:T(8,128)(2,1)S(1)}, bf16[2,64,1536]{2,1,0:T(8,128)(2,1)S(1)}, u32[]{:S(2)}, u32[]{:S(2)}) collective-permute-start(bf16[2,64,1536]{2,1,0:T(8,128)(2,1)S(1)} %slice.1582), channel_id=1, source_target_pairs={{0,16},{16,0},{1,17},{17,1},{2,18},{18,2},{3,19},{19,3},{4,20},{20... | collective-permute-start | bytes 1179656 | tf_op jit(solution)/shard_map/ppermute | solution.py:709
  950.7 39.8 %collective-permute-start.132 = (bf16[2,256,384]{2,1,0:T(8,128)(2,1)S(1)}, bf16[2,256,384]{2,1,0:T(8,128)(2,1)S(1)}, u32[]{:S(2)}, u32[]{:S(2)}) collective-permute-start(bf16[2,256,384]{2,1,0:T(8,128)(2,1)S(1)} %copy-done.74), channel_id=1, source_target_pairs={{0,5},{1,4},{2,13},{3,12},{4,21},{5,20},{6,29},{7,28},{8,7},{9,6},... | collective-permute-start | bytes 1179656 | tf_op jit(solution)/shard_map/ppermute | solution.py:784
  1032.1 210.8 %reduce-scatter.13.cloned.1.call-start = ((), (), s32[]{:S(2)}) async-start(), calls=%async_computation.20 | async-start | bytes 3932160 | tf_op jit(solution)/shard_map/reduce_scatter | solution.py:769
  1069.7 61.9 %collective-permute-start.144 = (f32[3,1536]{1,0:T(4,128)}, f32[3,1536]{1,0:T(4,128)}, u32[]{:S(2)}, u32[]{:S(2)}) collective-permute-start(f32[3,1536]{1,0:T(4,128)} %add.733), channel_id=1, source_target_pairs={{0,2},{2,4},{4,6},{6,0},{1,3},{3,5},{5,7},{7,1},{8,10},{10,12},{12... | collective-permute-start | bytes 55304 | tf_op jit(solution)/shard_map/ppermute | solution.py:743
  1071.5 60.1 %collective-permute-start.145 = (f32[3,1536]{1,0:T(4,128)}, f32[3,1536]{1,0:T(4,128)}, u32[]{:S(2)}, u32[]{:S(2)}) collective-permute-start(f32[3,1536]{1,0:T(4,128)} %add.733), channel_id=1, source_target_pairs={{0,4},{2,6},{4,0},{6,2},{1,5},{3,7},{5,1},{7,3},{8,12},{10,14},{12... | collective-permute-start | bytes 55304 | tf_op jit(solution)/shard_map/ppermute | solution.py:743
  1071.5 60.1 %collective-permute-start.146 = (f32[3,1536]{1,0:T(4,128)}, f32[3,1536]{1,0:T(4,128)}, u32[]{:S(2)}, u32[]{:S(2)}) collective-permute-start(f32[3,1536]{1,0:T(4,128)} %add.733), channel_id=1, source_target_pairs={{0,6},{2,0},{4,2},{6,4},{1,7},{3,1},{5,3},{7,5},{8,14},{10,8},{12,... | collective-permute-start | bytes 55304 | tf_op jit(solution)/shard_map/ppermute | solution.py:743
  1137.2 109.9 %reduce-scatter.11.cloned.1.call-start = ((), (), s32[]{:S(2)}) async-start(), calls=%async_computation.19 | async-start | bytes 1474560 | tf_op jit(solution)/shard_map/reduce_scatter | solution.py:769
  1168.1 118.3 %reduce-scatter.9.cloned.1.call-start = ((), (), s32[]{:S(2)}) async-start(), calls=%async_computation.18 | async-start | bytes 2949120 | tf_op jit(solution)/shard_map/reduce_scatter | solution.py:769
  1247.2 37.4 %collective-permute-start.151 = (bf16[96,1536]{1,0:T(8,128)(2,1)}, bf16[96,1536]{1,0:T(8,128)(2,1)}, u32[]{:S(2)}, u32[]{:S(2)}) collective-permute-start(bf16[96,1536]{1,0:T(8,128)(2,1)} %bitcast.790), channel_id=1, source_target_pairs={{0,0},{2,1},{4,2},{6,3},{1,4},{3,5},{5,6},{7,7},{8,8},{10,9},{12,1... | collective-permute-start | bytes 884744 | tf_op jit(solution)/shard_map/ppermute | solution.py:838
  1261.1 43.6 %collective-permute-start.125 = (f32[2,64,1536]{2,1,0:T(8,128)}, f32[2,64,1536]{2,1,0:T(8,128)}, u32[]{:S(2)}, u32[]{:S(2)}) collective-permute-start(f32[2,64,1536]{2,1,0:T(8,128)} %fusion.16), channel_id=1, source_target_pairs={{0,0},{1,1},{2,8},{3,9},{4,16},{5,17},{6,24},{7,25},{8,2},{9,3},{1... | collective-permute-start | bytes 2359304 | tf_op jit(solution)/shard_map/ppermute | solution.py:705
  (284 other events, 3576.2 us)
Sparse Core Ops, SparseCore 0:
  97.8 49.0 all-gather.20
  164.3 29.3 all-gather.12
  195.9 62.6 all-gather.22
  260.0 35.7 all-gather.14
  297.8 155.3 all-gather.24
  455.2 54.3 all-gather.16
  511.7 70.9 all-gather.26
  584.3 35.4 all-gather.18
  643.9 35.1 reduce-scatter.22
  696.9 39.4 reduce-scatter.18
  739.0 75.9 reduce-scatter.20
  838.2 115.6 reduce-scatter.16
  1019.5 34.1 reduce-scatter.14
  1055.8 60.8 reduce-scatter.12
  1168.3 30.0 reduce-scatter.10
  1202.8 51.3 reduce-scatter.8

commit v2 on v1

--- a/solution.py
+++ b/solution.py
@@ -684,50 +684,59 @@
     )
 
 
-EVERY = ("y", "c", "z", "x")
-PLANE = ("y", "c", "x")
+EVERY = ("u", "c", "y", "x", "v")
+PLANE = ("y", "x", "c")
+SQUARES = ("u", "v")
 BF = jnp.bfloat16
 F32 = jnp.float32
 
 
 def params(**more):
-    return pltpu.CompilerParams(vmem_limit_bytes=60 * 2**20, **more)
+    return pltpu.CompilerParams(vmem_limit_bytes=32 * 2**20, **more)
+
+
+def bit_route(move):
+    route = []
+    for place in range(2 ** len(EVERY)):
+        bits = [place >> (len(EVERY) - 1 - k) & 1 for k in range(len(EVERY))]
+        goal = 0
+        for bit in move(*bits):
+            goal = 2 * goal + bit
+        if goal != place:
+            route.append((place, goal))
+    return route
 
 
 def swap_planes(block):
-    planes = lax.axis_size("z")
-    inner = lax.axis_size("x")
-    route = []
-    for d in range(planes):
-        for z in range(planes):
-            for x in range(inner):
-                route.append(((d * planes + z) * inner + x, (z * planes + d) * inner + x))
-    return lax.ppermute(block, EVERY, route)
+    away = lax.axis_index("c") != lax.axis_index("v")
+    route = bit_route(lambda u, c, y, x, v: (u, v, y, x, c))
+    return jnp.where(away, lax.ppermute(block, EVERY, route), block)
 
 
 def other(block, axis):
     return lax.ppermute(block, axis, [(0, 1), (1, 0)])
 
 
+def gather_line(block):
+    from_y = other(block, "y")
+    return jnp.stack([block, other(block, "x"), from_y, other(from_y, "x")])
+
+
 def gather_plane(block):
-    from_y = other(block, "y")
-    from_x = other(block, "x")
-    corner = jnp.concatenate([other(from_y[:1], "x"), other(from_x[1:], "y")], axis=0)
-    own = jnp.stack([block, from_x, from_y, corner])
+    own = gather_line(block)
     return jnp.concatenate([own, other(own, "c")], axis=0)
 
 
+def scatter_line(mine, kind):
+    to_y = (mine[2] + other(mine[3].astype(kind), "x").astype(F32)).astype(kind)
+    from_x = other(mine[1].astype(kind), "x").astype(F32)
+    return mine[0] + from_x + other(to_y, "y").astype(F32)
+
+
 def scatter_plane(parts):
-    kind = parts.dtype
     half = parts.shape[0] // 2
     mine = parts[:half].astype(F32) + other(parts[half:], "c").astype(F32)
-    sent = mine[1:].astype(kind)
-    to_x, to_y, corner = sent[0], sent[1], sent[2]
-    via_y = other(corner[:1], "y").astype(F32)
-    via_x = other(corner[1:], "x").astype(F32)
-    to_x = jnp.concatenate([(mine[1][:1] + via_y).astype(kind), to_x[1:]], axis=0)
-    to_y = jnp.concatenate([to_y[:1], (mine[2][1:] + via_x).astype(kind)], axis=0)
-    return mine[0] + other(to_x, "x").astype(F32) + other(to_y, "y").astype(F32)
+    return scatter_line(mine, parts.dtype)
 
 
 def sum_plane(parts):
@@ -738,104 +747,87 @@
     return lax.all_to_all(block, axes, 0, 0, tiled=True)
 
 
-def turned(block, distance):
-    planes = lax.axis_size("z")
-    return lax.ppermute(block, "z", [(z, (z + distance) % planes) for z in range(planes)])
-
-
-def gather_z(block):
-    planes = lax.axis_size("z")
-    ring = [block] + [turned(block, planes - k) for k in range(1, planes)]
-    ring = jnp.stack(ring + ring[:-1])
-    first = (planes - lax.axis_index("z")) % planes
-    return lax.dynamic_slice_in_dim(ring, first, planes, 0)
-
-
-def gather_small(block):
-    for axis in ("x", "c", "y"):
-        pair = (block, other(block, axis))
-        here = lax.axis_index(axis) == 0
-        block = jnp.stack([jnp.where(here, pair[0], pair[1]), jnp.where(here, pair[1], pair[0])])
-    return gather_z(block)
+def gather_small(block, axes):
+    for axis in reversed(axes):
+        block = in_order(block, other(block, axis), axis)
+    return block
 
 
 def total_small(block):
-    for axis in ("x", "y", "c"):
+    for axis in EVERY:
         block = block + other(block, axis)
-    return block + sum(turned(block, k) for k in range(1, lax.axis_size("z")))
-
-
-def reduce_z(parts):
-    return lax.psum_scatter(parts, "z", scatter_dimension=0)
-
-
-def deal(pieces, back):
-    planes, inner = lax.axis_size("z"), lax.axis_size("x")
-    result = []
-    for k, piece in enumerate(pieces):
-        turn, flip = k // inner, k % inner
-        route = []
-        for d in range(planes):
-            for z in range(planes):
-                for x in range(inner):
-                    goal = (z, d ^ turn, x ^ flip) if back else (z ^ turn, d, x ^ flip)
-                    place = (d * planes + z) * inner + x
-                    route.append((place, (goal[0] * planes + goal[1]) * inner + goal[2]))
-        result.append(lax.ppermute(piece, EVERY, route))
-    return result
+    return block
+
+
+def pair_sum(parts, axis):
+    here = lax.axis_index(axis)
+    theirs = other(lax.dynamic_index_in_dim(parts, 1 - here, 0, False), axis)
+    mine = lax.dynamic_index_in_dim(parts, here, 0, False)
+    return mine.astype(F32) + theirs.astype(F32)
+
+
+def reduce_squares(parts):
+    return lax.psum_scatter(parts, SQUARES, scatter_dimension=0)
+
+
+def gather_squares(block):
+    return lax.all_gather(block, SQUARES, axis=0)
+
+
+def settle(stage, *pieces):
+    return lax.optimization_barrier((stage,) + pieces)
+
+
+def tie(value, *stages):
+    return lax.optimization_barrier((value,) + stages)[0]
+
+
+def in_order(mine, theirs, axis):
+    first = lax.axis_index(axis) == 0
+    return jnp.stack([jnp.where(first, mine, theirs), jnp.where(first, theirs, mine)])
+
+
+def kv_owners(parts):
+    for axis in PLANE:
+        lead = parts.ndim - {"y": 6, "x": 5, "c": 4}[axis]
+        stay = lax.index_in_dim(parts, 0, lead, False)
+        leave = lax.index_in_dim(parts, 1, lead, False)
+        parts = in_order(stay, other(leave, axis), axis)
+    side, y_size, c_size, two, count, width = parts.shape
+    return parts.transpose(0, 4, 3, 2, 1, 5).reshape(side, count, two * y_size * c_size * width)
 
 
 def rows_gather(block):
-    x = lax.axis_index("x")
-    mine = lax.dynamic_index_in_dim(block, x, 0, False)
-    theirs = lax.dynamic_index_in_dim(block, 1 - x, 0, False)
-    pair = jnp.stack([mine, other(theirs, "x")])
-    four = jnp.concatenate([pair, other(pair, "y")], axis=0)
-    return jnp.concatenate([four, other(four, "c")], axis=0)
+    here = lax.axis_index("c")
+    mine = lax.dynamic_index_in_dim(block, here, 0, False)
+    theirs = lax.dynamic_index_in_dim(block, 1 - here, 0, False)
+    return gather_line(jnp.stack([mine, other(theirs, "c")]))
 
 
 def rows_scatter(parts):
-    kind = parts.dtype
-    for axis in ("c", "y"):
-        half = parts.shape[0] // 2
-        parts = (
-            parts[:half].astype(F32) + other(parts[half:].astype(kind), axis).astype(F32)
-        )
-    mine, theirs = parts[0], other(parts[1].astype(kind), "x").astype(F32)
-    first = lax.axis_index("x") == 0
-    return jnp.stack([jnp.where(first, mine, theirs), jnp.where(first, theirs, mine)])
+    parts = parts.reshape((4, 2) + parts.shape[1:])
+    pair = scatter_line(parts.astype(F32), parts.dtype)
+    return in_order(pair[0], other(pair[1].astype(parts.dtype), "c").astype(F32), "c")
 
 
 def rows_of(gathered):
-    planes, members, rows, width = gathered.shape
-    inner = lax.axis_size("x")
-    split = gathered.reshape(planes, members // inner, inner, rows, width)
-    return split.transpose(1, 0, 2, 3, 4).reshape(planes * members * rows, width)
-
-
-def by_plane(grad):
-    planes, inner = lax.axis_size("z"), lax.axis_size("x")
+    squares, members, rows, width = gathered.shape
+    split = gathered.reshape(2, 2, members // 2, 2, rows, width)
+    return split.transpose(0, 3, 2, 1, 4, 5).reshape(squares * members * rows, width)
+
+
+def by_square(grad):
     total, width = grad.shape
-    rows = total // (planes * planes * inner)
-    split = grad.reshape(planes, planes, inner, rows, width).transpose(1, 0, 2, 3, 4)
-    return split.reshape(planes, planes * inner, rows, width)
-
-
-def columns_in(payload):
-    return rows_of(lax.all_gather(trade(payload, PLANE), "z", axis=0))
-
-
-def columns_out(grad):
-    return trade(reduce_z(by_plane(grad.astype(BF))), PLANE)
+    split = grad.reshape(2, 2, 4, 2, total // 32, width).transpose(0, 3, 2, 1, 4, 5)
+    return split.reshape(4, 8, total // 32, width)
 
 
 def relocate(block, back):
-    planes, inner = lax.axis_size("z"), lax.axis_size("x")
-    route = []
-    for place in range(planes * inner):
-        goal = (place % planes) * inner + place // planes
-        route.append((goal, place) if back else (place, goal))
-    return lax.ppermute(block, ("z", "x"), route)
+    route = bit_route(lambda u, c, y, x, v: (x, y, u, c, v))
+    moving = jnp.zeros((2 ** len(EVERY),), bool).at[jnp.array([place for place, goal in route])].set(True)
+    here = lax.axis_index(EVERY)
+    moved = lax.ppermute(block, EVERY, [(goal, place) for place, goal in route] if back else route)
+    return jnp.where(moving[here], moved, block)
 
 
 def dot(left, right, left_dim, right_dim):
@@ -868,8 +860,7 @@
 
 
 def conv_forward(order, projected, taps, bias):
-    blocks, rows, group, both = projected.shape
-    width = both // 2
+    blocks, rows, group, width = projected.shape
     spec = pl.BlockSpec((1, rows, group, width), lambda i, order: (order[i], 0, 0, 0))
     shape = (blocks, rows, group, width)
     return pl.pallas_call(
@@ -1077,11 +1068,11 @@
                 past = past_ref[0, row, base + k]
                 fade = jnp.exp(now * decay)
                 back = widen(c_ref[0, row, base + k], width) * grad + backs[row]
-                dc_ref[0, row, base + k] = narrow(states[row] * grad)
+                dc_ref[0, row, base + k] = narrow(states[row] * grad).astype(BF)
                 firsts[row][k] = jnp.sum(
                     widen(b_ref[0, row, base + k], width) * back, axis=0, keepdims=True
                 )
-                db_ref[0, row, base + k] = narrow(back * drives[row][k : k + 1])
+                db_ref[0, row, base + k] = narrow(back * drives[row][k : k + 1]).astype(BF)
                 faded = fade * back
                 flow = faded * past
                 seconds[row][k] = jnp.sum(flow * decay, axis=0, keepdims=True)
@@ -1140,8 +1131,8 @@
         out_shape=[
             jax.ShapeDtypeStruct(mixed.shape, F32),
             jax.ShapeDtypeStruct(mixed.shape, F32),
-            jax.ShapeDtypeStruct((blocks, rows, group, states, 128), F32),
-            jax.ShapeDtypeStruct((blocks, rows, group, states, 128), F32),
+            jax.ShapeDtypeStruct((blocks, rows, group, states, 128), BF),
+            jax.ShapeDtypeStruct((blocks, rows, group, states, 128), BF),
             jax.ShapeDtypeStruct(decay.shape, F32),
             jax.ShapeDtypeStruct(end.shape, F32),
         ],
@@ -1153,7 +1144,7 @@
 def own_positions(shape, axis, first, member, group):
     index = first + lax.broadcasted_iota(jnp.int32, shape, axis)
     slot = index // group
-    block = (((slot & 2) << 1) | ((slot & 4) >> 1) | (slot & 1)) ^ member
+    block = slot ^ member
     return block * group + index % group
 
 
@@ -1172,15 +1163,15 @@
     scale = HEAD_DIM ** (-0.5)
     queries = q_ref[...]
     pieces = ck_ref.shape[0]
-    size = ck_ref.shape[2]
+    size = ck_ref.shape[1]
     tokens = k_ref.shape[0]
     member = meta_ref[1]
     group = tokens // pieces
     query = own_positions((count, 1), 0, first, member, group)
     scores = []
     for piece in range(pieces):
-        score = dot(queries, ck_ref[piece, 0], 1, 1) * scale
-        inside = seen_cache(query, member ^ piece, (1, size), size)
+        score = dot(queries, ck_ref[piece], 1, 1) * scale
+        inside = seen_cache(query, piece, (1, size), size)
         scores.append(jnp.where(inside, score, NEGATIVE))
     score = dot(queries, k_ref[...], 1, 1) * scale
     key = own_positions((1, tokens), 1, 0, member, group)
@@ -1193,29 +1184,27 @@
     for piece, score in enumerate(scores):
         part = jnp.exp(score - top)
         total = total + jnp.sum(part, axis=1, keepdims=True)
-        contents = cv_ref[piece, 0] if piece < pieces else v_ref[...]
+        contents = cv_ref[piece] if piece < pieces else v_ref[...]
         result = result + dot(part.astype(BF), contents, 1, 0)
     out_ref[...] = result / total
     log_ref[0] = jnp.broadcast_to(top + jnp.log(total), (count, 128))
 
 
-def attend(meta, qkv, cache):
+def attend(meta, qkv, cached_keys, cached_contents):
     tokens, width = qkv.shape
     width = width // 3
     heads = width // HEAD_DIM
     count = 256
-    shards, two, group, unused = cache.shape
+    shards, group, unused = cached_keys.shape
     own = lambda base: pl.BlockSpec((tokens, HEAD_DIM), lambda h, i, meta: (0, base + h))
-    held = lambda which: pl.BlockSpec(
-        (shards, 1, group, HEAD_DIM), lambda h, i, meta: (0, which, 0, h)
-    )
+    held = pl.BlockSpec((shards, group, HEAD_DIM), lambda h, i, meta: (0, 0, h))
     block = pl.BlockSpec((count, HEAD_DIM), lambda h, i, meta: (i, h))
     return pl.pallas_call(
         attend_body,
         grid_spec=pltpu.PrefetchScalarGridSpec(
             num_scalar_prefetch=1,
             grid=(heads, tokens // count),
-            in_specs=[block, held(0), held(1), own(heads), own(2 * heads)],
+            in_specs=[block, held, held, own(heads), own(2 * heads)],
             out_specs=[block, pl.BlockSpec((1, count, 128), lambda h, i, meta: (h, i, 0))],
         ),
         out_shape=[
@@ -1224,7 +1213,7 @@
         ],
         compiler_params=params(),
         name="attend",
-    )(meta, qkv, cache, cache, qkv, qkv)
+    )(meta, qkv, cached_keys, cached_contents, qkv, qkv)
 
 
 def attend_back_body(
@@ -1237,7 +1226,8 @@
     cv_ref,
     k_ref,
     v_ref,
-    dcache_ref,
+    dck_ref,
+    dcv_ref,
     dq_ref,
     dk_ref,
     dv_ref,
@@ -1250,7 +1240,7 @@
     queries = q_ref[...]
     grad = grad_ref[...]
     count = queries.shape[0]
-    size = ck_ref.shape[2]
+    size = ck_ref.shape[1]
     member = meta_ref[1]
     group = count // (2 * pieces)
     query = own_positions((count, 1), 0, 0, member, group)
@@ -1263,20 +1253,31 @@
 
     def work(keys, contents, inside):
         score = dot(queries, keys, 1, 1) * scale
-        part = jnp.where(inside, jnp.exp(score - log_ref[0][:, :1]), 0.0)
+        part = jnp.exp(score - log_ref[0][:, :1])
+        if inside is not None:
+            part = jnp.where(inside, part, 0.0)
         dcontents = dot(part.astype(BF), grad, 0, 0)
         slope = dot(grad, contents, 1, 1)
         dscore = (part * (slope - delta[:, :1])).astype(BF)
         total[...] += dot(dscore, keys, 1, 0) * scale
         return dot(dscore, queries, 0, 0) * scale, dcontents
 
-    @pl.when(piece < pieces)
-    def cached():
-        for half in range(2):
-            inside = seen_cache(query, member ^ (2 * piece + half), (1, size), size)
-            dkeys, dcontents = work(ck_ref[half, 0], cv_ref[half, 0], inside)
-            dcache_ref[half, 0] = dkeys.astype(BF)
-            dcache_ref[half, 1] = dcontents.astype(BF)
+    def cached(inside):
+        keys = ck_ref[...].reshape(2 * size, HEAD_DIM)
+        contents = cv_ref[...].reshape(2 * size, HEAD_DIM)
+        dkeys, dcontents = work(keys, contents, inside)
+        dck_ref[...] = dkeys.astype(BF).reshape(2, size, HEAD_DIM)
+        dcv_ref[...] = dcontents.astype(BF).reshape(2, size, HEAD_DIM)
+
+    edge = piece * 2 * size < count
+
+    @pl.when((piece < pieces) & edge)
+    def near():
+        cached(seen_cache(query, 2 * piece, (1, 2 * size), size))
+
+    @pl.when((piece < pieces) & jnp.logical_not(edge))
+    def far():
+        cached(None)
 
     @pl.when(piece == pieces)
     def own():
@@ -1287,16 +1288,14 @@
         dq_ref[...] = total[...].astype(BF)
 
 
-def attend_back(meta, qkv, grad, out, log, cache):
+def attend_back(meta, qkv, grad, out, log, cached_keys, cached_contents):
     tokens, width = grad.shape
     heads = width // HEAD_DIM
-    shards, two, group, unused = cache.shape
+    shards, group, unused = cached_keys.shape
     pieces = shards // 2
     own = lambda base: pl.BlockSpec((tokens, HEAD_DIM), lambda h, i, meta: (0, base + h))
     place = lambda i: jnp.minimum(i, pieces - 1)
-    held = lambda which: pl.BlockSpec(
-        (2, 1, group, HEAD_DIM), lambda h, i, meta: (place(i), which, 0, h)
-    )
+    held = pl.BlockSpec((2, group, HEAD_DIM), lambda h, i, meta: (place(i), 0, h))
     result = jax.ShapeDtypeStruct((tokens, width), BF)
     return pl.pallas_call(
         attend_back_body,
@@ -1308,13 +1307,14 @@
                 own(0),
                 own(0),
                 pl.BlockSpec((1, tokens, 128), lambda h, i, meta: (h, 0, 0)),
-                held(0),
-                held(1),
+                held,
+                held,
                 own(heads),
                 own(2 * heads),
             ],
             out_specs=[
-                pl.BlockSpec((2, 2, group, HEAD_DIM), lambda h, i, meta: (place(i), 0, 0, h)),
+                held,
+                held,
                 own(0),
                 own(0),
                 own(0),
@@ -1324,10 +1324,25 @@
                 pltpu.VMEM((tokens, 128), F32),
             ],
         ),
-        out_shape=[jax.ShapeDtypeStruct(cache.shape, BF), result, result, result],
+        out_shape=[jax.ShapeDtypeStruct(cached_keys.shape, BF)] * 2 + [result, result, result],
         compiler_params=params(),
         name="attend_back",
-    )(meta, qkv, grad, out, log, cache, cache, qkv, qkv)
+    )(meta, qkv, grad, out, log, cached_keys, cached_contents, qkv, qkv)
+
+
+def assemble(gots, moves, shape):
+    def body(*refs):
+        out_ref = refs[-1]
+        for (row, column), height, (which, member, left, width) in moves:
+            part = refs[which][member, :, left : left + width].astype(F32)
+            out_ref[row : row + height, column : column + width] = part
+
+    return pl.pallas_call(
+        body,
+        out_shape=jax.ShapeDtypeStruct(shape, F32),
+        compiler_params=params(),
+        name="assemble",
+    )(*gots)
 
 
 def silu_slope(values):
@@ -1340,31 +1355,18 @@
     return back
 
 
-def plane_forward_ffn(stream, gain, gate_up, down):
-    rows, group, wide = stream.shape
-    normed = gather_plane(rms_gain(stream, gain).astype(BF)).reshape(-1, wide)
+def ffn_gate(normed, gate_up):
     both = dot(normed, gate_up, 1, 0)
-    hidden_width = down.shape[0]
-    hidden = (jax.nn.silu(both[:, :hidden_width]) * both[:, hidden_width:]).astype(BF)
-    parts = dot(hidden, down, 1, 0).astype(BF).reshape(-1, rows, group, wide)
-    return stream + scatter_plane(parts), (normed, both, hidden)
-
-
-def plane_backward_ffn(stream, grad, grad_whole, gain, gate_up, down, kept):
-    normed, both, hidden = kept
-    rows, group, wide = stream.shape
-    hidden_width = down.shape[0]
-    grad_hidden = dot(grad_whole, down, 1, 1)
-    gate, up = both[:, :hidden_width], both[:, hidden_width:]
-    grad_both = jnp.concatenate(
+    width = both.shape[1] // 2
+    return both, (jax.nn.silu(both[:, :width]) * both[:, width:]).astype(BF)
+
+
+def ffn_gate_back(grad_hidden, both):
+    width = both.shape[1] // 2
+    gate, up = both[:, :width], both[:, width:]
+    return jnp.concatenate(
         [grad_hidden * up * silu_slope(gate), grad_hidden * jax.nn.silu(gate)], axis=1
     ).astype(BF)
-    parts = dot(grad_both, gate_up, 1, 1).astype(BF).reshape(-1, rows, group, wide)
-    grad_normed = scatter_plane(parts)
-    grad_stream, grad_gain = norm_back(stream, gain, grad_normed)
-    grad_down = dot(hidden, grad_whole, 0, 0)
-    grad_gate_up = dot(normed, grad_both, 0, 0)
-    return grad + grad_stream, grad_gain, grad_gate_up, grad_down
 
 
 def plane_local(
@@ -1394,25 +1396,41 @@
     second_down,
 ):
     rows, group, wide = activations.shape
-    planes, inner = lax.axis_size("z"), lax.axis_size("x")
+    planes, inner = lax.axis_size(SQUARES), lax.axis_size("c")
     members = planes * inner
-    y, c, z, x = (lax.axis_index(name) for name in EVERY)
-    member = (y * 2 + c) * inner + x
-    place = z * inner + x
-    slots = jnp.arange(members) ^ member
-    order = (((slots & 2) << 1) | ((slots & 4) >> 1) | (slots & 1)).astype(jnp.int32)
-    tokens = swap_planes(activations)
-    stream = tokens.astype(F32)
-    lengths = swap_planes(row_lengths)
-
+    u, c, y, x, v = (lax.axis_index(name) for name in EVERY)
+    member = (y * 2 + x) * inner + c
+    place = (y * 2 + x) * inner + v
+    offset = jnp.arange(members) ^ member
+    order = (((offset & 1) << 2) | (offset >> 1)).astype(jnp.int32)
     shard = mamba_gain.shape[0]
-    gains = jnp.stack([mamba_gain, first_gain, attention_gain, second_gain])
-    gains = gather_small(gains).reshape(planes, planes, inner, 4, shard).transpose(3, 1, 0, 2, 4)
-    gains = gains.reshape(4, wide).astype(F32)
     channels = skip_gain.shape[0]
     width = channels * planes
     rank = step_proj.shape[0]
     states = decay_log.shape[0]
+    units = first_down.shape[0]
+    head_width = wide // planes
+    cache_rows = carried_kv.shape[1]
+
+    def parts_of(product_of):
+        return product_of.astype(BF).reshape(members, rows, group, wide)
+
+    gains = jnp.stack([mamba_gain, first_gain, attention_gain, second_gain], axis=1)
+    gains = jnp.pad(gains, ((0, 0), (0, 124)))
+    payload = mamba_in.reshape(shard, 2, members, width).transpose(2, 0, 1, 3)
+    spread = jnp.broadcast_to(gains[None], (members,) + gains.shape)
+    payload = payload.reshape(members, shard, 2 * width)
+    payload = jnp.concatenate([payload[:, :, :width], spread, payload[:, :, width:]], axis=2)
+    dealt = trade(payload, PLANE)
+    tokens = swap_planes(tie(activations, payload))
+    stream = tokens.astype(F32)
+    own_inner = rows_of(gather_squares(dealt[:, :, : width + 128]))
+    gains = own_inner[:, width : width + 4].T.astype(F32)
+    own_inner = own_inner[:, :width]
+    normed = gather_plane(tokens).reshape(-1, wide).astype(F32)
+    normed = rms_gain(normed, gains[0]).astype(BF)
+
+
     cuts = (selection.shape[1], rank, CONV, 1, 1, states, 1)
     packed = jnp.concatenate(
         [
@@ -1427,7 +1445,7 @@
         axis=1,
     )
     packed = jnp.pad(packed, ((0, 0), (0, -packed.shape[1] % 128)))
-    packed = gather_z(relocate(packed, False)).reshape(width, -1)
+    packed = gather_small(relocate(tie(packed, tokens), False), SQUARES).reshape(width, -1)
     starts = [sum(cuts[:index]) for index in range(len(cuts) + 1)]
     pieces = [packed[:, starts[index] : starts[index + 1]] for index in range(len(cuts))]
     own_selection = pieces[0].astype(BF)
@@ -1437,186 +1455,220 @@
     own_step_bias = pieces[4].T
     decay = -jnp.exp(pieces[5].T)
     skip = pieces[6].T
-    own_in = columns_in(
-        mamba_in.reshape(shard, 2, members, width).transpose(2, 0, 1, 3).reshape(members, shard, -1)
-    )
-    own_out = lax.all_gather(relocate(mamba_out, False), "z", axis=0, tiled=True)
-
-    def hidden_columns(gate_up, units):
-        split = gate_up.reshape(shard, 2, planes, planes, inner, units)
-        return split.transpose(2, 4, 0, 1, 3, 5).reshape(members, shard, -1)
-
-    units = first_down.shape[0]
-    head_width = wide // planes
+    moved = jnp.concatenate([mamba_out, attention_out], axis=0)
+    moved = relocate(tie(moved, packed), False)
+    own_out = gather_squares(moved[:channels]).reshape(width, wide)
+    start = lax.dynamic_slice_in_dim(carried_state, place * width, width, 2)
+    marks = jnp.broadcast_to(row_lengths.astype(F32)[:, None, None], (rows, 8, width))
+    start = swap_planes(tie(jnp.concatenate([start, marks], axis=1), packed))
+    lengths = start[:, states, 0].astype(jnp.int32)
+    start = start[:, :states]
+    own_gate = rows_of(gather_squares(tie(dealt[:, :, width + 128 :], normed)))
+
+    def hidden_columns(gate_up):
+        split = gate_up.reshape(shard, 2, 2, 2, 2, 2, 2, units)
+        return split.transpose(4, 5, 3, 0, 1, 2, 6, 7).reshape(members, shard, -1)
+
     split = attention_qkv.reshape(shard, 3, planes, head_width).transpose(2, 0, 1, 3)
     split = jnp.broadcast_to(
         split.reshape(planes, 1, shard, 3 * head_width), (planes, inner, shard, 3 * head_width)
     )
-    dealt = trade(
-        jnp.concatenate(
+    split = split.reshape(members, shard, 3 * head_width)
+    dealt_first = trade(tie(hidden_columns(first_gate_up), normed), PLANE)
+    own_first_down = gather_squares(first_down).reshape(-1, wide)
+
+    def heads_of(block):
+        return jnp.stack(
             [
-                hidden_columns(first_gate_up, units),
-                split.reshape(members, shard, 3 * head_width),
-                hidden_columns(second_gate_up, units),
-            ],
-            axis=2,
-        ),
-        PLANE,
-    )
-    edges = (0, 2 * planes * units, 2 * planes * units + 3 * head_width, dealt.shape[2])
-    own_first, own_qkv, own_second = (
-        rows_of(lax.all_gather(dealt[:, :, edges[k] : edges[k + 1]], "z", axis=0)) for k in range(3)
-    )
-    own_first_down = lax.all_gather(first_down, "z", axis=0, tiled=True)
-    own_attention_out = lax.all_gather(attention_out, ("z", "x"), axis=0, tiled=True)
-    own_second_down = lax.all_gather(second_down, "z", axis=0, tiled=True)
-    cache_rows = carried_kv.shape[1]
-    chunks = []
-    for k in range(members):
-        group_of, row_of = z ^ (k // inner), x ^ (k % inner)
-        row = lax.dynamic_index_in_dim(carried_kv, row_of, 0, False)
-        chunks.append(
-            jnp.stack(
-                [
-                    lax.dynamic_slice_in_dim(row, which * wide + group_of * head_width, head_width, 1)
-                    for which in range(2)
-                ]
-            )
+                block[r, :, g * head_width : (g + 1) * head_width]
+                for g in range(planes)
+                for r in range(rows)
+            ]
         )
-    cache = jnp.stack(deal(chunks, False))
-    start = swap_planes(lax.dynamic_slice_in_dim(carried_state, place * width, width, 2))
-    grad = swap_planes(cotangent)
-    grad_whole = gather_plane(grad).reshape(-1, wide)
-    grad = grad.astype(F32)
-
-    normed = gather_plane(tokens).reshape(-1, wide).astype(F32)
-    normed = rms_gain(normed, gains[0]).astype(BF)
-    projected = dot(normed, own_in, 1, 0).reshape(members, rows, group, 2 * width)
-    gate = projected[..., width:]
-    total, mixed, mixed_low = conv_forward(order, projected, taps, tap_bias)
+
+    late_keys = swap_planes(tie(carried_kv[:, :, :wide], tokens))
+    cached_keys = trade(tie(heads_of(late_keys), normed), PLANE)
+    late = jnp.concatenate([carried_kv[:, :, wide:], cotangent.reshape(rows, -1, wide)], axis=1)
+    late = swap_planes(tie(late, normed))
+
+    inner_part = dot(normed, own_inner, 1, 0).reshape(members, rows, group, width)
+    total, mixed, mixed_low = conv_forward(order, inner_part, taps, tap_bias)
     flat_low = mixed_low.reshape(-1, width)
     select = sum_plane(dot(flat_low, own_selection, 1, 0).reshape(members, rows, group, -1))
+    gate = dot(normed, own_gate, 1, 0).reshape(members, rows, group, width)
+    select, dealt_first, cached_keys, late = settle(select, dealt_first, cached_keys, late)
     step_low = select[..., :rank].astype(BF).reshape(-1, rank)
     pre = dot(step_low, own_step_proj, 1, 1).reshape(members, rows, group, width) + own_step_bias
     blocks = jnp.zeros((members,), jnp.int32).at[order].set(jnp.arange(members, dtype=jnp.int32))
     positions = blocks[:, None] * group + jnp.arange(group)[None, :]
     valid = (positions[:, None, :] < lengths[None, :, None]).astype(F32)[..., None]
     step = jax.nn.softplus(pre) * valid
+    cached_contents = trade(tie(heads_of(late[:, :cache_rows]), step), PLANE)
     wide_shape = (members, rows, group, states, 128)
     wide_b = jnp.broadcast_to(select[..., rank : rank + states, None], wide_shape)
     wide_c = jnp.broadcast_to(select[..., rank + states :, None], wide_shape)
     core, past, end = scan_forward(order, mixed, step, wide_b, wide_c, decay, start)
+    core, cached_contents = settle(core, cached_contents)
+    own_first = rows_of(gather_squares(dealt_first))
+    dealt_qkv = trade(tie(split, core), PLANE)
+    rear = gather_squares(jnp.concatenate([moved[channels:], second_down], axis=0))
     mixed_out = core + skip * mixed
     gated = (mixed_out * jax.nn.silu(gate)).astype(BF).reshape(-1, width)
-    parts = dot(gated, own_out, 1, 0).astype(BF).reshape(members, rows, group, wide)
-    first_stream = stream + scatter_plane(parts)
-    new_state = swap_planes(end)
-
-    second_stream, first_kept = plane_forward_ffn(first_stream, gains[1], own_first, own_first_down)
-
-    def kv_back(pieces, kind):
-        count = pieces[0].shape[1]
-        whole = jnp.zeros((rows, count, 2 * wide), kind)
-        for k, piece in enumerate(deal(pieces, True)):
-            group_of, row_of = z ^ (k // inner), x ^ (k % inner)
-            for which in range(2):
-                whole = lax.dynamic_update_slice(
-                    whole,
-                    piece[which : which + 1].astype(kind),
-                    (row_of, 0, which * wide + group_of * head_width),
-                )
-        return whole
-
-    length = jnp.concatenate([lax.dynamic_slice_in_dim(lengths, x, 1), member[None]])
+    first_stream = stream + scatter_plane(parts_of(dot(gated, own_out, 1, 0)))
+    first_stream, dealt_qkv = settle(first_stream, dealt_qkv)
+    own_qkv = rows_of(gather_squares(dealt_qkv))
+
+    first_normed = gather_plane(rms_gain(first_stream, gains[1]).astype(BF)).reshape(-1, wide)
+    dealt_second = trade(tie(hidden_columns(second_gate_up), first_normed), PLANE)
+    first_both, first_hidden = ffn_gate(first_normed, own_first)
+    second_stream = first_stream + scatter_plane(parts_of(dot(first_hidden, own_first_down, 1, 0)))
+
+    second_stream, dealt_second = settle(second_stream, dealt_second)
+    own_second = rows_of(gather_squares(dealt_second))
+
+    def rows_parts(product_of):
+        return product_of.astype(BF).reshape(members, group, wide)
+
+    grad = late[:, cache_rows:].reshape(rows, group, wide)
+    own_attention_out = rear[:, :shard]
+    own_attention_out = in_order(own_attention_out, other(own_attention_out, "c"), "c")
+    own_attention_out = own_attention_out.reshape(-1, wide)
+    own_second_down = rear[:, shard:].reshape(-1, wide)
+    length = jnp.concatenate([lax.dynamic_slice_in_dim(lengths, c, 1), member[None]])
     normed_rows = rows_gather(rms_gain(second_stream, gains[2]).astype(BF)).reshape(-1, wide)
     qkv = dot(normed_rows, own_qkv, 1, 0).astype(BF)
-    attended, log = attend(length, qkv, cache)
+    grad_whole = gather_plane(tie(grad, qkv)).reshape(-1, wide)
+    grad = grad.astype(F32)
+    attended, log = attend(length, qkv, cached_keys, cached_contents)
     attended_low = attended.astype(BF)
-    parts = dot(attended_low, own_attention_out, 1, 0).astype(BF)
-    third_stream = second_stream + rows_scatter(parts.reshape(members, group, wide))
-    slot_of = [((k & 2) << 1) | ((k & 4) >> 1) | (k & 1) for k in range(members)]
+    third_stream = second_stream + rows_scatter(rows_parts(dot(attended_low, own_attention_out, 1, 0)))
     own_kv = qkv[:, head_width:].reshape(members, group, 2, head_width).transpose(0, 2, 1, 3)
-    segment_kv = kv_back([own_kv[slot_of[k]] for k in range(members)], BF)
-
-    fourth_stream, second_kept = plane_forward_ffn(
-        third_stream, gains[3], own_second, own_second_down
-    )
-    output = swap_planes(fourth_stream.astype(BF))
-
-    def hidden_back(grad_columns):
-        got = columns_out(grad_columns).astype(F32)
-        got = got.reshape(planes, inner, shard, 2, planes, units)
-        return got.transpose(2, 3, 0, 4, 1, 5).reshape(shard, -1)
-
-    def down_back(grad_down):
-        return reduce_z(grad_down.astype(BF).reshape(planes, units, wide)).astype(F32)
-
-    grad, second_gain_grad, grad_columns, grad_down = plane_backward_ffn(
-        third_stream, grad, grad_whole, gains[3], own_second, own_second_down, second_kept
-    )
-    second_gate_up_grad = hidden_back(grad_columns)
-    second_down_grad = down_back(grad_down)
+    own_kv = tie(own_kv, third_stream).reshape(2, 2, inner, 2, group, head_width)
+
+    second_normed = gather_plane(rms_gain(third_stream, gains[3]).astype(BF)).reshape(-1, wide)
+    second_both, second_hidden = ffn_gate(second_normed, own_second)
+    second_parts = parts_of(dot(second_hidden, own_second_down, 1, 0))
+    fourth_stream = third_stream + scatter_plane(second_parts)
+    def hidden_back(got):
+        moves = []
+        for column in range(2 * planes * members):
+            part, uu, cc, yx, vv = column >> 5, column >> 4 & 1, column >> 3 & 1, column >> 1 & 3, column & 1
+            source = (0, yx * 2 + cc, ((part * 2 + uu) * 2 + vv) * units, units)
+            moves.append(((0, column * units), shard, source))
+        return assemble([got], moves, (shard, 2 * planes * members * units))
+
+    def cache_back(part):
+        part = part.reshape(planes, rows, cache_rows, head_width)
+        return swap_planes(jnp.concatenate([part[g] for g in range(planes)], axis=2))
+
+    grad_both = ffn_gate_back(dot(grad_whole, own_second_down, 1, 1), second_both)
+    grad_normed = scatter_plane(parts_of(dot(grad_both, own_second, 1, 1)))
+    second_columns = reduce_squares(by_square(dot(second_normed, grad_both, 0, 0).astype(BF)))
+    second_rows = dot(second_hidden, grad_whole, 0, 0).astype(BF)
+    grad_stream, second_gain_grad = norm_back(third_stream, gains[3], grad_normed)
+    grad = grad + grad_stream
 
     grad_rows = rows_gather(grad.astype(BF)).reshape(-1, wide)
     grad_attended = dot(grad_rows, own_attention_out, 1, 1).astype(BF)
-    grad_cache, dq, dk, dv = attend_back(length, qkv, grad_attended, attended, log, cache)
+    own_kv = kv_owners(tie(own_kv, grad_attended))
+    returned = swap_planes(jnp.concatenate([fourth_stream.astype(BF), own_kv], axis=2))
+    output, segment_kv = returned[..., :wide], returned[..., wide:]
+    back_keys, back_contents, dq, dk, dv = attend_back(
+        length, qkv, grad_attended, attended, log, cached_keys, cached_contents
+    )
     grad_qkv = jnp.concatenate([dq, dk, dv], axis=1)
-    parts = dot(grad_qkv, own_qkv, 1, 1).astype(BF)
-    grad_normed = rows_scatter(parts.reshape(members, group, wide))
+    grad_normed = rows_scatter(rows_parts(dot(grad_qkv, own_qkv, 1, 1)))
     grad_stream, attention_gain_grad = norm_back(second_stream, gains[2], grad_normed)
     grad = grad + grad_stream
-    grad_cache = kv_back([grad_cache[k] for k in range(members)], F32)
-    grad_out = dot(attended_low, grad_rows, 0, 0).astype(BF)
-    grad_out = reduce_z(grad_out.reshape(planes, inner, shard, wide))
-    theirs = other(lax.dynamic_index_in_dim(grad_out, 1 - x, 0, False), "x").astype(F32)
-    attention_out_grad = lax.dynamic_index_in_dim(grad_out, x, 0, False).astype(F32) + theirs
-    got = columns_out(dot(normed_rows, grad_qkv, 0, 0)).astype(F32)
-    got = jnp.sum(got.reshape(planes, inner, shard, 3, head_width), axis=1)
-    attention_qkv_grad = got.transpose(1, 2, 0, 3).reshape(shard, 3 * wide)
+    grad, second_columns = settle(grad, second_columns)
+
+    grad_out = dot(attended_low, grad_rows, 0, 0).astype(BF).reshape(inner, planes, shard, wide)
+    grad_out = pair_sum(grad_out, "c").astype(BF)
+    attention_out_grad = reduce_squares(grad_out)
+    second_down_grad = reduce_squares(second_rows.reshape(planes, units, wide)).astype(F32)
+    qkv_columns = reduce_squares(by_square(dot(normed_rows, grad_qkv, 0, 0).astype(BF)))
 
     grad_whole = gather_plane(grad.astype(BF)).reshape(-1, wide)
-    grad, first_gain_grad, grad_columns, grad_down = plane_backward_ffn(
-        first_stream, grad, grad_whole, gains[1], own_first, own_first_down, first_kept
-    )
-    first_gate_up_grad = hidden_back(grad_columns)
-    first_down_grad = down_back(grad_down)
+    grad_whole, second_down_grad = settle(grad_whole, second_down_grad)
+    back_keys = trade(tie(back_keys, grad_whole), PLANE)
+    grad_both = ffn_gate_back(dot(grad_whole, own_first_down, 1, 1), first_both)
+    grad_normed = scatter_plane(parts_of(dot(grad_both, own_first, 1, 1)))
+    first_columns = reduce_squares(by_square(dot(first_normed, grad_both, 0, 0).astype(BF)))
+    first_rows = dot(first_hidden, grad_whole, 0, 0).astype(BF)
+    grad_stream, first_gain_grad = norm_back(first_stream, gains[1], grad_normed)
+    grad = grad + grad_stream
+    grad, qkv_columns, attention_out_grad = settle(grad, qkv_columns, attention_out_grad)
+    first_down_grad = reduce_squares(first_rows.reshape(planes, units, wide)).astype(F32)
 
     grad_whole = gather_plane(grad.astype(BF)).reshape(-1, wide)
+    grad_whole, back_keys = settle(grad_whole, back_keys)
+    back_keys = cache_back(back_keys)
+    second_got = trade(tie(second_columns, grad_whole), PLANE)
     grad_gated = dot(grad_whole, own_out, 1, 1).reshape(mixed.shape)
     grad_core = grad_gated * jax.nn.silu(gate)
-    grad_gate = (grad_gated * mixed_out * silu_slope(gate)).astype(BF)
+    grad_core, second_got = settle(grad_core, second_got)
+    second_gate_up_grad = hidden_back(second_got)
+    back_contents = trade(tie(back_contents, grad_core), PLANE)
+    grad_gate = (grad_gated * mixed_out * silu_slope(gate)).astype(BF).reshape(-1, width)
     skip_grad = jnp.sum(grad_core * mixed, axis=(0, 1, 2))
     grad_mixed, grad_step, grad_b, grad_c, grad_decay, grad_start = scan_back(
         order, mixed, step, wide_b, wide_c, grad_core, past, decay, end
     )
-    grad_state = swap_planes(grad_start)
+    new_state, grad_state = swap_planes(jnp.stack([end, grad_start]))
+    grad_out = dot(gated, grad_whole, 0, 0).astype(BF).reshape(planes, channels, wide)
+    out_rows = reduce_squares(grad_out)
+    gate_columns = reduce_squares(by_square(dot(normed, grad_gate, 0, 0).astype(BF)))
+    grad_step, back_contents, first_columns, first_down_grad = settle(
+        grad_step, back_contents, first_columns, first_down_grad
+    )
+    back_contents = cache_back(back_contents)
+    got = trade(tie(qkv_columns, grad_step), PLANE)
     grad_pre = grad_step * valid * jax.nn.sigmoid(pre)
     step_bias_grad = jnp.sum(grad_pre, axis=(0, 1, 2))
     grad_pre = grad_pre.astype(BF).reshape(-1, width)
     step_proj_grad = dot(grad_pre, step_low, 0, 0)
     grad_low = dot(grad_pre, own_step_proj, 1, 0).reshape(members, rows, group, rank)
-    grad_select = sum_plane(
-        jnp.concatenate([grad_low, jnp.sum(grad_b, axis=-1), jnp.sum(grad_c, axis=-1)], axis=-1)
-    )
+    grad_select = sum_plane(jnp.concatenate(
+            [grad_low] + [jnp.sum(part.astype(F32), axis=-1) for part in (grad_b, grad_c)], axis=-1
+        ))
     grad_select = grad_select.astype(BF).reshape(-1, rank + 2 * states)
+    grad_select, got, gate_columns, out_rows, back_keys = settle(
+        grad_select, got, gate_columns, out_rows, back_keys
+    )
+    got = jnp.sum(got.reshape(planes, inner, shard, -1).astype(F32), axis=1)
+    moves = []
+    for owner in range(planes):
+        for part in range(3):
+            source = (0, owner, part * head_width, head_width)
+            moves.append(((0, part * wide + owner * head_width), shard, source))
+    attention_qkv_grad = assemble([got], moves, (shard, 3 * wide))
+    first_got = trade(tie(first_columns, grad_select), PLANE)
     selection_grad = dot(flat_low, grad_select, 0, 0)
     grad_mixed = (
         grad_mixed
         + grad_core * skip
         + dot(grad_select, own_selection, 1, 1).reshape(mixed.shape)
     )
-    grad_inner, tap_sums = conv_back(order, grad_mixed, total, projected, taps)
-    grad_projected = jnp.concatenate([grad_inner, grad_gate], axis=-1).reshape(-1, 2 * width)
-    parts = dot(grad_projected, own_in, 1, 1).astype(BF).reshape(members, rows, group, wide)
-    grad_normed = scatter_plane(parts)
+    grad_inner, tap_sums = conv_back(order, grad_mixed, total, inner_part, taps)
+    grad_inner, first_got = settle(grad_inner.reshape(-1, width), first_got)
+    first_gate_up_grad = hidden_back(first_got)
+    inner_columns = by_square(dot(normed, grad_inner, 0, 0).astype(BF))
+    grad_inner = tie(grad_inner, inner_columns)
+    inner_columns = reduce_squares(inner_columns)
+    parts = dot(grad_inner, own_inner, 1, 1) + dot(grad_gate, own_gate, 1, 1)
+    gate_columns = trade(tie(gate_columns, grad_inner), PLANE)
+    moved = relocate(jnp.concatenate([out_rows, attention_out_grad], axis=0), True).astype(F32)
+    mamba_out_grad, attention_out_grad = moved[:channels], moved[channels:]
+    inner_columns = trade(inner_columns, PLANE)
+    grad_normed = scatter_plane(parts_of(parts))
     grad_stream, mamba_gain_grad = norm_back(stream, gains[0], grad_normed)
     grad_input = swap_planes(grad + grad_stream)
-
-    got = columns_out(dot(normed, grad_projected, 0, 0)).astype(F32)
-    got = got.reshape(members, shard, 2, width)
-    mamba_in_grad = got.transpose(1, 2, 0, 3).reshape(shard, -1)
-    grad_out = dot(gated, grad_whole, 0, 0).astype(BF).reshape(planes, channels, wide)
-    mamba_out_grad = relocate(reduce_z(grad_out), True).astype(F32)
+    moves = []
+    for which in range(2):
+        for owner in range(members):
+            column = (which * members + owner) * width
+            moves.append(((0, column), shard, (which, owner, 0, width)))
+    mamba_in_grad = assemble([inner_columns, gate_columns], moves, mamba_in.shape)
     packed = jnp.concatenate(
         [
             selection_grad,
@@ -1629,26 +1681,20 @@
         axis=1,
     )
     packed = jnp.pad(packed, ((0, 0), (0, -packed.shape[1] % 128)))
-    packed = packed.reshape(planes, channels, -1)
-    summed = lax.dynamic_index_in_dim(packed, z, 0, False)
-    for distance in range(1, planes):
-        goal = (z + distance) % planes
-        summed = summed + turned(lax.dynamic_index_in_dim(packed, goal, 0, False), distance)
-    packed = relocate(summed, True)
+    packed = pair_sum(pair_sum(packed.reshape(2, 2, channels, -1), "u"), "v")
+    packed = relocate(packed, True)
     pieces = [packed[:, starts[index] : starts[index + 1]] for index in range(len(cuts))]
 
-    gain_grads = total_small(jnp.stack([first_gain_grad, attention_gain_grad, second_gain_grad]))
-    mamba_gain_grad = total_small(mamba_gain_grad[None])
-    gain_grads = jnp.concatenate([mamba_gain_grad, gain_grads], axis=0)
-    index = ((y * 2 + c) * planes + z) * inner + x
-    gain_grads = lax.dynamic_slice_in_dim(gain_grads, index * shard, shard, 1)
+    gain_grads = jnp.stack([mamba_gain_grad, first_gain_grad, attention_gain_grad, second_gain_grad])
+    index = (u * 2 + c) * members + place
+    gain_grads = lax.dynamic_slice_in_dim(total_small(gain_grads), index * shard, shard, 1)
     return (
         output,
         new_state,
         segment_kv,
         grad_input,
         grad_state,
-        grad_cache,
+        jnp.concatenate([back_keys, back_contents], axis=2).astype(F32),
         gain_grads[0],
         mamba_in_grad,
         pieces[2].T,
@@ -1743,8 +1789,8 @@
             local, mesh=mesh, in_specs=places, out_specs=results, check_vma=False
         )
     dp, seq = mesh.shape["dp"], mesh.shape["seq"]
-    devices = mesh.devices.reshape(dp // 2, 2, dp, seq // dp)
-    places, results = placements(("y", "c"), ("z", "x"))
+    devices = mesh.devices.reshape(dp // 2, 2, seq // 4, 2, 2)
+    places, results = placements(("u", "c"), ("y", "x", "v"))
     return jax.shard_map(
         plane_local,
         mesh=Mesh(devices, EVERY),

time: 1330 us -> 1210 us (0.910)
  starting transfers between devices: 521 us -> 179 us
  waiting for transfers between devices: 309 us -> 549 us
  Pallas kernels: 107 us -> 83.4 us
  other arithmetic: 108 us -> 125 us
    ppermute x102 -> x94, waiting for transfers between devices: 202 us -> 471 us  [other(): return lax.ppermute(block, axis, [(0, 1), (1, 0)])]
    ppermute x102 -> x94, starting transfers between devices: 312 us -> 102 us  [other(): return lax.ppermute(block, axis, [(0, 1), (1, 0)])]
    ppermute x51 -> x13, starting transfers between devices: 179 us -> 18 us  [the longest x9 13.6 us: swap_planes(): return jnp.where(away, lax.ppermute(block, EVERY, route), block)]
    ppermute x51 -> x13, waiting for transfers between devices: 81.8 us -> 0.03 us  [the longest x9 0.02 us: swap_planes(): return jnp.where(away, lax.ppermute(block, EVERY, route), block)]
    all_to_all x6 -> x13, waiting for transfers between devices: 7.53 us -> 54.3 us  [trade(): return lax.all_to_all(block, axes, 0, 0, tiled=True)]
    all_to_all x6 -> x13, starting transfers between devices: 27.9 us -> 57 us  [trade(): return lax.all_to_all(block, axes, 0, 0, tiled=True)]
    reshape x23 -> x11, local copies, waits for them, and re-layouts: 27.9 us -> 12.5 us  [the longest x4 4.22 us: hidden_columns(): split = gate_up.reshape(shard, 2, 2, 2, 2, 2, 2, units)]
    unnamed x361 -> x395, local copies, waits for them, and re-layouts: 39.6 us -> 48.5 us
  transfers between devices with their start and end apart: 175 -> 137, of which waited for: 75 -> 69; matrix products, arithmetic and copies ran while one was open for 25% -> 27% of each run, Pallas kernels for 8% -> 7%
where the time goes in v2:
time: 1210 us; the launch traced here: 1200 us
  waiting for transfers between devices  549 us (45%)
  starting transfers between devices  179 us (15%)
  local copies, waits for them, and re-layouts  146 us (12%)
  other arithmetic  125 us (10%)
  matrix products  102 us (8%)
  Pallas kernels  83.4 us (7%)
  between operations  17.8 us (1%)
    ppermute x94, waiting for transfers between devices, other(): return lax.ppermute(block, axis, [(0, 1), (1, 0)])  471 us
    ppermute x94, starting transfers between devices, other(): return lax.ppermute(block, axis, [(0, 1), (1, 0)])  102 us
    dot_general x33, matrix products, dot(): lax.dot_general(left, right, (((left_dim,), (right_dim,)), ((), ())), pre...  102 us
    all_to_all x13, starting transfers between devices, trade(): return lax.all_to_all(block, axes, 0, 0, tiled=True)  57 us
    all_to_all x13, waiting for transfers between devices, trade(): return lax.all_to_all(block, axes, 0, 0, tiled=True)  54.3 us
    unnamed x395, local copies, waits for them, and re-layouts  48.5 us
    pallas_call x1, Pallas kernels, scan_back(): pl.pallas_call(scan_back_body, grid_spec=pltpu.PrefetchScalarGridSpec(num...  24.2 us
  transfers between devices with their start and end apart: 137, of which 69 were waited for; matrix products, arithmetic and copies ran while one was open for 27% of the time, Pallas kernels for 7%

profile of v2, /device:TPU:0, one launch (start us, length us, event | category | flops | bytes accessed | tf_op | source)
XLA Modules:
  0.0 1201.9 jit_solution(634776210791821757)
XLA Ops:
  10.5 6.3 all-to-all-start
  41.4 10.9 collective-permute-start.2
  58.8 11.9 collective-permute-done.2
  95.5 23.1 %all-gather.17.cloned.1.call-done = bf16[32,48,512]{2,1,0:T(8,128)(2,1)} async-done(((bf16[8,48,512]{2,1,0:T(8,128)(2,1)}), bf16[32,48,512]{2,1,0:T(8,128)(2,1)}) %all-gather.17.cloned.1.call-update) | async-done | bytes 1572880 | tf_op jit(solution)/shard_map/all_gather | solution.py:774
  141.7 9.9 all-to-all-done.1
  158.4 24.9 %collective-permute-done.10 = f32[2,64,128]{2,1,0:T(8,128)S(1)} collective-permute-done((f32[2,64,128]{2,1,0:T(8,128)S(1)}, f32[2,64,128]{2,1,0:T(8,128)S(1)}, u32[]{:S(2)}, u32[]{:S(2)}) %collective-permute-start.10) | collective-permute-done | bytes 65568 | tf_op jit(solution)/shard_map/ppermute | solution.py:717
  189.1 6.8 collective-permute-done.11
  237.9 13.9 %scan_forward.1 = (f32[8,2,64,384]{3,2,1,0:T(8,128)S(1)}, f32[8,2,64,16,384]{4,3,2,1,0:T(8,128)}, f32[2,16,384]{2,1,0:T(8,128)S(1)}) custom-call(s32[8]{0:T(128)S(1)} %shift-right-arithmetic_or_fusion.order, f32[8,2,64,384]{3,2,1,0:T(8,128)S(1)} %get-tuple-element.102.mixed_ref, f32[8,2,64,384]{3,2,1,0:T(8,128)S(1)} %copy-done.10, ...), custom_call_target="tpu_custom_call" | custom-call | tf_op jit(solution)/shard_map/scan_forward/pallas_call | solution.py:994
  291.2 23.8 %collective-permute-done.21 = bf16[2,64,1536]{2,1,0:T(8,128)(2,1)S(1)} collective-permute-done((bf16[2,64,1536]{2,1,0:T(8,128)(2,1)S(1)}, bf16[2,64,1536]{2,1,0:T(8,128)(2,1)S(1)}, u32[]{:S(2)}, u32[]{:S(2)}) %collective-permute-start.21) | collective-permute-done | bytes 393248 | tf_op jit(solution)/shard_map/ppermute | solution.py:717
  315.7 6.5 collective-permute-done.23
  327.6 16.9 %collective-permute-done.25 = bf16[2,64,1536]{2,1,0:T(8,128)(2,1)S(1)} collective-permute-done((bf16[2,64,1536]{2,1,0:T(8,128)(2,1)S(1)}, bf16[2,64,1536]{2,1,0:T(8,128)(2,1)S(1)}, u32[]{:S(2)}, u32[]{:S(2)}) %collective-permute-start.25) | collective-permute-done | bytes 393248 | tf_op jit(solution)/shard_map/ppermute | solution.py:717
  344.6 10.8 collective-permute-done.26
  400.4 23.8 %collective-permute-done.29 = bf16[2,64,1536]{2,1,0:T(8,128)(2,1)S(1)} collective-permute-done((bf16[2,64,1536]{2,1,0:T(8,128)(2,1)}, bf16[2,64,1536]{2,1,0:T(8,128)(2,1)S(1)}, u32[]{:S(2)}, u32[]{:S(2)}) %collective-permute-start.29) | collective-permute-done | bytes 393248 | tf_op jit(solution)/shard_map/ppermute | solution.py:717
  424.2 8.4 collective-permute-done.31
  445.3 12.9 %collective-permute-done.34 = bf16[2,64,1536]{2,1,0:T(8,128)(2,1)S(1)} collective-permute-done((bf16[2,64,1536]{2,1,0:T(8,128)(2,1)}, bf16[2,64,1536]{2,1,0:T(8,128)(2,1)S(1)}, u32[]{:S(2)}, u32[]{:S(2)}) %collective-permute-start.34) | collective-permute-done | bytes 393248 | tf_op jit(solution)/shard_map/ppermute | solution.py:717
  464.3 7.4 collective-permute-done.35
  478.2 10.7 attend.1
  492.3 11.1 collective-permute-done.38
  505.7 10.6 collective-permute-done.37
  516.3 7.7 collective-permute-done.39
  530.2 17.0 %collective-permute-done.42 = bf16[2,64,1536]{2,1,0:T(8,128)(2,1)S(1)} collective-permute-done((bf16[2,64,1536]{2,1,0:T(8,128)(2,1)S(1)}, bf16[2,64,1536]{2,1,0:T(8,128)(2,1)S(1)}, u32[]{:S(2)}, u32[]{:S(2)}) %collective-permute-start.42) | collective-permute-done | bytes 393248 | tf_op jit(solution)/shard_map/ppermute | solution.py:717
  548.7 9.5 collective-permute-done.43
  581.6 6.5 convolution_convert_fusion.6
  599.8 10.0 collective-permute-done.55
  612.8 10.2 collective-permute-done.54
  640.9 13.6 %collective-permute-done.59 = bf16[2,64,1536]{2,1,0:T(8,128)(2,1)} collective-permute-done((bf16[2,64,1536]{2,1,0:T(8,128)(2,1)}, bf16[2,64,1536]{2,1,0:T(8,128)(2,1)}, u32[]{:S(2)}, u32[]{:S(2)}) %collective-permute-start.59) | collective-permute-done | bytes 393248 | tf_op jit(solution)/shard_map/ppermute | solution.py:717
  659.3 18.8 %collective-permute-done.58 = bf16[2,64,1536]{2,1,0:T(8,128)(2,1)S(1)} collective-permute-done((bf16[2,64,1536]{2,1,0:T(8,128)(2,1)}, bf16[2,64,1536]{2,1,0:T(8,128)(2,1)S(1)}, u32[]{:S(2)}, u32[]{:S(2)}) %collective-permute-start.58) | collective-permute-done | bytes 393248 | tf_op jit(solution)/shard_map/ppermute | solution.py:717
  678.1 8.0 collective-permute-done.60
  688.8 21.7 %attend_back.1 = (bf16[8,256,384]{2,1,0:T(8,128)(2,1)}, bf16[8,256,384]{2,1,0:T(8,128)(2,1)S(1)}, bf16[512,384]{1,0:T(8,128)(2,1)S(1)}, bf16[512,384]{1,0:T(8,128)(2,1)S(1)}, bf16[512,384]{1,0:T(8,128)(2,1)S(1)}) custom-call(s32[2]{0:T(128)S(1)} %pad_add_fusion.meta_ref, bf16[512,1152]{1,0:T(8,128)(2,1)S(1)} %convolution_convert_fusion.9.q_ref.k_ref.v_ref, ...), custom_call_target="tpu_custom_call" | custom-call | tf_op jit(solution)/shard_map/attend_back/pallas_call | solution.py:1300
  717.0 8.8 collective-permute-done.66
  728.2 10.2 collective-permute-done.65
  738.4 6.3 collective-permute-done.67
  761.7 17.6 %collective-permute-done.70 = bf16[2,64,1536]{2,1,0:T(8,128)(2,1)S(1)} collective-permute-done((bf16[2,64,1536]{2,1,0:T(8,128)(2,1)S(1)}, bf16[2,64,1536]{2,1,0:T(8,128)(2,1)S(1)}, u32[]{:S(2)}, u32[]{:S(2)}) %collective-permute-start.70) | collective-permute-done | bytes 393248 | tf_op jit(solution)/shard_map/ppermute | solution.py:717
  779.4 10.8 collective-permute-done.71
  819.4 15.4 %collective-permute-done.61 = bf16[2,2,2,64,384]{4,3,2,1,0:T(8,128)(2,1)} collective-permute-done((bf16[2,2,2,64,384]{4,3,2,1,0:T(8,128)(2,1)S(1)}, bf16[2,2,2,64,384]{4,3,2,1,0:T(8,128)(2,1)}, u32[]{:S(2)}, u32[]{:S(2)}) %collective-permute-start.61) | collective-permute-done | bytes 393248 | tf_op jit(solution)/shard_map/ppermute | solution.py:717
  848.2 17.0 %collective-permute-done.74 = bf16[2,64,1536]{2,1,0:T(8,128)(2,1)} collective-permute-done((bf16[2,64,1536]{2,1,0:T(8,128)(2,1)}, bf16[2,64,1536]{2,1,0:T(8,128)(2,1)}, u32[]{:S(2)}, u32[]{:S(2)}) %collective-permute-start.74) | collective-permute-done | bytes 393248 | tf_op jit(solution)/shard_map/ppermute | solution.py:717
  873.3 16.2 %collective-permute-done.79 = bf16[2,64,1536]{2,1,0:T(8,128)(2,1)} collective-permute-done((bf16[2,64,1536]{2,1,0:T(8,128)(2,1)}, bf16[2,64,1536]{2,1,0:T(8,128)(2,1)}, u32[]{:S(2)}, u32[]{:S(2)}) %collective-permute-start.79) | collective-permute-done | bytes 393248 | tf_op jit(solution)/shard_map/ppermute | solution.py:717
  895.9 7.7 collective-permute-done.80
  914.7 17.4 %all-to-all-done.6 = bf16[8,256,384]{2,1,0:T(8,128)(2,1)S(1)} async-done(((bf16[8,256,384]{2,1,0:T(8,128)(2,1)}), bf16[8,256,384]{2,1,0:T(8,128)(2,1)S(1)}, u32[]{:S(2)}, u32[]{:S(2)}) %all-to-all-start.6) | async-done | bytes 1572896 | tf_op jit(solution)/shard_map/all_to_all | solution.py:747
  949.7 7.5 all-to-all-done.7.refs_0_
  973.4 24.2 %scan_back.1 = (f32[8,2,64,384]{3,2,1,0:T(8,128)S(1)}, f32[8,2,64,384]{3,2,1,0:T(8,128)S(1)}, bf16[8,2,64,16,128]{4,3,2,1,0:T(8,128)(2,1)S(1)}, bf16[8,2,64,16,1...) custom-call(s32[8]{0:T(128)S(1)} %copy-done.29, f32[8,2,64,384]{3,2,1,0:T(8,128)S(1)} %copy-done.5, ...), custom_call_target="tpu_custom_call" | custom-call | tf_op jit(solution)/shard_map/scan_back/pallas_call | solution.py:1119
  1031.2 12.2 %collective-permute-done.85 = f32[2,64,128]{2,1,0:T(8,128)S(1)} collective-permute-done((f32[2,64,128]{2,1,0:T(8,128)S(1)}, f32[2,64,128]{2,1,0:T(8,128)S(1)}, u32[]{:S(2)}, u32[]{:S(2)}) %collective-permute-start.85) | collective-permute-done | bytes 65568 | tf_op jit(solution)/shard_map/ppermute | solution.py:717
  1076.1 12.1 %all-to-all-done.10.refs_0_ = bf16[8,48,1024]{2,1,0:T(8,128)(2,1)} async-done(((bf16[8,48,1024]{2,1,0:T(8,128)(2,1)}), bf16[8,48,1024]{2,1,0:T(8,128)(2,1)}, u32[]{:S(2)}, u32[]{:S(2)}) %all-to-all-start.10) | async-done | bytes 786464 | tf_op jit(solution)/shard_map/all_to_all | solution.py:747
  1118.2 7.5 collective-permute-start.93
  1125.7 8.0 collective-permute-done.94
  1134.6 7.3 collective-permute-done.93
  1141.9 7.9 collective-permute-done.95
  1165.4 8.5 collective-permute-done.100
  (939 shorter events, 588.0 us)
Async XLA Ops:
  10.5 75.9 %all-to-all-start = ((bf16[8,48,896]{2,1,0:T(8,128)(2,1)}), bf16[8,48,896]{2,1,0:T(8,128)(2,1)}, u32[]{:S(2)}, u32[]{:S(2)}) async-start(bf16[8,48,896]{2,1,0:T(8,128)(2,1)} %pad_maximum_fusion.22), calls=%async_computation | async-start | bytes 1376256 | tf_op jit(solution)/shard_map/all_to_all | solution.py:747
  16.8 101.7 %all-gather.17.cloned.1.call-start = ((), (), s32[]{:S(2)}) async-start(), calls=%async_computation.22 | async-start | bytes 1966080 | tf_op jit(solution)/shard_map/all_gather | solution.py:774
  41.4 29.4 %collective-permute-start.2 = (bf16[2,64,1536]{2,1,0:T(8,128)(2,1)}, bf16[2,64,1536]{2,1,0:T(8,128)(2,1)}, u32[]{:S(2)}, u32[]{:S(2)}) collective-permute-start(bf16[2,64,1536]{2,1,0:T(8,128)(2,1)} %get-tuple-element.323), channel_id=1, source_target_pairs={{0,4},{4,0},{1,5},{5,1},{2,6},{6,2},{3,7},{7,3},{8,12},{12,8},{9,1... | collective-permute-start | bytes 1179656 | tf_op jit(solution)/shard_map/ppermute | solution.py:717
  57.0 33.3 %collective-permute-start.16 = (bf16[2,256,1536]{2,1,0:T(8,128)(2,1)}, bf16[2,256,1536]{2,1,0:T(8,128)(2,1)}, u32[]{:S(2)}, u32[]{:S(2)}) collective-permute-start(bf16[2,256,1536]{2,1,0:T(8,128)(2,1)} %get-tuple-element.105), channel_id=1, source_target_pairs={{1,8},{3,10},{5,12},{7,14},{8,1},{10,3},{12,5},{14,7},{17,24},{19,... | collective-permute-start | bytes 4718600 | tf_op jit(solution)/shard_map/ppermute | solution.py:713
  76.6 81.5 %collective-permute-start.18 = (f32[2,24,384]{2,1,0:T(8,128)S(1)}, f32[2,24,384]{2,1,0:T(8,128)}, u32[]{:S(2)}, u32[]{:S(2)}) collective-permute-start(f32[2,24,384]{2,1,0:T(8,128)S(1)} %pad_maximum_fusion.35), channel_id=1, source_target_pairs={{1,8},{3,10},{5,12},{7,14},{8,1},{10,3},{12,5},{14,7},{17,24},{19,... | collective-permute-start | bytes 221192 | tf_op jit(solution)/shard_map/ppermute | solution.py:713
  77.9 145.1 %collective-permute-start.19 = (bf16[144,1536]{1,0:T(8,128)(2,1)}, bf16[144,1536]{1,0:T(8,128)(2,1)}, u32[]{:S(2)}, u32[]{:S(2)}) collective-permute-start(bf16[144,1536]{1,0:T(8,128)(2,1)} %pad_maximum_fusion.25), channel_id=1, source_target_pairs={{2,16},{3,17},{4,8},{5,9},{6,24},{7,25},{8,2},{9,3},{10,18},{11,19... | collective-permute-start | bytes 1327112 | tf_op jit(solution)/shard_map/ppermute | solution.py:829
  138.9 71.0 %collective-permute-start.17 = (bf16[2,320,1536]{2,1,0:T(8,128)(2,1)}, bf16[2,320,1536]{2,1,0:T(8,128)(2,1)}, u32[]{:S(2)}, u32[]{:S(2)}) collective-permute-start(bf16[2,320,1536]{2,1,0:T(8,128)(2,1)} %pad_maximum_fusion.2), channel_id=1, source_target_pairs={{1,8},{3,10},{5,12},{7,14},{8,1},{10,3},{12,5},{14,7},{17,24},{19,... | collective-permute-start | bytes 5898248 | tf_op jit(solution)/shard_map/ppermute | solution.py:713
  151.5 61.5 %all-to-all-start.2 = ((bf16[8,256,384]{2,1,0:T(8,128)(2,1)}), bf16[8,256,384]{2,1,0:T(8,128)(2,1)S(1)}, u32[]{:S(2)}, u32[]{:S(2)}) async-start(bf16[8,256,384]{2,1,0:T(8,128)(2,1)} %pad_maximum_fusion.4), calls=%async_computation.2 | async-start | bytes 3145728 | tf_op jit(solution)/shard_map/all_to_all | solution.py:747
  155.3 72.8 %all-gather.19.cloned.1.call-start = ((), (), s32[]{:S(2)}) async-start(), calls=%async_computation.23 | async-start | bytes 1474560 | tf_op jit(solution)/shard_map/all_gather | solution.py:774
  158.2 30.9 %collective-permute-start.9 = (f32[2,64,128]{2,1,0:T(8,128)S(1)}, f32[2,64,128]{2,1,0:T(8,128)S(1)}, u32[]{:S(2)}, u32[]{:S(2)}) collective-permute-start(f32[2,64,128]{2,1,0:T(8,128)S(1)} %get-tuple-element.440), channel_id=1, source_target_pairs={{0,2},{2,0},{1,3},{3,1},{4,6},{6,4},{5,7},{7,5},{8,10},{10,8},{9,1... | collective-permute-start | bytes 196616 | tf_op jit(solution)/shard_map/ppermute | solution.py:717
  218.5 42.3 %all-to-all-start.3 = ((bf16[8,256,384]{2,1,0:T(8,128)(2,1)}), bf16[8,256,384]{2,1,0:T(8,128)(2,1)}, u32[]{:S(2)}, u32[]{:S(2)}) async-start(bf16[8,256,384]{2,1,0:T(8,128)(2,1)} %pad_maximum_fusion.5), calls=%async_computation.3 | async-start | bytes 3145728 | tf_op jit(solution)/shard_map/all_to_all | solution.py:747
  222.9 43.9 %all-gather.21.cloned.1.call-start = ((), (), s32[]{:S(2)}) async-start(), calls=%async_computation.24 | async-start | bytes 1474560 | tf_op jit(solution)/shard_map/all_gather | solution.py:774
  226.3 132.4 %all-gather.23.cloned.1.call-start = ((), (), s32[]{:S(2)}) async-start(), calls=%async_computation.25 | async-start | bytes 3932160 | tf_op jit(solution)/shard_map/all_gather | solution.py:774
  278.2 45.6 %all-to-all-start.4 = ((bf16[8,48,1152]{2,1,0:T(8,128)(2,1)}), bf16[8,48,1152]{2,1,0:T(8,128)(2,1)}, u32[]{:S(2)}, u32[]{:S(2)}) async-start(bf16[8,48,1152]{2,1,0:T(8,128)(2,1)} %bitcast.58), calls=%async_computation.4 | async-start | bytes 1769472 | tf_op jit(solution)/shard_map/all_to_all | solution.py:747
  282.4 88.5 %all-gather.25.cloned.1.call-start = ((), (), s32[]{:S(2)}) async-start(), calls=%async_computation.26 | async-start | bytes 1966080 | tf_op jit(solution)/shard_map/all_gather | solution.py:774
  282.4 32.5 %collective-permute-start.21 = (bf16[2,64,1536]{2,1,0:T(8,128)(2,1)S(1)}, bf16[2,64,1536]{2,1,0:T(8,128)(2,1)S(1)}, u32[]{:S(2)}, u32[]{:S(2)}) collective-permute-start(bf16[2,64,1536]{2,1,0:T(8,128)(2,1)S(1)} %get-tuple-element.404), channel_id=1, source_target_pairs={{0,2},{2,0},{1,3},{3,1},{4,6},{6,4},{5,7},{7,5},{8,10},{10,8},{9,1... | collective-permute-start | bytes 1179656 | tf_op jit(solution)/shard_map/ppermute | solution.py:717
  291.0 31.3 %collective-permute-start.23 = (bf16[2,64,1536]{2,1,0:T(8,128)(2,1)S(1)}, bf16[2,64,1536]{2,1,0:T(8,128)(2,1)S(1)}, u32[]{:S(2)}, u32[]{:S(2)}) collective-permute-start(bf16[2,64,1536]{2,1,0:T(8,128)(2,1)S(1)} %fusion.48), channel_id=1, source_target_pairs={{0,4},{4,0},{1,5},{5,1},{2,6},{6,2},{3,7},{7,3},{8,12},{12,8},{9,1... | collective-permute-start | bytes 1179656 | tf_op jit(solution)/shard_map/ppermute | solution.py:717
  291.1 144.6 %all-gather.29.cloned.1.call-start = ((), (), s32[]{:S(2)}) async-start(), calls=%async_computation.28 | async-start | bytes 2703360 | tf_op jit(solution)/shard_map/all_gather | solution.py:774
  358.4 103.6 %all-gather.27.cloned.1.call-start = ((), (), s32[]{:S(2)}) async-start(), calls=%async_computation.27 | async-start | bytes 4423680 | tf_op jit(solution)/shard_map/all_gather | solution.py:774
  390.5 43.5 %all-to-all-start.5 = ((bf16[8,48,1024]{2,1,0:T(8,128)(2,1)}), bf16[8,48,1024]{2,1,0:T(8,128)(2,1)}, u32[]{:S(2)}, u32[]{:S(2)}) async-start(bf16[8,48,1024]{2,1,0:T(8,128)(2,1)} %reshape.588), calls=%async_computation.5 | async-start | bytes 1572864 | tf_op jit(solution)/shard_map/all_to_all | solution.py:747
  394.7 169.2 %all-gather.31.cloned.1.call-start = ((), (), s32[]{:S(2)}) async-start(), calls=%async_computation.29 | async-start | bytes 3932160 | tf_op jit(solution)/shard_map/all_gather | solution.py:774
  394.8 29.4 %collective-permute-start.29 = (bf16[2,64,1536]{2,1,0:T(8,128)(2,1)}, bf16[2,64,1536]{2,1,0:T(8,128)(2,1)S(1)}, u32[]{:S(2)}, u32[]{:S(2)}) collective-permute-start(bf16[2,64,1536]{2,1,0:T(8,128)(2,1)} %get-tuple-element.402), channel_id=1, source_target_pairs={{0,2},{2,0},{1,3},{3,1},{4,6},{6,4},{5,7},{7,5},{8,10},{10,8},{9,1... | collective-permute-start | bytes 1179656 | tf_op jit(solution)/shard_map/ppermute | solution.py:717
  398.3 34.3 %collective-permute-start.31 = (bf16[2,64,1536]{2,1,0:T(8,128)(2,1)S(1)}, bf16[2,64,1536]{2,1,0:T(8,128)(2,1)}, u32[]{:S(2)}, u32[]{:S(2)}) collective-permute-start(bf16[2,64,1536]{2,1,0:T(8,128)(2,1)S(1)} %fusion.43), channel_id=1, source_target_pairs={{0,4},{4,0},{1,5},{5,1},{2,6},{6,2},{3,7},{7,3},{8,12},{12,8},{9,1... | collective-permute-start | bytes 1179656 | tf_op jit(solution)/shard_map/ppermute | solution.py:717
  461.8 295.2 %reduce-scatter.28.cloned.1.call-start = ((), (), s32[]{:S(2)}) async-start(), calls=%async_computation.30 | async-start | bytes 3932160
  475.2 30.2 %collective-permute-start.50 = (bf16[2,64,1536]{2,1,0:T(8,128)(2,1)S(1)}, bf16[2,64,1536]{2,1,0:T(8,128)(2,1)S(1)}, u32[]{:S(2)}, u32[]{:S(2)}) collective-permute-start(bf16[2,64,1536]{2,1,0:T(8,128)(2,1)S(1)} %slice.572), channel_id=1, source_target_pairs={{0,4},{4,0},{1,5},{5,1},{2,6},{6,2},{3,7},{7,3},{8,12},{12,8},{9,1... | collective-permute-start | bytes 1179656 | tf_op jit(solution)/shard_map/ppermute | solution.py:717
  475.6 48.6 %collective-permute-start.49 = (bf16[2,64,1536]{2,1,0:T(8,128)(2,1)S(1)}, bf16[2,64,1536]{2,1,0:T(8,128)(2,1)S(1)}, u32[]{:S(2)}, u32[]{:S(2)}) collective-permute-start(bf16[2,64,1536]{2,1,0:T(8,128)(2,1)S(1)} %slice.572), channel_id=1, source_target_pairs={{0,2},{2,0},{1,3},{3,1},{4,6},{6,4},{5,7},{7,5},{8,10},{10,8},{9,1... | collective-permute-start | bytes 1179656 | tf_op jit(solution)/shard_map/ppermute | solution.py:717
  528.7 32.1 %collective-permute-start.52 = (bf16[4,2,64,1536]{3,2,1,0:T(8,128)(2,1)S(1)}, bf16[4,2,64,1536]{3,2,1,0:T(8,128)(2,1)S(1)}, u32[]{:S(2)}, u32[]{:S(2)}) collective-permute-start(bf16[4,2,64,1536]{3,2,1,0:T(8,128)(2,1)S(1)} %pad_maximum_fusion.9), channel_id=1, source_target_pairs={{0,8},{8,0},{1,9},{9,1},{2,10},{10,2},{3,11},{11,3},{4,12},{12,4},... | collective-permute-start | bytes 4718600 | tf_op jit(solution)/shard_map/ppermute | solution.py:717
  590.2 201.1 %reduce-scatter.30.cloned.1.call-start = ((), (), s32[]{:S(2)}) async-start(), calls=%async_computation.31 | async-start | bytes 1966080
  638.8 229.7 %reduce-scatter.34.cloned.1.call-start = ((), (), s32[]{:S(2)}) async-start(), calls=%async_computation.33 | async-start | bytes 737280
  638.8 115.2 %collective-permute-start.46 = (bf16[2,64,1536]{2,1,0:T(8,128)(2,1)}, bf16[2,64,1536]{2,1,0:T(8,128)(2,1)}, u32[]{:S(2)}, u32[]{:S(2)}) collective-permute-start(bf16[2,64,1536]{2,1,0:T(8,128)(2,1)} %get-tuple-element.394), channel_id=1, source_target_pairs={{0,2},{2,0},{1,3},{3,1},{4,6},{6,4},{5,7},{7,5},{8,10},{10,8},{9,1... | collective-permute-start | bytes 1179656 | tf_op jit(solution)/shard_map/ppermute | solution.py:717
  639.4 38.8 %collective-permute-start.58 = (bf16[2,64,1536]{2,1,0:T(8,128)(2,1)}, bf16[2,64,1536]{2,1,0:T(8,128)(2,1)S(1)}, u32[]{:S(2)}, u32[]{:S(2)}) collective-permute-start(bf16[2,64,1536]{2,1,0:T(8,128)(2,1)} %get-tuple-element.429), channel_id=1, source_target_pairs={{0,2},{2,0},{1,3},{3,1},{4,6},{6,4},{5,7},{7,5},{8,10},{10,8},{9,1... | collective-permute-start | bytes 1179656 | tf_op jit(solution)/shard_map/ppermute | solution.py:717
  654.6 31.6 %collective-permute-start.60 = (bf16[2,64,1536]{2,1,0:T(8,128)(2,1)}, bf16[2,64,1536]{2,1,0:T(8,128)(2,1)S(1)}, u32[]{:S(2)}, u32[]{:S(2)}) collective-permute-start(bf16[2,64,1536]{2,1,0:T(8,128)(2,1)} %collective-permute-done.59), channel_id=1, source_target_pairs={{0,2},{2,0},{1,3},{3,1},{4,6},{6,4},{5,7},{7,5},{8,10},{10,8},{9,1... | collective-permute-start | bytes 1179656 | tf_op jit(solution)/shard_map/ppermute | solution.py:717
  656.7 97.4 %collective-permute-start.48 = (bf16[2,64,1536]{2,1,0:T(8,128)(2,1)}, bf16[2,64,1536]{2,1,0:T(8,128)(2,1)}, u32[]{:S(2)}, u32[]{:S(2)}) collective-permute-start(bf16[2,64,1536]{2,1,0:T(8,128)(2,1)} %fusion.37), channel_id=1, source_target_pairs={{0,4},{4,0},{1,5},{5,1},{2,6},{6,2},{3,7},{7,3},{8,12},{12,8},{9,1... | collective-permute-start | bytes 1179656 | tf_op jit(solution)/shard_map/ppermute | solution.py:717
  728.2 140.3 %reduce-scatter.32.cloned.1.call-start = ((), (), s32[]{:S(2)}) async-start(), calls=%async_computation.32 | async-start | bytes 4423680
  750.9 210.7 %reduce-scatter.38.cloned.1.call-start = ((), (), s32[]{:S(2)}) async-start(), calls=%async_computation.35 | async-start | bytes 1966080
  813.2 197.2 %reduce-scatter.36.cloned.1.call-start = ((), (), s32[]{:S(2)}) async-start(), calls=%async_computation.34 | async-start | bytes 3932160
  836.9 33.9 %collective-permute-start.62 = (bf16[2,2,2,64,384]{4,3,2,1,0:T(8,128)(2,1)}, bf16[2,2,2,64,384]{4,3,2,1,0:T(8,128)(2,1)}, u32[]{:S(2)}, u32[]{:S(2)}) collective-permute-start(bf16[2,2,2,64,384]{4,3,2,1,0:T(8,128)(2,1)} %fusion.60), channel_id=1, source_target_pairs={{0,2},{2,0},{1,3},{3,1},{4,6},{6,4},{5,7},{7,5},{8,10},{10,8},{9,1... | collective-permute-start | bytes 1179656 | tf_op jit(solution)/shard_map/ppermute | solution.py:717
  836.9 28.2 %collective-permute-start.74 = (bf16[2,64,1536]{2,1,0:T(8,128)(2,1)}, bf16[2,64,1536]{2,1,0:T(8,128)(2,1)}, u32[]{:S(2)}, u32[]{:S(2)}) collective-permute-start(bf16[2,64,1536]{2,1,0:T(8,128)(2,1)} %get-tuple-element.388), channel_id=1, source_target_pairs={{0,2},{2,0},{1,3},{3,1},{4,6},{6,4},{5,7},{7,5},{8,10},{10,8},{9,1... | collective-permute-start | bytes 1179656 | tf_op jit(solution)/shard_map/ppermute | solution.py:717
  890.7 41.3 %all-to-all-start.6 = ((bf16[8,256,384]{2,1,0:T(8,128)(2,1)}), bf16[8,256,384]{2,1,0:T(8,128)(2,1)S(1)}, u32[]{:S(2)}, u32[]{:S(2)}) async-start(bf16[8,256,384]{2,1,0:T(8,128)(2,1)} %get-tuple-element.138), calls=%async_computation.6 | async-start | bytes 3145728 | tf_op jit(solution)/shard_map/all_to_all | solution.py:747
  906.4 29.9 %collective-permute-start.64 = (bf16[2,64,4608]{2,1,0:T(8,128)(2,1)}, bf16[2,64,4608]{2,1,0:T(8,128)(2,1)}, u32[]{:S(2)}, u32[]{:S(2)}) collective-permute-start(bf16[2,64,4608]{2,1,0:T(8,128)(2,1)} %pad_maximum_fusion.20), channel_id=1, source_target_pairs={{1,8},{3,10},{5,12},{7,14},{8,1},{10,3},{12,5},{14,7},{17,24},{19,... | collective-permute-start | bytes 3538952 | tf_op jit(solution)/shard_map/ppermute | solution.py:713
  936.3 126.5 %reduce-scatter.42.cloned.1.call-start = ((), (), s32[]{:S(2)}) async-start(), calls=%async_computation.37 | async-start | bytes 1474560
  957.2 53.1 %all-to-all-start.8 = ((bf16[8,256,384]{2,1,0:T(8,128)(2,1)}), bf16[8,256,384]{2,1,0:T(8,128)(2,1)}, u32[]{:S(2)}, u32[]{:S(2)}) async-start(bf16[8,256,384]{2,1,0:T(8,128)(2,1)} %copy-done.17), calls=%async_computation.8 | async-start | bytes 3145728 | tf_op jit(solution)/shard_map/all_to_all | solution.py:747
  961.5 101.2 %reduce-scatter.40.cloned.1.call-start = ((), (), s32[]{:S(2)}) async-start(), calls=%async_computation.36 | async-start | bytes 1474560
  966.5 52.6 %collective-permute-start.91 = (bf16[2,256,1536]{2,1,0:T(8,128)(2,1)}, bf16[2,256,1536]{2,1,0:T(8,128)(2,1)}, u32[]{:S(2)}, u32[]{:S(2)}) collective-permute-start(bf16[2,256,1536]{2,1,0:T(8,128)(2,1)} %pad_maximum_fusion.13), channel_id=1, source_target_pairs={{1,8},{3,10},{5,12},{7,14},{8,1},{10,3},{12,5},{14,7},{17,24},{19,... | collective-permute-start | bytes 4718600 | tf_op jit(solution)/shard_map/ppermute | solution.py:713
  1020.7 42.1 %all-to-all-start.9 = ((bf16[8,48,1152]{2,1,0:T(8,128)(2,1)}), bf16[8,48,1152]{2,1,0:T(8,128)(2,1)}, u32[]{:S(2)}, u32[]{:S(2)}) async-start(bf16[8,48,1152]{2,1,0:T(8,128)(2,1)} %bitcast.678), calls=%async_computation.9 | async-start | bytes 1769472 | tf_op jit(solution)/shard_map/all_to_all | solution.py:747
  1055.4 51.2 %collective-permute-start.97 = (bf16[2,256,1536]{2,1,0:T(8,128)(2,1)}, bf16[2,256,1536]{2,1,0:T(8,128)(2,1)}, u32[]{:S(2)}, u32[]{:S(2)}) collective-permute-start(bf16[2,256,1536]{2,1,0:T(8,128)(2,1)} %pad_maximum_fusion.14), channel_id=1, source_target_pairs={{1,8},{3,10},{5,12},{7,14},{8,1},{10,3},{12,5},{14,7},{17,24},{19,... | collective-permute-start | bytes 4718600 | tf_op jit(solution)/shard_map/ppermute | solution.py:713
  1067.1 111.9 %reduce-scatter.44.cloned.1.call-start = ((), (), s32[]{:S(2)}) async-start(), calls=%async_computation.38 | async-start | bytes 1474560
  1099.6 82.8 %collective-permute-start.106 = (bf16[144,1536]{1,0:T(8,128)(2,1)}, bf16[144,1536]{1,0:T(8,128)(2,1)}, u32[]{:S(2)}, u32[]{:S(2)}) collective-permute-start(bf16[144,1536]{1,0:T(8,128)(2,1)} %constant_dynamic-update-slice_fusion.42), channel_id=1, source_target_pairs={{16,2},{17,3},{8,4},{9,5},{24,6},{25,7},{2,8},{3,9},{18,10},{19,11... | collective-permute-start | bytes 1327112 | tf_op jit(solution)/shard_map/ppermute | solution.py:829
  (269 other events, 3805.0 us)
Sparse Core Ops, SparseCore 0:
  88.3 30.1 all-gather.16
  201.0 26.9 all-gather.18
  230.5 27.7 all-gather.20
  259.9 43.9 all-gather.22
  305.6 30.9 all-gather.24
  358.5 35.0 all-gather.28
  395.5 47.2 all-gather.26
  462.0 43.8 all-gather.30
  590.3 43.0 reduce-scatter.27
  638.9 29.1 reduce-scatter.29
  728.3 23.9 reduce-scatter.33
  755.5 47.2 reduce-scatter.31
  813.3 29.3 reduce-scatter.37
  848.3 43.3 reduce-scatter.35
  943.6 30.3 reduce-scatter.41
  977.0 31.0 reduce-scatter.39
  1134.7 27.8 reduce-scatter.43

commit v3 on v2

--- a/solution.py
+++ b/solution.py
@@ -754,8 +754,12 @@
 
 
 def total_small(block):
-    for axis in EVERY:
-        block = block + other(block, axis)
+    block = block + other(block, "c")
+    for axes in (("y", "x"), ("u", "v")):
+        turned = [
+            lax.ppermute(block, axes, [(k, k ^ turn) for k in range(4)]) for turn in (1, 2, 3)
+        ]
+        block = block + sum(turned)
     return block
 
 
@@ -1427,7 +1431,7 @@
     own_inner = rows_of(gather_squares(dealt[:, :, : width + 128]))
     gains = own_inner[:, width : width + 4].T.astype(F32)
     own_inner = own_inner[:, :width]
-    normed = gather_plane(tokens).reshape(-1, wide).astype(F32)
+    normed = gather_plane(tie(tokens, dealt)).reshape(-1, wide).astype(F32)
     normed = rms_gain(normed, gains[0]).astype(BF)
 
 
@@ -1642,7 +1646,6 @@
             source = (0, owner, part * head_width, head_width)
             moves.append(((0, part * wide + owner * head_width), shard, source))
     attention_qkv_grad = assemble([got], moves, (shard, 3 * wide))
-    first_got = trade(tie(first_columns, grad_select), PLANE)
     selection_grad = dot(flat_low, grad_select, 0, 0)
     grad_mixed = (
         grad_mixed
@@ -1650,7 +1653,8 @@
         + dot(grad_select, own_selection, 1, 1).reshape(mixed.shape)
     )
     grad_inner, tap_sums = conv_back(order, grad_mixed, total, inner_part, taps)
-    grad_inner, first_got = settle(grad_inner.reshape(-1, width), first_got)
+    grad_inner = grad_inner.reshape(-1, width)
+    first_got = trade(tie(first_columns, grad_inner), PLANE)
     first_gate_up_grad = hidden_back(first_got)
     inner_columns = by_square(dot(normed, grad_inner, 0, 0).astype(BF))
     grad_inner = tie(grad_inner, inner_columns)
@@ -1659,8 +1663,9 @@
     gate_columns = trade(tie(gate_columns, grad_inner), PLANE)
     moved = relocate(jnp.concatenate([out_rows, attention_out_grad], axis=0), True).astype(F32)
     mamba_out_grad, attention_out_grad = moved[:channels], moved[channels:]
+    grad_normed = scatter_plane(parts_of(parts))
+    grad_normed, inner_columns = settle(grad_normed, inner_columns)
     inner_columns = trade(inner_columns, PLANE)
-    grad_normed = scatter_plane(parts_of(parts))
     grad_stream, mamba_gain_grad = norm_back(stream, gains[0], grad_normed)
     grad_input = swap_planes(grad + grad_stream)
     moves = []

time: 1210 us -> 1200 us (level)
    all_gather x8, waiting for transfers between devices: 23.9 us -> 0.4 us  [gather_squares(): return lax.all_gather(block, SQUARES, axis=0)]
    ppermute x0 -> x6, waiting for transfers between devices: none -> 16.5 us  [total_small(): lax.ppermute(block, axes, [(k, k ^ turn) for k in range(4)])]
    ppermute x94 -> x90, waiting for transfers between devices: 471 us -> 485 us  [other(): return lax.ppermute(block, axis, [(0, 1), (1, 0)])]
    unnamed x395 -> x413, local copies, waits for them, and re-layouts: 48.5 us -> 42.7 us
    ppermute x94 -> x90, starting transfers between devices: 102 us -> 101 us  [other(): return lax.ppermute(block, axis, [(0, 1), (1, 0)])]
  transfers between devices with their start and end apart: 137 -> 139, of which waited for: 69 -> 67; matrix products, arithmetic and copies ran while one was open for 27% -> 26% of each run, Pallas kernels for 7% -> 7%
where the time goes in v3:
time: 1200 us; the launch traced here: 1180 us
  waiting for transfers between devices  546 us (46%)
  starting transfers between devices  186 us (16%)
  local copies, waits for them, and re-layouts  134 us (11%)
  other arithmetic  116 us (10%)
  matrix products  101 us (8%)
  Pallas kernels  82 us (7%)
  between operations  17.7 us (1%)
    ppermute x90, waiting for transfers between devices, other(): return lax.ppermute(block, axis, [(0, 1), (1, 0)])  485 us
    ppermute x90, starting transfers between devices, other(): return lax.ppermute(block, axis, [(0, 1), (1, 0)])  101 us
    dot_general x33, matrix products, dot(): lax.dot_general(left, right, (((left_dim,), (right_dim,)), ((), ())), pre...  101 us
    all_to_all x13, starting transfers between devices, trade(): return lax.all_to_all(block, axes, 0, 0, tiled=True)  56 us
    all_to_all x13, waiting for transfers between devices, trade(): return lax.all_to_all(block, axes, 0, 0, tiled=True)  43.8 us
    unnamed x413, local copies, waits for them, and re-layouts  42.7 us
    pallas_call x1, Pallas kernels, scan_back(): pl.pallas_call(scan_back_body, grid_spec=pltpu.PrefetchScalarGridSpec(num...  24.2 us
  transfers between devices with their start and end apart: 139, of which 67 were waited for; matrix products, arithmetic and copies ran while one was open for 26% of the time, Pallas kernels for 7%

profile of v3, /device:TPU:0, one launch (start us, length us, event | category | flops | bytes accessed | tf_op | source)
XLA Modules:
  0.0 1183.6 jit_solution(8320719699053395724)
XLA Ops:
  10.5 6.3 all-to-all-start
  64.5 18.2 %collective-permute-done.2 = bf16[2,64,1536]{2,1,0:T(8,128)(2,1)S(1)} collective-permute-done((bf16[2,64,1536]{2,1,0:T(8,128)(2,1)S(1)}, bf16[2,64,1536]{2,1,0:T(8,128)(2,1)S(1)}, u32[]{:S(2)}, u32[]{:S(2)}) %collective-permute-start.2) | collective-permute-done | bytes 393248 | tf_op jit(solution)/shard_map/ppermute | solution.py:717
  82.8 16.1 %collective-permute-done.1 = bf16[2,64,1536]{2,1,0:T(8,128)(2,1)S(1)} collective-permute-done((bf16[2,64,1536]{2,1,0:T(8,128)(2,1)S(1)}, bf16[2,64,1536]{2,1,0:T(8,128)(2,1)S(1)}, u32[]{:S(2)}, u32[]{:S(2)}) %collective-permute-start.1) | collective-permute-done | bytes 393248 | tf_op jit(solution)/shard_map/ppermute | solution.py:717
  128.7 9.2 all-to-all-done.1
  144.8 24.9 %collective-permute-done.10 = f32[2,64,128]{2,1,0:T(8,128)S(1)} collective-permute-done((f32[2,64,128]{2,1,0:T(8,128)S(1)}, f32[2,64,128]{2,1,0:T(8,128)S(1)}, u32[]{:S(2)}, u32[]{:S(2)}) %collective-permute-start.10) | collective-permute-done | bytes 65568 | tf_op jit(solution)/shard_map/ppermute | solution.py:717
  175.4 6.8 collective-permute-done.11
  223.7 13.9 %scan_forward.1 = (f32[8,2,64,384]{3,2,1,0:T(8,128)S(1)}, f32[8,2,64,16,384]{4,3,2,1,0:T(8,128)}, f32[2,16,384]{2,1,0:T(8,128)S(1)}) custom-call(s32[8]{0:T(128)S(1)} %shift-right-arithmetic_or_fusion.order, f32[8,2,64,384]{3,2,1,0:T(8,128)S(1)} %get-tuple-element.104.mixed_ref, f32[8,2,64,384]{3,2,1,0:T(8,128)S(1)} %copy-done.10, ...), custom_call_target="tpu_custom_call" | custom-call | tf_op jit(solution)/shard_map/scan_forward/pallas_call | solution.py:998
  247.2 6.1 multiply_convert_fusion.8
  278.4 23.8 %collective-permute-done.21 = bf16[2,64,1536]{2,1,0:T(8,128)(2,1)S(1)} collective-permute-done((bf16[2,64,1536]{2,1,0:T(8,128)(2,1)S(1)}, bf16[2,64,1536]{2,1,0:T(8,128)(2,1)S(1)}, u32[]{:S(2)}, u32[]{:S(2)}) %collective-permute-start.21) | collective-permute-done | bytes 393248 | tf_op jit(solution)/shard_map/ppermute | solution.py:717
  302.9 6.6 collective-permute-done.23
  314.8 16.9 %collective-permute-done.25 = bf16[2,64,1536]{2,1,0:T(8,128)(2,1)S(1)} collective-permute-done((bf16[2,64,1536]{2,1,0:T(8,128)(2,1)S(1)}, bf16[2,64,1536]{2,1,0:T(8,128)(2,1)S(1)}, u32[]{:S(2)}, u32[]{:S(2)}) %collective-permute-start.25) | collective-permute-done | bytes 393248 | tf_op jit(solution)/shard_map/ppermute | solution.py:717
  331.9 10.8 collective-permute-done.26
  387.7 23.8 %collective-permute-done.29 = bf16[2,64,1536]{2,1,0:T(8,128)(2,1)S(1)} collective-permute-done((bf16[2,64,1536]{2,1,0:T(8,128)(2,1)}, bf16[2,64,1536]{2,1,0:T(8,128)(2,1)S(1)}, u32[]{:S(2)}, u32[]{:S(2)}) %collective-permute-start.29) | collective-permute-done | bytes 393248 | tf_op jit(solution)/shard_map/ppermute | solution.py:717
  411.5 8.4 collective-permute-done.31
  432.6 12.9 %collective-permute-done.34 = bf16[2,64,1536]{2,1,0:T(8,128)(2,1)S(1)} collective-permute-done((bf16[2,64,1536]{2,1,0:T(8,128)(2,1)}, bf16[2,64,1536]{2,1,0:T(8,128)(2,1)S(1)}, u32[]{:S(2)}, u32[]{:S(2)}) %collective-permute-start.34) | collective-permute-done | bytes 393248 | tf_op jit(solution)/shard_map/ppermute | solution.py:717
  451.5 7.5 collective-permute-done.35
  465.4 10.4 attend.1
  479.2 11.4 collective-permute-done.38
  492.9 10.6 collective-permute-done.37
  503.5 7.7 collective-permute-done.39
  517.5 17.0 %collective-permute-done.42 = bf16[2,64,1536]{2,1,0:T(8,128)(2,1)S(1)} collective-permute-done((bf16[2,64,1536]{2,1,0:T(8,128)(2,1)S(1)}, bf16[2,64,1536]{2,1,0:T(8,128)(2,1)S(1)}, u32[]{:S(2)}, u32[]{:S(2)}) %collective-permute-start.42) | collective-permute-done | bytes 393248 | tf_op jit(solution)/shard_map/ppermute | solution.py:717
  535.9 9.5 collective-permute-done.43
  568.8 6.5 convolution_convert_fusion.6
  586.7 9.9 collective-permute-done.55
  600.0 9.9 collective-permute-done.54
  609.9 6.0 collective-permute-done.56
  628.1 14.1 %collective-permute-done.59 = bf16[2,64,1536]{2,1,0:T(8,128)(2,1)} collective-permute-done((bf16[2,64,1536]{2,1,0:T(8,128)(2,1)}, bf16[2,64,1536]{2,1,0:T(8,128)(2,1)}, u32[]{:S(2)}, u32[]{:S(2)}) %collective-permute-start.59) | collective-permute-done | bytes 393248 | tf_op jit(solution)/shard_map/ppermute | solution.py:717
  646.5 19.2 %collective-permute-done.58 = bf16[2,64,1536]{2,1,0:T(8,128)(2,1)S(1)} collective-permute-done((bf16[2,64,1536]{2,1,0:T(8,128)(2,1)}, bf16[2,64,1536]{2,1,0:T(8,128)(2,1)S(1)}, u32[]{:S(2)}, u32[]{:S(2)}) %collective-permute-start.58) | collective-permute-done | bytes 393248 | tf_op jit(solution)/shard_map/ppermute | solution.py:717
  665.7 8.0 collective-permute-done.60
  676.4 21.7 %attend_back.1 = (bf16[8,256,384]{2,1,0:T(8,128)(2,1)}, bf16[8,256,384]{2,1,0:T(8,128)(2,1)S(1)}, bf16[512,384]{1,0:T(8,128)(2,1)S(1)}, bf16[512,384]{1,0:T(8,128)(2,1)S(1)}, bf16[512,384]{1,0:T(8,128)(2,1)S(1)}) custom-call(s32[2]{0:T(128)S(1)} %pad_add_fusion.meta_ref, bf16[512,1152]{1,0:T(8,128)(2,1)S(1)} %convolution_convert_fusion.9.q_ref.k_ref.v_ref, ...), custom_call_target="tpu_custom_call" | custom-call | tf_op jit(solution)/shard_map/attend_back/pallas_call | solution.py:1304
  704.5 8.8 collective-permute-done.66
  715.4 10.2 collective-permute-done.65
  725.6 6.7 collective-permute-done.67
  748.8 17.6 %collective-permute-done.70 = bf16[2,64,1536]{2,1,0:T(8,128)(2,1)S(1)} collective-permute-done((bf16[2,64,1536]{2,1,0:T(8,128)(2,1)S(1)}, bf16[2,64,1536]{2,1,0:T(8,128)(2,1)S(1)}, u32[]{:S(2)}, u32[]{:S(2)}) %collective-permute-start.70) | collective-permute-done | bytes 393248 | tf_op jit(solution)/shard_map/ppermute | solution.py:717
  766.5 10.8 collective-permute-done.71
  806.9 14.9 %collective-permute-done.61 = bf16[2,2,2,64,384]{4,3,2,1,0:T(8,128)(2,1)} collective-permute-done((bf16[2,2,2,64,384]{4,3,2,1,0:T(8,128)(2,1)S(1)}, bf16[2,2,2,64,384]{4,3,2,1,0:T(8,128)(2,1)}, u32[]{:S(2)}, u32[]{:S(2)}) %collective-permute-start.61) | collective-permute-done | bytes 393248 | tf_op jit(solution)/shard_map/ppermute | solution.py:717
  835.6 16.7 %collective-permute-done.74 = bf16[2,64,1536]{2,1,0:T(8,128)(2,1)} collective-permute-done((bf16[2,64,1536]{2,1,0:T(8,128)(2,1)}, bf16[2,64,1536]{2,1,0:T(8,128)(2,1)}, u32[]{:S(2)}, u32[]{:S(2)}) %collective-permute-start.74) | collective-permute-done | bytes 393248 | tf_op jit(solution)/shard_map/ppermute | solution.py:717
  861.2 16.2 %collective-permute-done.79 = bf16[2,64,1536]{2,1,0:T(8,128)(2,1)} collective-permute-done((bf16[2,64,1536]{2,1,0:T(8,128)(2,1)}, bf16[2,64,1536]{2,1,0:T(8,128)(2,1)}, u32[]{:S(2)}, u32[]{:S(2)}) %collective-permute-start.79) | collective-permute-done | bytes 393248 | tf_op jit(solution)/shard_map/ppermute | solution.py:717
  883.4 8.4 collective-permute-done.80
  902.8 16.8 %all-to-all-done.6 = bf16[8,256,384]{2,1,0:T(8,128)(2,1)S(1)} async-done(((bf16[8,256,384]{2,1,0:T(8,128)(2,1)}), bf16[8,256,384]{2,1,0:T(8,128)(2,1)S(1)}, u32[]{:S(2)}, u32[]{:S(2)}) %all-to-all-start.6) | async-done | bytes 1572896 | tf_op jit(solution)/shard_map/all_to_all | solution.py:747
  931.1 6.3 multiply_convert_fusion.7
  937.3 7.5 all-to-all-done.7.refs_0_
  961.3 24.2 %scan_back.1 = (f32[8,2,64,384]{3,2,1,0:T(8,128)S(1)}, f32[8,2,64,384]{3,2,1,0:T(8,128)S(1)}, bf16[8,2,64,16,128]{4,3,2,1,0:T(8,128)(2,1)S(1)}, bf16[8,2,64,16,1...) custom-call(s32[8]{0:T(128)S(1)} %copy-done.29, f32[8,2,64,384]{3,2,1,0:T(8,128)S(1)} %copy-done.5, ...), custom_call_target="tpu_custom_call" | custom-call | tf_op jit(solution)/shard_map/scan_back/pallas_call | solution.py:1123
  1007.7 6.0 all-to-all-start.9
  1018.5 12.1 %collective-permute-done.85 = f32[2,64,128]{2,1,0:T(8,128)S(1)} collective-permute-done((f32[2,64,128]{2,1,0:T(8,128)S(1)}, f32[2,64,128]{2,1,0:T(8,128)S(1)}, u32[]{:S(2)}, u32[]{:S(2)}) %collective-permute-start.85) | collective-permute-done | bytes 65568 | tf_op jit(solution)/shard_map/ppermute | solution.py:717
  1092.2 6.2 collective-permute-start.94
  1114.2 10.0 collective-permute-done.93
  1138.2 16.5 %collective-permute-done.100 = f32[4,1536]{1,0:T(4,128)S(1)} collective-permute-done((f32[4,1536]{1,0:T(4,128)S(1)}, f32[4,1536]{1,0:T(4,128)S(1)}, u32[]{:S(2)}, u32[]{:S(2)}) %collective-permute-start.100) | collective-permute-done | bytes 24608 | tf_op jit(solution)/shard_map/ppermute | solution.py:760
  (958 shorter events, 575.9 us)
Async XLA Ops:
  10.5 42.3 %all-to-all-start = ((bf16[8,48,896]{2,1,0:T(8,128)(2,1)}), bf16[8,48,896]{2,1,0:T(8,128)(2,1)}, u32[]{:S(2)}, u32[]{:S(2)}) async-start(bf16[8,48,896]{2,1,0:T(8,128)(2,1)} %pad_maximum_fusion.22), calls=%async_computation | async-start | bytes 1376256 | tf_op jit(solution)/shard_map/all_to_all | solution.py:747
  16.8 92.5 %all-gather.17.cloned.1.call-start = ((), (), s32[]{:S(2)}) async-start(), calls=%async_computation.22 | async-start | bytes 1966080 | tf_op jit(solution)/shard_map/all_gather | solution.py:778
  47.4 56.1 %collective-permute-start.16 = (bf16[2,256,1536]{2,1,0:T(8,128)(2,1)S(1)}, bf16[2,256,1536]{2,1,0:T(8,128)(2,1)}, u32[]{:S(2)}, u32[]{:S(2)}) collective-permute-start(bf16[2,256,1536]{2,1,0:T(8,128)(2,1)S(1)} %get-tuple-element.107), channel_id=1, source_target_pairs={{1,8},{3,10},{5,12},{7,14},{8,1},{10,3},{12,5},{14,7},{17,24},{19,... | collective-permute-start | bytes 4718600 | tf_op jit(solution)/shard_map/ppermute | solution.py:713
  56.2 88.3 %collective-permute-start.18 = (f32[2,24,384]{2,1,0:T(8,128)S(1)}, f32[2,24,384]{2,1,0:T(8,128)}, u32[]{:S(2)}, u32[]{:S(2)}) collective-permute-start(f32[2,24,384]{2,1,0:T(8,128)S(1)} %pad_maximum_fusion.35), channel_id=1, source_target_pairs={{1,8},{3,10},{5,12},{7,14},{8,1},{10,3},{12,5},{14,7},{17,24},{19,... | collective-permute-start | bytes 221192 | tf_op jit(solution)/shard_map/ppermute | solution.py:713
  57.5 151.9 %collective-permute-start.19 = (bf16[144,1536]{1,0:T(8,128)(2,1)}, bf16[144,1536]{1,0:T(8,128)(2,1)}, u32[]{:S(2)}, u32[]{:S(2)}) collective-permute-start(bf16[144,1536]{1,0:T(8,128)(2,1)} %pad_maximum_fusion.25), channel_id=1, source_target_pairs={{2,16},{3,17},{4,8},{5,9},{6,24},{7,25},{8,2},{9,3},{10,18},{11,19... | collective-permute-start | bytes 1327112 | tf_op jit(solution)/shard_map/ppermute | solution.py:833
  59.0 40.0 %collective-permute-start.1 = (bf16[2,64,1536]{2,1,0:T(8,128)(2,1)S(1)}, bf16[2,64,1536]{2,1,0:T(8,128)(2,1)S(1)}, u32[]{:S(2)}, u32[]{:S(2)}) collective-permute-start(bf16[2,64,1536]{2,1,0:T(8,128)(2,1)S(1)} %get-tuple-element.102), channel_id=1, source_target_pairs={{0,2},{2,0},{1,3},{3,1},{4,6},{6,4},{5,7},{7,5},{8,10},{10,8},{9,1... | collective-permute-start | bytes 1179656 | tf_op jit(solution)/shard_map/ppermute | solution.py:717
  126.0 70.3 %collective-permute-start.17 = (bf16[2,320,1536]{2,1,0:T(8,128)(2,1)}, bf16[2,320,1536]{2,1,0:T(8,128)(2,1)}, u32[]{:S(2)}, u32[]{:S(2)}) collective-permute-start(bf16[2,320,1536]{2,1,0:T(8,128)(2,1)} %pad_maximum_fusion.2), channel_id=1, source_target_pairs={{1,8},{3,10},{5,12},{7,14},{8,1},{10,3},{12,5},{14,7},{17,24},{19,... | collective-permute-start | bytes 5898248 | tf_op jit(solution)/shard_map/ppermute | solution.py:713
  137.9 61.5 %all-to-all-start.2 = ((bf16[8,256,384]{2,1,0:T(8,128)(2,1)}), bf16[8,256,384]{2,1,0:T(8,128)(2,1)S(1)}, u32[]{:S(2)}, u32[]{:S(2)}) async-start(bf16[8,256,384]{2,1,0:T(8,128)(2,1)} %pad_maximum_fusion.4), calls=%async_computation.2 | async-start | bytes 3145728 | tf_op jit(solution)/shard_map/all_to_all | solution.py:747
  141.6 72.2 %all-gather.19.cloned.1.call-start = ((), (), s32[]{:S(2)}) async-start(), calls=%async_computation.23 | async-start | bytes 1474560 | tf_op jit(solution)/shard_map/all_gather | solution.py:778
  144.6 30.9 %collective-permute-start.9 = (f32[2,64,128]{2,1,0:T(8,128)S(1)}, f32[2,64,128]{2,1,0:T(8,128)S(1)}, u32[]{:S(2)}, u32[]{:S(2)}) collective-permute-start(f32[2,64,128]{2,1,0:T(8,128)S(1)} %get-tuple-element.442), channel_id=1, source_target_pairs={{0,2},{2,0},{1,3},{3,1},{4,6},{6,4},{5,7},{7,5},{8,10},{10,8},{9,1... | collective-permute-start | bytes 196616 | tf_op jit(solution)/shard_map/ppermute | solution.py:717
  204.9 42.3 %all-to-all-start.3 = ((bf16[8,256,384]{2,1,0:T(8,128)(2,1)}), bf16[8,256,384]{2,1,0:T(8,128)(2,1)}, u32[]{:S(2)}, u32[]{:S(2)}) async-start(bf16[8,256,384]{2,1,0:T(8,128)(2,1)} %pad_maximum_fusion.5), calls=%async_computation.3 | async-start | bytes 3145728 | tf_op jit(solution)/shard_map/all_to_all | solution.py:747
  209.4 43.9 %all-gather.21.cloned.1.call-start = ((), (), s32[]{:S(2)}) async-start(), calls=%async_computation.24 | async-start | bytes 1474560 | tf_op jit(solution)/shard_map/all_gather | solution.py:778
  212.7 133.4 %all-gather.23.cloned.1.call-start = ((), (), s32[]{:S(2)}) async-start(), calls=%async_computation.25 | async-start | bytes 3932160 | tf_op jit(solution)/shard_map/all_gather | solution.py:778
  265.2 45.9 %all-to-all-start.4 = ((bf16[8,48,1152]{2,1,0:T(8,128)(2,1)}), bf16[8,48,1152]{2,1,0:T(8,128)(2,1)}, u32[]{:S(2)}, u32[]{:S(2)}) async-start(bf16[8,48,1152]{2,1,0:T(8,128)(2,1)} %bitcast.58), calls=%async_computation.4 | async-start | bytes 1769472 | tf_op jit(solution)/shard_map/all_to_all | solution.py:747
  269.5 88.9 %all-gather.25.cloned.1.call-start = ((), (), s32[]{:S(2)}) async-start(), calls=%async_computation.26 | async-start | bytes 1966080 | tf_op jit(solution)/shard_map/all_gather | solution.py:778
  269.6 32.6 %collective-permute-start.21 = (bf16[2,64,1536]{2,1,0:T(8,128)(2,1)S(1)}, bf16[2,64,1536]{2,1,0:T(8,128)(2,1)S(1)}, u32[]{:S(2)}, u32[]{:S(2)}) collective-permute-start(bf16[2,64,1536]{2,1,0:T(8,128)(2,1)S(1)} %get-tuple-element.406), channel_id=1, source_target_pairs={{0,2},{2,0},{1,3},{3,1},{4,6},{6,4},{5,7},{7,5},{8,10},{10,8},{9,1... | collective-permute-start | bytes 1179656 | tf_op jit(solution)/shard_map/ppermute | solution.py:717
  278.2 31.3 %collective-permute-start.23 = (bf16[2,64,1536]{2,1,0:T(8,128)(2,1)S(1)}, bf16[2,64,1536]{2,1,0:T(8,128)(2,1)}, u32[]{:S(2)}, u32[]{:S(2)}) collective-permute-start(bf16[2,64,1536]{2,1,0:T(8,128)(2,1)S(1)} %fusion.49), channel_id=1, source_target_pairs={{0,4},{4,0},{1,5},{5,1},{2,6},{6,2},{3,7},{7,3},{8,12},{12,8},{9,1... | collective-permute-start | bytes 1179656 | tf_op jit(solution)/shard_map/ppermute | solution.py:717
  278.3 144.7 %all-gather.29.cloned.1.call-start = ((), (), s32[]{:S(2)}) async-start(), calls=%async_computation.28 | async-start | bytes 2703360 | tf_op jit(solution)/shard_map/all_gather | solution.py:778
  345.6 103.5 %all-gather.27.cloned.1.call-start = ((), (), s32[]{:S(2)}) async-start(), calls=%async_computation.27 | async-start | bytes 4423680 | tf_op jit(solution)/shard_map/all_gather | solution.py:778
  377.8 43.5 %all-to-all-start.5 = ((bf16[8,48,1024]{2,1,0:T(8,128)(2,1)}), bf16[8,48,1024]{2,1,0:T(8,128)(2,1)}, u32[]{:S(2)}, u32[]{:S(2)}) async-start(bf16[8,48,1024]{2,1,0:T(8,128)(2,1)} %reshape.599), calls=%async_computation.5 | async-start | bytes 1572864 | tf_op jit(solution)/shard_map/all_to_all | solution.py:747
  382.1 169.1 %all-gather.31.cloned.1.call-start = ((), (), s32[]{:S(2)}) async-start(), calls=%async_computation.29 | async-start | bytes 3932160 | tf_op jit(solution)/shard_map/all_gather | solution.py:778
  385.8 34.1 %collective-permute-start.31 = (bf16[2,64,1536]{2,1,0:T(8,128)(2,1)S(1)}, bf16[2,64,1536]{2,1,0:T(8,128)(2,1)}, u32[]{:S(2)}, u32[]{:S(2)}) collective-permute-start(bf16[2,64,1536]{2,1,0:T(8,128)(2,1)S(1)} %fusion.44), channel_id=1, source_target_pairs={{0,4},{4,0},{1,5},{5,1},{2,6},{6,2},{3,7},{7,3},{8,12},{12,8},{9,1... | collective-permute-start | bytes 1179656 | tf_op jit(solution)/shard_map/ppermute | solution.py:717
  449.0 295.5 %reduce-scatter.28.cloned.1.call-start = ((), (), s32[]{:S(2)}) async-start(), calls=%async_computation.30 | async-start | bytes 3932160
  462.4 30.1 %collective-permute-start.50 = (bf16[2,64,1536]{2,1,0:T(8,128)(2,1)S(1)}, bf16[2,64,1536]{2,1,0:T(8,128)(2,1)S(1)}, u32[]{:S(2)}, u32[]{:S(2)}) collective-permute-start(bf16[2,64,1536]{2,1,0:T(8,128)(2,1)S(1)} %slice.572), channel_id=1, source_target_pairs={{0,4},{4,0},{1,5},{5,1},{2,6},{6,2},{3,7},{7,3},{8,12},{12,8},{9,1... | collective-permute-start | bytes 1179656 | tf_op jit(solution)/shard_map/ppermute | solution.py:717
  462.9 48.6 %collective-permute-start.49 = (bf16[2,64,1536]{2,1,0:T(8,128)(2,1)S(1)}, bf16[2,64,1536]{2,1,0:T(8,128)(2,1)S(1)}, u32[]{:S(2)}, u32[]{:S(2)}) collective-permute-start(bf16[2,64,1536]{2,1,0:T(8,128)(2,1)S(1)} %slice.572), channel_id=1, source_target_pairs={{0,2},{2,0},{1,3},{3,1},{4,6},{6,4},{5,7},{7,5},{8,10},{10,8},{9,1... | collective-permute-start | bytes 1179656 | tf_op jit(solution)/shard_map/ppermute | solution.py:717
  516.0 32.1 %collective-permute-start.52 = (bf16[4,2,64,1536]{3,2,1,0:T(8,128)(2,1)S(1)}, bf16[4,2,64,1536]{3,2,1,0:T(8,128)(2,1)S(1)}, u32[]{:S(2)}, u32[]{:S(2)}) collective-permute-start(bf16[4,2,64,1536]{3,2,1,0:T(8,128)(2,1)S(1)} %pad_maximum_fusion.9), channel_id=1, source_target_pairs={{0,8},{8,0},{1,9},{9,1},{2,10},{10,2},{3,11},{11,3},{4,12},{12,4},... | collective-permute-start | bytes 4718600 | tf_op jit(solution)/shard_map/ppermute | solution.py:717
  577.5 201.0 %reduce-scatter.30.cloned.1.call-start = ((), (), s32[]{:S(2)}) async-start(), calls=%async_computation.31 | async-start | bytes 1966080
  626.0 230.3 %reduce-scatter.34.cloned.1.call-start = ((), (), s32[]{:S(2)}) async-start(), calls=%async_computation.33 | async-start | bytes 737280
  626.0 115.6 %collective-permute-start.46 = (bf16[2,64,1536]{2,1,0:T(8,128)(2,1)}, bf16[2,64,1536]{2,1,0:T(8,128)(2,1)}, u32[]{:S(2)}, u32[]{:S(2)}) collective-permute-start(bf16[2,64,1536]{2,1,0:T(8,128)(2,1)} %get-tuple-element.396), channel_id=1, source_target_pairs={{0,2},{2,0},{1,3},{3,1},{4,6},{6,4},{5,7},{7,5},{8,10},{10,8},{9,1... | collective-permute-start | bytes 1179656 | tf_op jit(solution)/shard_map/ppermute | solution.py:717
  626.6 39.2 %collective-permute-start.58 = (bf16[2,64,1536]{2,1,0:T(8,128)(2,1)}, bf16[2,64,1536]{2,1,0:T(8,128)(2,1)S(1)}, u32[]{:S(2)}, u32[]{:S(2)}) collective-permute-start(bf16[2,64,1536]{2,1,0:T(8,128)(2,1)} %get-tuple-element.431), channel_id=1, source_target_pairs={{0,2},{2,0},{1,3},{3,1},{4,6},{6,4},{5,7},{7,5},{8,10},{10,8},{9,1... | collective-permute-start | bytes 1179656 | tf_op jit(solution)/shard_map/ppermute | solution.py:717
  642.2 31.6 %collective-permute-start.60 = (bf16[2,64,1536]{2,1,0:T(8,128)(2,1)}, bf16[2,64,1536]{2,1,0:T(8,128)(2,1)S(1)}, u32[]{:S(2)}, u32[]{:S(2)}) collective-permute-start(bf16[2,64,1536]{2,1,0:T(8,128)(2,1)} %collective-permute-done.59), channel_id=1, source_target_pairs={{0,2},{2,0},{1,3},{3,1},{4,6},{6,4},{5,7},{7,5},{8,10},{10,8},{9,1... | collective-permute-start | bytes 1179656 | tf_op jit(solution)/shard_map/ppermute | solution.py:717
  644.2 97.3 %collective-permute-start.48 = (bf16[2,64,1536]{2,1,0:T(8,128)(2,1)}, bf16[2,64,1536]{2,1,0:T(8,128)(2,1)}, u32[]{:S(2)}, u32[]{:S(2)}) collective-permute-start(bf16[2,64,1536]{2,1,0:T(8,128)(2,1)} %fusion.38), channel_id=1, source_target_pairs={{0,4},{4,0},{1,5},{5,1},{2,6},{6,2},{3,7},{7,3},{8,12},{12,8},{9,1... | collective-permute-start | bytes 1179656 | tf_op jit(solution)/shard_map/ppermute | solution.py:717
  715.4 140.9 %reduce-scatter.32.cloned.1.call-start = ((), (), s32[]{:S(2)}) async-start(), calls=%async_computation.32 | async-start | bytes 4423680
  738.5 210.7 %reduce-scatter.38.cloned.1.call-start = ((), (), s32[]{:S(2)}) async-start(), calls=%async_computation.35 | async-start | bytes 1966080
  800.3 197.2 %reduce-scatter.36.cloned.1.call-start = ((), (), s32[]{:S(2)}) async-start(), calls=%async_computation.34 | async-start | bytes 3932160
  824.0 34.4 %collective-permute-start.62 = (bf16[2,2,2,64,384]{4,3,2,1,0:T(8,128)(2,1)}, bf16[2,2,2,64,384]{4,3,2,1,0:T(8,128)(2,1)}, u32[]{:S(2)}, u32[]{:S(2)}) collective-permute-start(bf16[2,2,2,64,384]{4,3,2,1,0:T(8,128)(2,1)} %fusion.61), channel_id=1, source_target_pairs={{0,2},{2,0},{1,3},{3,1},{4,6},{6,4},{5,7},{7,5},{8,10},{10,8},{9,1... | collective-permute-start | bytes 1179656 | tf_op jit(solution)/shard_map/ppermute | solution.py:717
  878.0 41.6 %all-to-all-start.6 = ((bf16[8,256,384]{2,1,0:T(8,128)(2,1)}), bf16[8,256,384]{2,1,0:T(8,128)(2,1)S(1)}, u32[]{:S(2)}, u32[]{:S(2)}) async-start(bf16[8,256,384]{2,1,0:T(8,128)(2,1)} %get-tuple-element.140), calls=%async_computation.6 | async-start | bytes 3145728 | tf_op jit(solution)/shard_map/all_to_all | solution.py:747
  923.9 126.2 %reduce-scatter.42.cloned.1.call-start = ((), (), s32[]{:S(2)}) async-start(), calls=%async_computation.37 | async-start | bytes 1474560
  944.8 52.7 %all-to-all-start.8 = ((bf16[8,256,384]{2,1,0:T(8,128)(2,1)}), bf16[8,256,384]{2,1,0:T(8,128)(2,1)}, u32[]{:S(2)}, u32[]{:S(2)}) async-start(bf16[8,256,384]{2,1,0:T(8,128)(2,1)} %copy-done.17), calls=%async_computation.8 | async-start | bytes 3145728 | tf_op jit(solution)/shard_map/all_to_all | solution.py:747
  949.1 101.0 %reduce-scatter.40.cloned.1.call-start = ((), (), s32[]{:S(2)}) async-start(), calls=%async_computation.36 | async-start | bytes 1474560
  954.1 52.0 %collective-permute-start.91 = (bf16[2,256,1536]{2,1,0:T(8,128)(2,1)}, bf16[2,256,1536]{2,1,0:T(8,128)(2,1)}, u32[]{:S(2)}, u32[]{:S(2)}) collective-permute-start(bf16[2,256,1536]{2,1,0:T(8,128)(2,1)} %pad_maximum_fusion.13), channel_id=1, source_target_pairs={{1,8},{3,10},{5,12},{7,14},{8,1},{10,3},{12,5},{14,7},{17,24},{19,... | collective-permute-start | bytes 4718600 | tf_op jit(solution)/shard_map/ppermute | solution.py:713
  1007.7 42.4 %all-to-all-start.9 = ((bf16[8,48,1152]{2,1,0:T(8,128)(2,1)}), bf16[8,48,1152]{2,1,0:T(8,128)(2,1)}, u32[]{:S(2)}, u32[]{:S(2)}) async-start(bf16[8,48,1152]{2,1,0:T(8,128)(2,1)} %bitcast.680), calls=%async_computation.9 | async-start | bytes 1769472 | tf_op jit(solution)/shard_map/all_to_all | solution.py:747
  1013.7 114.2 %reduce-scatter.44.cloned.1.call-start = ((), (), s32[]{:S(2)}) async-start(), calls=%async_computation.38 | async-start | bytes 1474560
  1042.6 37.4 %collective-permute-start.97 = (bf16[2,256,1536]{2,1,0:T(8,128)(2,1)}, bf16[2,256,1536]{2,1,0:T(8,128)(2,1)}, u32[]{:S(2)}, u32[]{:S(2)}) collective-permute-start(bf16[2,256,1536]{2,1,0:T(8,128)(2,1)} %pad_maximum_fusion.14), channel_id=1, source_target_pairs={{1,8},{3,10},{5,12},{7,14},{8,1},{10,3},{12,5},{14,7},{17,24},{19,... | collective-permute-start | bytes 4718600 | tf_op jit(solution)/shard_map/ppermute | solution.py:713
  1062.8 100.6 %collective-permute-start.108 = (bf16[144,1536]{1,0:T(8,128)(2,1)}, bf16[144,1536]{1,0:T(8,128)(2,1)}, u32[]{:S(2)}, u32[]{:S(2)}) collective-permute-start(bf16[144,1536]{1,0:T(8,128)(2,1)} %constant_dynamic-update-slice_fusion.42), channel_id=1, source_target_pairs={{16,2},{17,3},{8,4},{9,5},{24,6},{25,7},{2,8},{3,9},{18,10},{19,11... | collective-permute-start | bytes 1327112 | tf_op jit(solution)/shard_map/ppermute | solution.py:833
  1069.1 59.3 %all-to-all-start.11 = ((bf16[8,48,384]{2,1,0:T(8,128)(2,1)}), bf16[8,48,384]{2,1,0:T(8,128)(2,1)S(1)}, u32[]{:S(2)}, u32[]{:S(2)}) async-start(bf16[8,48,384]{2,1,0:T(8,128)(2,1)} %bitcast.691), calls=%async_computation.11 | async-start | bytes 589824 | tf_op jit(solution)/shard_map/all_to_all | solution.py:747
  1128.3 31.6 %all-to-all-start.12 = ((bf16[8,48,1024]{2,1,0:T(8,128)(2,1)}), bf16[8,48,1024]{2,1,0:T(8,128)(2,1)S(1)}, u32[]{:S(2)}, u32[]{:S(2)}) async-start(bf16[8,48,1024]{2,1,0:T(8,128)(2,1)} %bitcast.682), calls=%async_computation.12 | async-start | bytes 1572864 | tf_op jit(solution)/shard_map/all_to_all | solution.py:747
  1137.4 37.4 %collective-permute-start.96 = (f32[2,64,1536]{2,1,0:T(8,128)}, f32[2,64,1536]{2,1,0:T(8,128)S(1)}, u32[]{:S(2)}, u32[]{:S(2)}) collective-permute-start(f32[2,64,1536]{2,1,0:T(8,128)} %fusion.20), channel_id=1, source_target_pairs={{1,8},{3,10},{5,12},{7,14},{8,1},{10,3},{12,5},{14,7},{17,24},{19,... | collective-permute-start | bytes 2359304 | tf_op jit(solution)/shard_map/ppermute | solution.py:713
  (280 other events, 3954.3 us)
Sparse Core Ops, SparseCore 0:
  64.6 30.0 all-gather.16
  187.4 26.4 all-gather.18
  216.3 27.7 all-gather.20
  245.7 43.9 all-gather.22
  291.4 30.9 all-gather.24
  345.7 34.6 all-gather.28
  382.2 47.2 all-gather.26
  449.2 43.4 all-gather.30
  577.6 42.5 reduce-scatter.27
  626.1 28.8 reduce-scatter.29
  715.5 23.6 reduce-scatter.33
  742.4 47.2 reduce-scatter.31
  800.5 29.1 reduce-scatter.37
  835.7 42.6 reduce-scatter.35
  931.2 29.4 reduce-scatter.41
  963.7 31.7 reduce-scatter.39
  1061.5 39.5 reduce-scatter.43

commit v4 on v3

--- a/solution.py
+++ b/solution.py
@@ -1607,11 +1607,8 @@
     grad_whole = gather_plane(grad.astype(BF)).reshape(-1, wide)
     grad_whole, back_keys = settle(grad_whole, back_keys)
     back_keys = cache_back(back_keys)
-    second_got = trade(tie(second_columns, grad_whole), PLANE)
     grad_gated = dot(grad_whole, own_out, 1, 1).reshape(mixed.shape)
     grad_core = grad_gated * jax.nn.silu(gate)
-    grad_core, second_got = settle(grad_core, second_got)
-    second_gate_up_grad = hidden_back(second_got)
     back_contents = trade(tie(back_contents, grad_core), PLANE)
     grad_gate = (grad_gated * mixed_out * silu_slope(gate)).astype(BF).reshape(-1, width)
     skip_grad = jnp.sum(grad_core * mixed, axis=(0, 1, 2))
@@ -1626,6 +1623,7 @@
         grad_step, back_contents, first_columns, first_down_grad
     )
     back_contents = cache_back(back_contents)
+    second_gate_up_grad = hidden_back(trade(tie(second_columns, grad_step), PLANE))
     got = trade(tie(qkv_columns, grad_step), PLANE)
     grad_pre = grad_step * valid * jax.nn.sigmoid(pre)
     step_bias_grad = jnp.sum(grad_pre, axis=(0, 1, 2))

time: 1200 us -> 1200 us (level)
  waiting for transfers between devices: 546 us -> 561 us
    unnamed x413 -> x389, local copies, waits for them, and re-layouts: 42.7 us -> 35.4 us
  transfers between devices with their start and end apart: 139 -> 139, of which waited for: 67 -> 70; matrix products, arithmetic and copies ran while one was open for 26% -> 25% of each run, Pallas kernels for 7% -> 7%
where the time goes in v4:
time: 1200 us; the launch traced here: 1180 us
  waiting for transfers between devices  561 us (47%)
  starting transfers between devices  180 us (15%)
  local copies, waits for them, and re-layouts  127 us (11%)
  other arithmetic  118 us (10%)
  matrix products  98.9 us (8%)
  Pallas kernels  81.6 us (7%)
  between operations  17.7 us (1%)
    ppermute x90, waiting for transfers between devices, other(): return lax.ppermute(block, axis, [(0, 1), (1, 0)])  496 us
    dot_general x33, matrix products, dot(): lax.dot_general(left, right, (((left_dim,), (right_dim,)), ((), ())), pre...  98.9 us
    ppermute x90, starting transfers between devices, other(): return lax.ppermute(block, axis, [(0, 1), (1, 0)])  94.3 us
    all_to_all x13, starting transfers between devices, trade(): return lax.all_to_all(block, axes, 0, 0, tiled=True)  58.2 us
    all_to_all x13, waiting for transfers between devices, trade(): return lax.all_to_all(block, axes, 0, 0, tiled=True)  44.1 us
    unnamed x389, local copies, waits for them, and re-layouts  35.4 us
    pallas_call x1, Pallas kernels, scan_back(): pl.pallas_call(scan_back_body, grid_spec=pltpu.PrefetchScalarGridSpec(num...  24.7 us
  transfers between devices with their start and end apart: 139, of which 70 were waited for; matrix products, arithmetic and copies ran while one was open for 25% of the time, Pallas kernels for 7%

profile of v4, /device:TPU:0, one launch (start us, length us, event | category | flops | bytes accessed | tf_op | source)
XLA Modules:
  0.0 1183.5 jit_solution(7391948935914485176)
XLA Ops:
  10.5 6.3 all-to-all-start
  46.0 6.2 collective-permute-start.7
  68.3 20.0 %collective-permute-done.2 = bf16[2,64,1536]{2,1,0:T(8,128)(2,1)S(1)} collective-permute-done((bf16[2,64,1536]{2,1,0:T(8,128)(2,1)S(1)}, bf16[2,64,1536]{2,1,0:T(8,128)(2,1)S(1)}, u32[]{:S(2)}, u32[]{:S(2)}) %collective-permute-start.2) | collective-permute-done | bytes 393248 | tf_op jit(solution)/shard_map/ppermute | solution.py:717
  88.3 14.4 %collective-permute-done.1 = bf16[2,64,1536]{2,1,0:T(8,128)(2,1)S(1)} collective-permute-done((bf16[2,64,1536]{2,1,0:T(8,128)(2,1)S(1)}, bf16[2,64,1536]{2,1,0:T(8,128)(2,1)S(1)}, u32[]{:S(2)}, u32[]{:S(2)}) %collective-permute-start.1) | collective-permute-done | bytes 393248 | tf_op jit(solution)/shard_map/ppermute | solution.py:717
  132.0 9.2 all-to-all-done.1
  147.2 25.7 %collective-permute-done.10 = f32[2,64,128]{2,1,0:T(8,128)S(1)} collective-permute-done((f32[2,64,128]{2,1,0:T(8,128)S(1)}, f32[2,64,128]{2,1,0:T(8,128)S(1)}, u32[]{:S(2)}, u32[]{:S(2)}) %collective-permute-start.10) | collective-permute-done | bytes 65568 | tf_op jit(solution)/shard_map/ppermute | solution.py:717
  178.0 7.6 collective-permute-done.11
  226.9 13.9 %scan_forward.1 = (f32[8,2,64,384]{3,2,1,0:T(8,128)S(1)}, f32[8,2,64,16,384]{4,3,2,1,0:T(8,128)}, f32[2,16,384]{2,1,0:T(8,128)S(1)}) custom-call(s32[8]{0:T(128)S(1)} %shift-right-arithmetic_or_fusion.order, f32[8,2,64,384]{3,2,1,0:T(8,128)S(1)} %copy-done.7, f32[8,2,64,384]{3,2,1,0:T(8,128)S(1)} %copy-done.9, ...), custom_call_target="tpu_custom_call" | custom-call | tf_op jit(solution)/shard_map/scan_forward/pallas_call | solution.py:998
  248.6 6.4 multiply_convert_fusion.8
  280.2 23.8 %collective-permute-done.21 = bf16[2,64,1536]{2,1,0:T(8,128)(2,1)S(1)} collective-permute-done((bf16[2,64,1536]{2,1,0:T(8,128)(2,1)S(1)}, bf16[2,64,1536]{2,1,0:T(8,128)(2,1)S(1)}, u32[]{:S(2)}, u32[]{:S(2)}) %collective-permute-start.21) | collective-permute-done | bytes 393248 | tf_op jit(solution)/shard_map/ppermute | solution.py:717
  304.0 7.1 collective-permute-done.23
  316.9 16.9 %collective-permute-done.25 = bf16[2,64,1536]{2,1,0:T(8,128)(2,1)S(1)} collective-permute-done((bf16[2,64,1536]{2,1,0:T(8,128)(2,1)S(1)}, bf16[2,64,1536]{2,1,0:T(8,128)(2,1)S(1)}, u32[]{:S(2)}, u32[]{:S(2)}) %collective-permute-start.25) | collective-permute-done | bytes 393248 | tf_op jit(solution)/shard_map/ppermute | solution.py:717
  334.0 10.7 collective-permute-done.26
  389.9 23.8 %collective-permute-done.29 = bf16[2,64,1536]{2,1,0:T(8,128)(2,1)S(1)} collective-permute-done((bf16[2,64,1536]{2,1,0:T(8,128)(2,1)}, bf16[2,64,1536]{2,1,0:T(8,128)(2,1)S(1)}, u32[]{:S(2)}, u32[]{:S(2)}) %collective-permute-start.29) | collective-permute-done | bytes 393248 | tf_op jit(solution)/shard_map/ppermute | solution.py:717
  413.7 8.4 collective-permute-done.31
  436.6 13.0 %collective-permute-done.34 = bf16[2,64,1536]{2,1,0:T(8,128)(2,1)} collective-permute-done((bf16[2,64,1536]{2,1,0:T(8,128)(2,1)}, bf16[2,64,1536]{2,1,0:T(8,128)(2,1)}, u32[]{:S(2)}, u32[]{:S(2)}) %collective-permute-start.34) | collective-permute-done | bytes 393248 | tf_op jit(solution)/shard_map/ppermute | solution.py:717
  456.1 6.9 collective-permute-done.35
  469.7 10.4 attend.1
  483.5 11.7 collective-permute-done.38
  498.5 9.7 collective-permute-done.37
  508.2 7.7 collective-permute-done.39
  523.0 16.0 %collective-permute-done.42 = bf16[2,64,1536]{2,1,0:T(8,128)(2,1)S(1)} collective-permute-done((bf16[2,64,1536]{2,1,0:T(8,128)(2,1)S(1)}, bf16[2,64,1536]{2,1,0:T(8,128)(2,1)S(1)}, u32[]{:S(2)}, u32[]{:S(2)}) %collective-permute-start.42) | collective-permute-done | bytes 393248 | tf_op jit(solution)/shard_map/ppermute | solution.py:717
  541.5 8.5 collective-permute-done.43
  573.4 6.5 convolution_convert_fusion.6
  591.6 10.0 collective-permute-done.55
  604.5 10.4 collective-permute-done.54
  632.8 13.4 %collective-permute-done.59 = bf16[2,64,1536]{2,1,0:T(8,128)(2,1)} collective-permute-done((bf16[2,64,1536]{2,1,0:T(8,128)(2,1)}, bf16[2,64,1536]{2,1,0:T(8,128)(2,1)}, u32[]{:S(2)}, u32[]{:S(2)}) %collective-permute-start.59) | collective-permute-done | bytes 393248 | tf_op jit(solution)/shard_map/ppermute | solution.py:717
  651.2 18.4 %collective-permute-done.58 = bf16[2,64,1536]{2,1,0:T(8,128)(2,1)S(1)} collective-permute-done((bf16[2,64,1536]{2,1,0:T(8,128)(2,1)}, bf16[2,64,1536]{2,1,0:T(8,128)(2,1)S(1)}, u32[]{:S(2)}, u32[]{:S(2)}) %collective-permute-start.58) | collective-permute-done | bytes 393248 | tf_op jit(solution)/shard_map/ppermute | solution.py:717
  669.6 8.0 collective-permute-done.60
  680.1 21.8 %attend_back.1 = (bf16[8,256,384]{2,1,0:T(8,128)(2,1)}, bf16[8,256,384]{2,1,0:T(8,128)(2,1)S(1)}, bf16[512,384]{1,0:T(8,128)(2,1)S(1)}, bf16[512,384]{1,0:T(8,128)(2,1)S(1)}, bf16[512,384]{1,0:T(8,128)(2,1)S(1)}) custom-call(s32[2]{0:T(128)S(1)} %pad_add_fusion.meta_ref, bf16[512,1152]{1,0:T(8,128)(2,1)S(1)} %convolution_convert_fusion.9.q_ref.k_ref.v_ref, ...), custom_call_target="tpu_custom_call" | custom-call | tf_op jit(solution)/shard_map/attend_back/pallas_call | solution.py:1304
  708.4 8.8 collective-permute-done.66
  720.0 10.1 collective-permute-done.65
  730.1 6.2 collective-permute-done.67
  755.2 25.8 %collective-permute-done.70 = bf16[2,64,1536]{2,1,0:T(8,128)(2,1)} collective-permute-done((bf16[2,64,1536]{2,1,0:T(8,128)(2,1)}, bf16[2,64,1536]{2,1,0:T(8,128)(2,1)}, u32[]{:S(2)}, u32[]{:S(2)}) %collective-permute-start.70) | collective-permute-done | bytes 393248 | tf_op jit(solution)/shard_map/ppermute | solution.py:717
  783.1 14.7 %collective-permute-done.71 = bf16[2,64,1536]{2,1,0:T(8,128)(2,1)S(1)} collective-permute-done((bf16[2,64,1536]{2,1,0:T(8,128)(2,1)}, bf16[2,64,1536]{2,1,0:T(8,128)(2,1)S(1)}, u32[]{:S(2)}, u32[]{:S(2)}) %collective-permute-start.71) | collective-permute-done | bytes 393248 | tf_op jit(solution)/shard_map/ppermute | solution.py:717
  832.3 6.7 collective-permute-done.75
  852.2 7.2 collective-permute-done.76
  866.5 15.4 %collective-permute-done.79 = bf16[2,64,1536]{2,1,0:T(8,128)(2,1)S(1)} collective-permute-done((bf16[2,64,1536]{2,1,0:T(8,128)(2,1)S(1)}, bf16[2,64,1536]{2,1,0:T(8,128)(2,1)S(1)}, u32[]{:S(2)}, u32[]{:S(2)}) %collective-permute-start.79) | collective-permute-done | bytes 393248 | tf_op jit(solution)/shard_map/ppermute | solution.py:717
  888.2 6.8 collective-permute-done.80
  901.6 24.4 %all-to-all-done.6 = bf16[8,256,384]{2,1,0:T(8,128)(2,1)} async-done(((bf16[8,256,384]{2,1,0:T(8,128)(2,1)}), bf16[8,256,384]{2,1,0:T(8,128)(2,1)}, u32[]{:S(2)}, u32[]{:S(2)}) %all-to-all-start.6) | async-done | bytes 1572896 | tf_op jit(solution)/shard_map/all_to_all | solution.py:747
  926.0 6.4 multiply_reduce_fusion.1
  948.3 24.7 %scan_back.1 = (f32[8,2,64,384]{3,2,1,0:T(8,128)S(1)}, f32[8,2,64,384]{3,2,1,0:T(8,128)S(1)}, bf16[8,2,64,16,128]{4,3,2,1,0:T(8,128)(2,1)S(1)}, bf16[8,2,64,16,1...) custom-call(s32[8]{0:T(128)S(1)} %copy-done.28, f32[8,2,64,384]{3,2,1,0:T(8,128)S(1)} %copy-done.8, ...), custom_call_target="tpu_custom_call" | custom-call | tf_op jit(solution)/shard_map/scan_back/pallas_call | solution.py:1123
  984.7 8.2 all-to-all-start.12
  1032.1 12.3 %collective-permute-done.88 = bf16[2,64,128]{2,1,0:T(8,128)(2,1)S(1)} collective-permute-done((bf16[2,64,128]{2,1,0:T(8,128)(2,1)S(1)}, bf16[2,64,128]{2,1,0:T(8,128)(2,1)S(1)}, u32[]{:S(2)}, u32[]{:S(2)}) %collective-permute-start.88) | collective-permute-done | bytes 32800 | tf_op jit(solution)/shard_map/ppermute | solution.py:717
  1078.3 7.3 collective-permute-done.105
  1103.4 11.1 collective-permute-done.94
  1120.4 7.8 collective-permute-done.95
  1139.7 16.5 %collective-permute-done.100 = f32[4,1536]{1,0:T(4,128)S(1)} collective-permute-done((f32[4,1536]{1,0:T(4,128)S(1)}, f32[4,1536]{1,0:T(4,128)S(1)}, u32[]{:S(2)}, u32[]{:S(2)}) %collective-permute-start.100) | collective-permute-done | bytes 24608 | tf_op jit(solution)/shard_map/ppermute | solution.py:760
  (934 shorter events, 572.7 us)
Async XLA Ops:
  10.5 47.1 %all-to-all-start = ((bf16[8,48,896]{2,1,0:T(8,128)(2,1)}), bf16[8,48,896]{2,1,0:T(8,128)(2,1)}, u32[]{:S(2)}, u32[]{:S(2)}) async-start(bf16[8,48,896]{2,1,0:T(8,128)(2,1)} %pad_maximum_fusion.22), calls=%async_computation | async-start | bytes 1376256 | tf_op jit(solution)/shard_map/all_to_all | solution.py:747
  16.8 96.4 %all-gather.17.cloned.1.call-start = ((), (), s32[]{:S(2)}) async-start(), calls=%async_computation.22 | async-start | bytes 1966080 | tf_op jit(solution)/shard_map/all_gather | solution.py:778
  52.2 55.2 %collective-permute-start.16 = (bf16[2,256,1536]{2,1,0:T(8,128)(2,1)S(1)}, bf16[2,256,1536]{2,1,0:T(8,128)(2,1)}, u32[]{:S(2)}, u32[]{:S(2)}) collective-permute-start(bf16[2,256,1536]{2,1,0:T(8,128)(2,1)S(1)} %get-tuple-element.105), channel_id=1, source_target_pairs={{1,8},{3,10},{5,12},{7,14},{8,1},{10,3},{12,5},{14,7},{17,24},{19,... | collective-permute-start | bytes 4718600 | tf_op jit(solution)/shard_map/ppermute | solution.py:713
  60.0 87.0 %collective-permute-start.18 = (f32[2,24,384]{2,1,0:T(8,128)S(1)}, f32[2,24,384]{2,1,0:T(8,128)}, u32[]{:S(2)}, u32[]{:S(2)}) collective-permute-start(f32[2,24,384]{2,1,0:T(8,128)S(1)} %copy-done.109), channel_id=1, source_target_pairs={{1,8},{3,10},{5,12},{7,14},{8,1},{10,3},{12,5},{14,7},{17,24},{19,... | collective-permute-start | bytes 221192 | tf_op jit(solution)/shard_map/ppermute | solution.py:713
  61.3 149.5 %collective-permute-start.19 = (bf16[144,1536]{1,0:T(8,128)(2,1)}, bf16[144,1536]{1,0:T(8,128)(2,1)}, u32[]{:S(2)}, u32[]{:S(2)}) collective-permute-start(bf16[144,1536]{1,0:T(8,128)(2,1)} %pad_maximum_fusion.25), channel_id=1, source_target_pairs={{2,16},{3,17},{4,8},{5,9},{6,24},{7,25},{8,2},{9,3},{10,18},{11,19... | collective-permute-start | bytes 1327112 | tf_op jit(solution)/shard_map/ppermute | solution.py:833
  62.8 39.9 %collective-permute-start.1 = (bf16[2,64,1536]{2,1,0:T(8,128)(2,1)S(1)}, bf16[2,64,1536]{2,1,0:T(8,128)(2,1)S(1)}, u32[]{:S(2)}, u32[]{:S(2)}) collective-permute-start(bf16[2,64,1536]{2,1,0:T(8,128)(2,1)S(1)} %get-tuple-element.100), channel_id=1, source_target_pairs={{0,2},{2,0},{1,3},{3,1},{4,6},{6,4},{5,7},{7,5},{8,10},{10,8},{9,1... | collective-permute-start | bytes 1179656 | tf_op jit(solution)/shard_map/ppermute | solution.py:717
  130.0 67.6 %collective-permute-start.17 = (bf16[2,320,1536]{2,1,0:T(8,128)(2,1)}, bf16[2,320,1536]{2,1,0:T(8,128)(2,1)}, u32[]{:S(2)}, u32[]{:S(2)}) collective-permute-start(bf16[2,320,1536]{2,1,0:T(8,128)(2,1)} %pad_maximum_fusion.2), channel_id=1, source_target_pairs={{1,8},{3,10},{5,12},{7,14},{8,1},{10,3},{12,5},{14,7},{17,24},{19,... | collective-permute-start | bytes 5898248 | tf_op jit(solution)/shard_map/ppermute | solution.py:713
  141.2 59.6 %all-to-all-start.2 = ((bf16[8,256,384]{2,1,0:T(8,128)(2,1)}), bf16[8,256,384]{2,1,0:T(8,128)(2,1)S(1)}, u32[]{:S(2)}, u32[]{:S(2)}) async-start(bf16[8,256,384]{2,1,0:T(8,128)(2,1)} %pad_maximum_fusion.4), calls=%async_computation.2 | async-start | bytes 3145728 | tf_op jit(solution)/shard_map/all_to_all | solution.py:747
  145.0 72.6 %all-gather.19.cloned.1.call-start = ((), (), s32[]{:S(2)}) async-start(), calls=%async_computation.23 | async-start | bytes 1474560 | tf_op jit(solution)/shard_map/all_gather | solution.py:778
  206.2 42.3 %all-to-all-start.3 = ((bf16[8,256,384]{2,1,0:T(8,128)(2,1)}), bf16[8,256,384]{2,1,0:T(8,128)(2,1)}, u32[]{:S(2)}, u32[]{:S(2)}) async-start(bf16[8,256,384]{2,1,0:T(8,128)(2,1)} %pad_maximum_fusion.5), calls=%async_computation.3 | async-start | bytes 3145728 | tf_op jit(solution)/shard_map/all_to_all | solution.py:747
  210.7 44.3 %all-gather.21.cloned.1.call-start = ((), (), s32[]{:S(2)}) async-start(), calls=%async_computation.24 | async-start | bytes 1474560 | tf_op jit(solution)/shard_map/all_gather | solution.py:778
  213.0 135.2 %all-gather.23.cloned.1.call-start = ((), (), s32[]{:S(2)}) async-start(), calls=%async_computation.25 | async-start | bytes 3932160 | tf_op jit(solution)/shard_map/all_gather | solution.py:778
  267.0 45.4 %all-to-all-start.4 = ((bf16[8,48,1152]{2,1,0:T(8,128)(2,1)}), bf16[8,48,1152]{2,1,0:T(8,128)(2,1)}, u32[]{:S(2)}, u32[]{:S(2)}) async-start(bf16[8,48,1152]{2,1,0:T(8,128)(2,1)} %bitcast.619), calls=%async_computation.4 | async-start | bytes 1769472 | tf_op jit(solution)/shard_map/all_to_all | solution.py:747
  271.2 89.3 %all-gather.25.cloned.1.call-start = ((), (), s32[]{:S(2)}) async-start(), calls=%async_computation.26 | async-start | bytes 1966080 | tf_op jit(solution)/shard_map/all_gather | solution.py:778
  271.3 32.7 %collective-permute-start.21 = (bf16[2,64,1536]{2,1,0:T(8,128)(2,1)S(1)}, bf16[2,64,1536]{2,1,0:T(8,128)(2,1)S(1)}, u32[]{:S(2)}, u32[]{:S(2)}) collective-permute-start(bf16[2,64,1536]{2,1,0:T(8,128)(2,1)S(1)} %copy-done.106), channel_id=1, source_target_pairs={{0,2},{2,0},{1,3},{3,1},{4,6},{6,4},{5,7},{7,5},{8,10},{10,8},{9,1... | collective-permute-start | bytes 1179656 | tf_op jit(solution)/shard_map/ppermute | solution.py:717
  280.0 31.1 %collective-permute-start.23 = (bf16[2,64,1536]{2,1,0:T(8,128)(2,1)S(1)}, bf16[2,64,1536]{2,1,0:T(8,128)(2,1)S(1)}, u32[]{:S(2)}, u32[]{:S(2)}) collective-permute-start(bf16[2,64,1536]{2,1,0:T(8,128)(2,1)S(1)} %fusion.49), channel_id=1, source_target_pairs={{0,4},{4,0},{1,5},{5,1},{2,6},{6,2},{3,7},{7,3},{8,12},{12,8},{9,1... | collective-permute-start | bytes 1179656 | tf_op jit(solution)/shard_map/ppermute | solution.py:717
  280.1 145.2 %all-gather.29.cloned.1.call-start = ((), (), s32[]{:S(2)}) async-start(), calls=%async_computation.28 | async-start | bytes 2703360 | tf_op jit(solution)/shard_map/all_gather | solution.py:778
  347.7 106.0 %all-gather.27.cloned.1.call-start = ((), (), s32[]{:S(2)}) async-start(), calls=%async_computation.27 | async-start | bytes 4423680 | tf_op jit(solution)/shard_map/all_gather | solution.py:778
  380.1 43.5 %all-to-all-start.5 = ((bf16[8,48,1024]{2,1,0:T(8,128)(2,1)}), bf16[8,48,1024]{2,1,0:T(8,128)(2,1)}, u32[]{:S(2)}, u32[]{:S(2)}) async-start(bf16[8,48,1024]{2,1,0:T(8,128)(2,1)} %reshape.599), calls=%async_computation.5 | async-start | bytes 1572864 | tf_op jit(solution)/shard_map/all_to_all | solution.py:747
  384.3 171.4 %all-gather.31.cloned.1.call-start = ((), (), s32[]{:S(2)}) async-start(), calls=%async_computation.29 | async-start | bytes 3932160 | tf_op jit(solution)/shard_map/all_gather | solution.py:778
  387.8 34.3 %collective-permute-start.31 = (bf16[2,64,1536]{2,1,0:T(8,128)(2,1)S(1)}, bf16[2,64,1536]{2,1,0:T(8,128)(2,1)}, u32[]{:S(2)}, u32[]{:S(2)}) collective-permute-start(bf16[2,64,1536]{2,1,0:T(8,128)(2,1)S(1)} %fusion.44), channel_id=1, source_target_pairs={{0,4},{4,0},{1,5},{5,1},{2,6},{6,2},{3,7},{7,3},{8,12},{12,8},{9,1... | collective-permute-start | bytes 1179656 | tf_op jit(solution)/shard_map/ppermute | solution.py:717
  453.7 297.1 %reduce-scatter.28.cloned.1.call-start = ((), (), s32[]{:S(2)}) async-start(), calls=%async_computation.30 | async-start | bytes 3932160
  466.7 31.3 %collective-permute-start.50 = (bf16[2,64,1536]{2,1,0:T(8,128)(2,1)}, bf16[2,64,1536]{2,1,0:T(8,128)(2,1)S(1)}, u32[]{:S(2)}, u32[]{:S(2)}) collective-permute-start(bf16[2,64,1536]{2,1,0:T(8,128)(2,1)} %slice.572), channel_id=1, source_target_pairs={{0,4},{4,0},{1,5},{5,1},{2,6},{6,2},{3,7},{7,3},{8,12},{12,8},{9,1... | collective-permute-start | bytes 1179656 | tf_op jit(solution)/shard_map/ppermute | solution.py:717
  467.3 48.7 %collective-permute-start.49 = (bf16[2,64,1536]{2,1,0:T(8,128)(2,1)}, bf16[2,64,1536]{2,1,0:T(8,128)(2,1)S(1)}, u32[]{:S(2)}, u32[]{:S(2)}) collective-permute-start(bf16[2,64,1536]{2,1,0:T(8,128)(2,1)} %slice.572), channel_id=1, source_target_pairs={{0,2},{2,0},{1,3},{3,1},{4,6},{6,4},{5,7},{7,5},{8,10},{10,8},{9,1... | collective-permute-start | bytes 1179656 | tf_op jit(solution)/shard_map/ppermute | solution.py:717
  521.6 31.1 %collective-permute-start.52 = (bf16[4,2,64,1536]{3,2,1,0:T(8,128)(2,1)S(1)}, bf16[4,2,64,1536]{3,2,1,0:T(8,128)(2,1)S(1)}, u32[]{:S(2)}, u32[]{:S(2)}) collective-permute-start(bf16[4,2,64,1536]{3,2,1,0:T(8,128)(2,1)S(1)} %pad_maximum_fusion.9), channel_id=1, source_target_pairs={{0,8},{8,0},{1,9},{9,1},{2,10},{10,2},{3,11},{11,3},{4,12},{12,4},... | collective-permute-start | bytes 4718600 | tf_op jit(solution)/shard_map/ppermute | solution.py:717
  582.0 199.0 %reduce-scatter.30.cloned.1.call-start = ((), (), s32[]{:S(2)}) async-start(), calls=%async_computation.31 | async-start | bytes 1966080
  630.7 233.1 %reduce-scatter.34.cloned.1.call-start = ((), (), s32[]{:S(2)}) async-start(), calls=%async_computation.33 | async-start | bytes 737280
  630.7 117.3 %collective-permute-start.46 = (bf16[2,64,1536]{2,1,0:T(8,128)(2,1)}, bf16[2,64,1536]{2,1,0:T(8,128)(2,1)}, u32[]{:S(2)}, u32[]{:S(2)}) collective-permute-start(bf16[2,64,1536]{2,1,0:T(8,128)(2,1)} %get-tuple-element.391), channel_id=1, source_target_pairs={{0,2},{2,0},{1,3},{3,1},{4,6},{6,4},{5,7},{7,5},{8,10},{10,8},{9,1... | collective-permute-start | bytes 1179656 | tf_op jit(solution)/shard_map/ppermute | solution.py:717
  631.3 38.3 %collective-permute-start.58 = (bf16[2,64,1536]{2,1,0:T(8,128)(2,1)}, bf16[2,64,1536]{2,1,0:T(8,128)(2,1)S(1)}, u32[]{:S(2)}, u32[]{:S(2)}) collective-permute-start(bf16[2,64,1536]{2,1,0:T(8,128)(2,1)} %get-tuple-element.426), channel_id=1, source_target_pairs={{0,2},{2,0},{1,3},{3,1},{4,6},{6,4},{5,7},{7,5},{8,10},{10,8},{9,1... | collective-permute-start | bytes 1179656 | tf_op jit(solution)/shard_map/ppermute | solution.py:717
  646.2 31.5 %collective-permute-start.60 = (bf16[2,64,1536]{2,1,0:T(8,128)(2,1)}, bf16[2,64,1536]{2,1,0:T(8,128)(2,1)S(1)}, u32[]{:S(2)}, u32[]{:S(2)}) collective-permute-start(bf16[2,64,1536]{2,1,0:T(8,128)(2,1)} %collective-permute-done.59), channel_id=1, source_target_pairs={{0,2},{2,0},{1,3},{3,1},{4,6},{6,4},{5,7},{7,5},{8,10},{10,8},{9,1... | collective-permute-start | bytes 1179656 | tf_op jit(solution)/shard_map/ppermute | solution.py:717
  648.3 99.8 %collective-permute-start.48 = (bf16[2,64,1536]{2,1,0:T(8,128)(2,1)}, bf16[2,64,1536]{2,1,0:T(8,128)(2,1)}, u32[]{:S(2)}, u32[]{:S(2)}) collective-permute-start(bf16[2,64,1536]{2,1,0:T(8,128)(2,1)} %fusion.38), channel_id=1, source_target_pairs={{0,4},{4,0},{1,5},{5,1},{2,6},{6,2},{3,7},{7,3},{8,12},{12,8},{9,1... | collective-permute-start | bytes 1179656 | tf_op jit(solution)/shard_map/ppermute | solution.py:717
  719.9 143.9 %reduce-scatter.32.cloned.1.call-start = ((), (), s32[]{:S(2)}) async-start(), calls=%async_computation.32 | async-start | bytes 4423680
  744.4 197.0 %reduce-scatter.38.cloned.1.call-start = ((), (), s32[]{:S(2)}) async-start(), calls=%async_computation.35 | async-start | bytes 1966080
  752.2 47.1 %collective-permute-start.61 = (bf16[2,2,2,64,384]{4,3,2,1,0:T(8,128)(2,1)S(1)}, bf16[2,2,2,64,384]{4,3,2,1,0:T(8,128)(2,1)}, u32[]{:S(2)}, u32[]{:S(2)}) collective-permute-start(bf16[2,2,2,64,384]{4,3,2,1,0:T(8,128)(2,1)S(1)} %slice_bitcast_fusion.26), channel_id=1, source_target_pairs={{0,4},{4,0},{1,5},{5,1},{2,6},{6,2},{3,7},{7,3},{8,12},{12,8},{9,1... | collective-permute-start | bytes 1179656 | tf_op jit(solution)/shard_map/ppermute | solution.py:717
  818.9 165.8 %reduce-scatter.36.cloned.1.call-start = ((), (), s32[]{:S(2)}) async-start(), calls=%async_computation.34 | async-start | bytes 3932160
  829.8 65.5 %collective-permute-start.64 = (bf16[2,64,4608]{2,1,0:T(8,128)(2,1)}, bf16[2,64,4608]{2,1,0:T(8,128)(2,1)}, u32[]{:S(2)}, u32[]{:S(2)}) collective-permute-start(bf16[2,64,4608]{2,1,0:T(8,128)(2,1)} %pad_maximum_fusion.20), channel_id=1, source_target_pairs={{1,8},{3,10},{5,12},{7,14},{8,1},{10,3},{12,5},{14,7},{17,24},{19,... | collective-permute-start | bytes 3538952 | tf_op jit(solution)/shard_map/ppermute | solution.py:713
  883.9 42.1 %all-to-all-start.6 = ((bf16[8,256,384]{2,1,0:T(8,128)(2,1)}), bf16[8,256,384]{2,1,0:T(8,128)(2,1)}, u32[]{:S(2)}, u32[]{:S(2)}) async-start(bf16[8,256,384]{2,1,0:T(8,128)(2,1)} %get-tuple-element.138), calls=%async_computation.6 | async-start | bytes 3145728 | tf_op jit(solution)/shard_map/all_to_all | solution.py:747
  932.4 52.3 %all-to-all-start.7 = ((bf16[8,256,384]{2,1,0:T(8,128)(2,1)}), bf16[8,256,384]{2,1,0:T(8,128)(2,1)}, u32[]{:S(2)}, u32[]{:S(2)}) async-start(bf16[8,256,384]{2,1,0:T(8,128)(2,1)} %copy-done.14), calls=%async_computation.7 | async-start | bytes 3145728 | tf_op jit(solution)/shard_map/all_to_all | solution.py:747
  936.7 114.3 %reduce-scatter.42.cloned.1.call-start = ((), (), s32[]{:S(2)}) async-start(), calls=%async_computation.37 | async-start | bytes 1474560
  941.3 109.6 %reduce-scatter.40.cloned.1.call-start = ((), (), s32[]{:S(2)}) async-start(), calls=%async_computation.36 | async-start | bytes 1474560
  946.2 51.6 %collective-permute-start.91 = (bf16[2,256,1536]{2,1,0:T(8,128)(2,1)}, bf16[2,256,1536]{2,1,0:T(8,128)(2,1)}, u32[]{:S(2)}, u32[]{:S(2)}) collective-permute-start(bf16[2,256,1536]{2,1,0:T(8,128)(2,1)} %pad_maximum_fusion.13), channel_id=1, source_target_pairs={{1,8},{3,10},{5,12},{7,14},{8,1},{10,3},{12,5},{14,7},{17,24},{19,... | collective-permute-start | bytes 4718600 | tf_op jit(solution)/shard_map/ppermute | solution.py:713
  984.7 31.0 %all-to-all-start.12 = ((bf16[8,48,1024]{2,1,0:T(8,128)(2,1)}), bf16[8,48,1024]{2,1,0:T(8,128)(2,1)S(1)}, u32[]{:S(2)}, u32[]{:S(2)}) async-start(bf16[8,48,1024]{2,1,0:T(8,128)(2,1)} %bitcast.684), calls=%async_computation.12 | async-start | bytes 1572864 | tf_op jit(solution)/shard_map/all_to_all | solution.py:747
  1015.7 35.3 %all-to-all-start.8 = ((bf16[8,48,1152]{2,1,0:T(8,128)(2,1)}), bf16[8,48,1152]{2,1,0:T(8,128)(2,1)}, u32[]{:S(2)}, u32[]{:S(2)}) async-start(bf16[8,48,1152]{2,1,0:T(8,128)(2,1)} %bitcast.682), calls=%async_computation.8 | async-start | bytes 1769472 | tf_op jit(solution)/shard_map/all_to_all | solution.py:747
  1019.9 109.5 %reduce-scatter.44.cloned.1.call-start = ((), (), s32[]{:S(2)}) async-start(), calls=%async_computation.38 | async-start | bytes 1474560
  1030.1 47.7 %collective-permute-start.97 = (bf16[2,256,1536]{2,1,0:T(8,128)(2,1)}, bf16[2,256,1536]{2,1,0:T(8,128)(2,1)}, u32[]{:S(2)}, u32[]{:S(2)}) collective-permute-start(bf16[2,256,1536]{2,1,0:T(8,128)(2,1)} %pad_maximum_fusion.14), channel_id=1, source_target_pairs={{1,8},{3,10},{5,12},{7,14},{8,1},{10,3},{12,5},{14,7},{17,24},{19,... | collective-permute-start | bytes 4718600 | tf_op jit(solution)/shard_map/ppermute | solution.py:713
  1063.0 100.2 %collective-permute-start.108 = (bf16[144,1536]{1,0:T(8,128)(2,1)}, bf16[144,1536]{1,0:T(8,128)(2,1)}, u32[]{:S(2)}, u32[]{:S(2)}) collective-permute-start(bf16[144,1536]{1,0:T(8,128)(2,1)} %constant_dynamic-update-slice_fusion.42), channel_id=1, source_target_pairs={{16,2},{17,3},{8,4},{9,5},{24,6},{25,7},{2,8},{3,9},{18,10},{19,11... | collective-permute-start | bytes 1327112 | tf_op jit(solution)/shard_map/ppermute | solution.py:833
  1066.9 63.0 %all-to-all-start.10 = ((bf16[8,48,384]{2,1,0:T(8,128)(2,1)}), bf16[8,48,384]{2,1,0:T(8,128)(2,1)S(1)}, u32[]{:S(2)}, u32[]{:S(2)}) async-start(bf16[8,48,384]{2,1,0:T(8,128)(2,1)} %bitcast.692), calls=%async_computation.10 | async-start | bytes 589824 | tf_op jit(solution)/shard_map/all_to_all | solution.py:747
  1139.0 35.7 %collective-permute-start.96 = (f32[2,64,1536]{2,1,0:T(8,128)}, f32[2,64,1536]{2,1,0:T(8,128)S(1)}, u32[]{:S(2)}, u32[]{:S(2)}) collective-permute-start(f32[2,64,1536]{2,1,0:T(8,128)} %fusion.20), channel_id=1, source_target_pairs={{1,8},{3,10},{5,12},{7,14},{8,1},{10,3},{12,5},{14,7},{17,24},{19,... | collective-permute-start | bytes 2359304 | tf_op jit(solution)/shard_map/ppermute | solution.py:713
  (268 other events, 3673.0 us)
Sparse Core Ops, SparseCore 0:
  68.4 31.4 all-gather.16
  190.2 27.3 all-gather.18
  220.0 27.7 all-gather.20
  250.0 43.9 all-gather.22
  295.7 30.9 all-gather.24
  347.8 35.4 all-gather.28
  385.2 47.2 all-gather.26
  453.8 44.0 all-gather.30
  582.1 43.1 reduce-scatter.27
  630.8 29.6 reduce-scatter.29
  720.0 24.3 reduce-scatter.33
  747.7 47.2 reduce-scatter.31
  819.0 33.7 reduce-scatter.37
  856.0 43.9 reduce-scatter.35
  941.4 33.3 reduce-scatter.41
  984.1 32.6 reduce-scatter.39
  1061.7 37.7 reduce-scatter.43
